TPU v7x, 32 devices: a whole 2x2x4 slice. The times are simulated.
32 devices in a mesh: ctx: 4 (over z), shard: 8 (over y, x, core).
Axes of the slice: x: 2, y: 2, z: 4, core: 2. Of those that a mesh axis runs over, the one named last changes fastest.
Arguments:
- tokens: bfloat16 [8, 1024, 1024], P('shard', 'ctx'), may hold values from -6 to 6
- segments: int32 [8, 1024], P('shard', 'ctx'), may hold values from 0 to 254, as said below
- valid: int32 [8, 1024], P('shard', 'ctx'), may hold values from 0 to 1, as said below
- routes: int32 [8, 1024, 2], P('shard', 'ctx'), may hold values from 0 to 7, all different within a row; in each aligned block of 256 rows (0 to 255, 256 to 511, ..., all dimensions but the last counted through in order) at most 80 rows name the same one
- teacher: bfloat16 [8, 1024, 1024], P('shard', 'ctx'), may hold values from -6 to 6
- norm_attn: bfloat16 [1024], P(('ctx', 'shard')), may hold values from 0.5 to 1.5
- w_query: bfloat16 [1024, 1024], P(('ctx', 'shard')), may hold values from -0.1875 to 0.1875
- w_key: bfloat16 [1024, 1024], P(('ctx', 'shard')), may hold values from -0.1875 to 0.1875
- w_value: bfloat16 [1024, 1024], P(('ctx', 'shard')), may hold values from -0.1875 to 0.1875
- output_weight: bfloat16 [1024, 1024], P(('ctx', 'shard')), may hold values from -1.5 to 1.5
- rel_bias: bfloat16 [512], P(('ctx', 'shard')), may hold values from -4 to 4
- norm_ffn: bfloat16 [1024], P(('ctx', 'shard')), may hold values from 0.5 to 1.5
- w_router: bfloat16 [1024, 8], P(('ctx', 'shard')), may hold values from -0.125 to 0.125
- w_gate: bfloat16 [8, 1024, 2816], P('shard'), may hold values from -0.1875 to 0.1875
- w_up: bfloat16 [8, 1024, 2816], P('shard'), may hold values from -0.1875 to 0.1875
- w_down: bfloat16 [8, 2816, 1024], P('shard'), may hold values from -0.21875 to 0.21875
Outputs:
- output: bfloat16 [8, 1024, 1024], P('shard', 'ctx')
- loss: float32 [], replicated
- input_grad: float32 [8, 1024, 1024], P('shard', 'ctx')
- norm_attn_grad: float32 [1024], P(('ctx', 'shard'))
- w_query_grad: float32 [1024, 1024], P(('ctx', 'shard'))
- w_key_grad: float32 [1024, 1024], P(('ctx', 'shard'))
- w_value_grad: float32 [1024, 1024], P(('ctx', 'shard'))
- w_out_grad: float32 [1024, 1024], P(('ctx', 'shard'))
- rel_bias_grad: float32 [512], P(('ctx', 'shard'))
- norm_ffn_grad: float32 [1024], P(('ctx', 'shard'))
- w_router_grad: float32 [1024, 8], P(('ctx', 'shard'))
- w_gate_grad: float32 [8, 1024, 2816], P('shard', 'ctx')
- w_up_grad: float32 [8, 1024, 2816], P('shard', 'ctx')
- w_down_grad: float32 [8, 2816, 1024], P('shard', 'ctx')
Inputs may be any that keep to these rules, and one draw needn't show every extreme that they name: `segments`: along each sequence the ids start at 0 and never fall. In each sequence one document begins among the first 128 positions and ends among the last 128. The first token of each sequence is valid. `routes`: each token names 2 different experts. Among the tokens of one device no expert is named more than 80 times, and in every draw some device names some expert exactly 80 times.
All inputs are finite; a program needn't handle non-finite values.
Results may differ from a plain program's by a relative error of at most 0.02.
Values may be sent and summed in bfloat16 or wider, within the bound.
A program may use at most 192 MiB of HBM per device.

v0:
```python
import math

import jax
import jax.numpy as jnp
from jax import lax
from jax.sharding import PartitionSpec as P

HEADS = 16
HEAD = 64
BUCKETS = 32


highest_precision = lax.Precision.HIGHEST
max_distance = 128
epsilon = 1e-06
negative = -1e30


def thresholds(buckets):
    exact_count = buckets // 2
    limits = list(range(1, exact_count))
    for bucket_level in range(exact_count, buckets):
        power = (bucket_level - exact_count) / exact_count
        limits.append(int(math.ceil(exact_count * (max_distance / exact_count) ** power)))
    return limits


def bucket_of(distance, buckets):
    bucket_total = jnp.zeros(distance.shape, jnp.int32)
    for threshold in thresholds(buckets):
        bucket_total = bucket_total + (distance >= threshold).astype(jnp.int32)
    return bucket_total


def rms_norm(values, gain_vector):
    return (
        values
        * lax.rsqrt(jnp.mean(values * values, axis=-1, keepdims=True) + epsilon)
        * gain_vector
    )


def contract(left_side, right_side, left_axis, right_axis, precision_mode=None):
    return lax.dot_general(
        left_side,
        right_side,
        (((left_axis,), (right_axis,)), ((), ())),
        precision=precision_mode,
        preferred_element_type=jnp.float32,
    )


def mask_and_bias(query_pos, query_seg, key_pos, key_seg, key_valid, bias_table, buckets):
    distance = query_pos[:, None] - key_pos[None, :]
    allowed = (
        (query_seg[:, None] == key_seg[None, :])
        & (distance >= 0)
        & ((key_valid[None, :] > 0) | (distance == 0))
    )
    levels = bucket_of(jnp.maximum(distance, 0), buckets)
    one_hot = (levels[:, :, None] == jnp.arange(buckets, dtype=jnp.int32)[None, None, :]).astype(
        jnp.bfloat16
    )
    bias_block = jnp.einsum("qkb,bh->hqk", one_hot, bias_table, preferred_element_type=jnp.float32)
    return (allowed, one_hot, bias_block)


def per_device(
    tokens,
    segments,
    valid,
    routes,
    teacher,
    norm_attn,
    w_query,
    w_key,
    w_value,
    output_weight,
    rel_bias,
    norm_ffn,
    w_router,
    w_gate,
    w_up,
    w_down,
):
    ctx_size = lax.axis_size("ctx")
    shard_size = lax.axis_size("shard")
    row_count = tokens.shape[1]
    feature_width = tokens.shape[2]
    head_count = HEADS
    head_size = HEAD
    top_count = routes.shape[2]
    experts = w_router.shape[1]
    capacity = (5 * row_count * top_count + 4 * experts - 1) // (4 * experts)
    seq_length = row_count * ctx_size
    score_scale = 1.0 / math.sqrt(head_size)
    full_query, full_key, full_value, full_out, gain_attn, gain_ffn, full_router, full_bias = (
        lax.all_gather(w_query, ("ctx", "shard"), axis=0, tiled=True),
        lax.all_gather(w_key, ("ctx", "shard"), axis=0, tiled=True),
        lax.all_gather(w_value, ("ctx", "shard"), axis=0, tiled=True),
        lax.all_gather(output_weight, ("ctx", "shard"), axis=0, tiled=True),
        lax.all_gather(norm_attn, ("ctx", "shard"), axis=0, tiled=True),
        lax.all_gather(norm_ffn, ("ctx", "shard"), axis=0, tiled=True),
        lax.all_gather(w_router, ("ctx", "shard"), axis=0, tiled=True),
        lax.all_gather(rel_bias, ("ctx", "shard"), axis=0, tiled=True),
    )
    table_low = full_bias.reshape(BUCKETS, head_count)
    inputs = tokens[0].astype(jnp.float32)
    gain_one = gain_attn.astype(jnp.float32)
    hidden_one = rms_norm(inputs, gain_one).astype(jnp.bfloat16)
    queries = jnp.dot(hidden_one, full_query, preferred_element_type=jnp.float32).astype(
        jnp.bfloat16
    )
    key_local = jnp.dot(hidden_one, full_key, preferred_element_type=jnp.float32).astype(
        jnp.bfloat16
    )
    value_local = jnp.dot(hidden_one, full_value, preferred_element_type=jnp.float32).astype(
        jnp.bfloat16
    )
    query_heads = queries.reshape(row_count, head_count, head_size)
    seg_all, valid_all = (
        lax.all_gather(segments[0], "ctx", axis=0, tiled=True),
        lax.all_gather(valid[0], "ctx", axis=0, tiled=True),
    )
    ctx_index = lax.axis_index("ctx")
    query_pos = ctx_index * row_count + jnp.arange(row_count, dtype=jnp.int32)
    query_seg = segments[0]
    last_query = ctx_index * row_count + row_count - 1

    def block_scores(key_piece, value_piece, block_begin, key_start, block_size):
        key_rows = lax.dynamic_slice_in_dim(key_piece, block_begin, block_size, 0).reshape(
            block_size, head_count, head_size
        )
        value_rows = lax.dynamic_slice_in_dim(value_piece, block_begin, block_size, 0).reshape(
            block_size, head_count, head_size
        )
        key_pos = key_start + jnp.arange(block_size, dtype=jnp.int32)
        key_seg = lax.dynamic_slice_in_dim(seg_all, key_start, block_size, 0)
        key_valid = lax.dynamic_slice_in_dim(valid_all, key_start, block_size, 0)
        allowed, one_hot, bias_block = mask_and_bias(
            query_pos, query_seg, key_pos, key_seg, key_valid, table_low, BUCKETS
        )
        scores = (
            jnp.einsum("qhd,khd->hqk", query_heads, key_rows, preferred_element_type=jnp.float32)
            * score_scale
            + bias_block
        )
        scores = jnp.where(allowed[None], scores, negative)
        return (key_rows, value_rows, allowed, one_hot, scores)

    forward_init = (
        jnp.full((head_count, row_count), negative, jnp.float32),
        jnp.zeros((head_count, row_count), jnp.float32),
        jnp.zeros((head_count, row_count, head_size), jnp.float32),
    )
    key_piece = lax.all_gather(key_local, "ctx", axis=0, tiled=True)
    value_piece = lax.all_gather(value_local, "ctx", axis=0, tiled=True)
    piece_length = key_piece.shape[0]
    block_size = math.gcd(piece_length, 512)

    def forward_block_step(block_index, carry_state):
        block_begin = block_index * block_size
        key_start = block_begin

        def forward_compute(kept_state):
            run_max, run_sum, run_acc = kept_state
            key_rows, value_rows, allowed, one_hot, scores = block_scores(
                key_piece, value_piece, block_begin, key_start, block_size
            )
            new_max = jnp.maximum(run_max, jnp.max(scores, axis=-1))
            factor = jnp.exp(run_max - new_max)
            weights = jnp.where(allowed[None], jnp.exp(scores - new_max[..., None]), 0.0)
            new_sum = run_sum * factor + jnp.sum(weights, axis=-1)
            new_acc = run_acc * factor[..., None] + jnp.einsum(
                "hqk,khd->hqd",
                weights.astype(jnp.bfloat16),
                value_rows,
                preferred_element_type=jnp.float32,
            )
            return (new_max, new_sum, new_acc)

        return lax.cond(
            key_start > last_query, lambda kept_state: kept_state, forward_compute, carry_state
        )

    run_max, run_sum, run_acc = lax.fori_loop(
        0, piece_length // block_size, forward_block_step, forward_init
    )
    attended = run_acc / run_sum[..., None]
    log_total = run_max + jnp.log(run_sum)
    attended_rows = jnp.transpose(attended, (1, 0, 2))
    mixed_low = attended_rows.reshape(row_count, feature_width).astype(jnp.bfloat16)
    attention_result = jnp.dot(mixed_low, full_out, preferred_element_type=jnp.float32)
    residual = inputs + attention_result
    gain_two = gain_ffn.astype(jnp.float32)
    ffn_low = rms_norm(residual, gain_two).astype(jnp.bfloat16)
    ffn_in = ffn_low.astype(jnp.float32)
    router = full_router.astype(jnp.float32)
    logits = jnp.dot(ffn_in, router, precision=highest_precision)
    route_local = routes[0]
    expert_ids = jnp.arange(experts, dtype=jnp.int32)
    route_hot = route_local[:, :, None] == expert_ids[None, None, :]
    picked = jnp.sum(jnp.where(route_hot, logits[:, None, :], 0.0), axis=-1)
    gate_probs = jax.nn.softmax(picked, axis=-1)
    flat_routes = route_local.reshape(row_count * top_count)
    route_hits = (flat_routes[:, None] == expert_ids[None, :]).astype(jnp.int32)
    before = jnp.cumsum(route_hits, axis=0) - route_hits
    slot_rank = jnp.sum(before * route_hits, axis=1)
    target = (flat_routes * capacity + slot_rank).reshape(row_count, top_count)
    slot_ids = jnp.arange(experts * capacity, dtype=jnp.int32)
    pick_first = (slot_ids[:, None] == target[None, :, 0]).astype(jnp.bfloat16)
    pick_second = (slot_ids[:, None] == target[None, :, 1]).astype(jnp.bfloat16)
    send_rows = (
        jnp.dot(pick_first + pick_second, ffn_low, preferred_element_type=jnp.float32)
        .astype(jnp.bfloat16)
        .reshape(experts, capacity, feature_width)
    )
    received = lax.all_to_all(send_rows, "shard", split_axis=0, concat_axis=0, tiled=True)
    expert_rows = received.reshape(shard_size * capacity, feature_width)
    gate_w = w_gate[0]
    up_w = w_up[0]
    down_w = w_down[0]
    gate_pre = jnp.dot(expert_rows, gate_w, preferred_element_type=jnp.float32)
    up_pre = jnp.dot(expert_rows, up_w, preferred_element_type=jnp.float32)

    def activation(gate_values, up_values):
        return jax.nn.gelu(gate_values) * up_values

    inner_value, activation_back = jax.vjp(activation, gate_pre, up_pre)
    inner = inner_value.astype(jnp.bfloat16)
    expert_out = (
        jnp.dot(inner, down_w, preferred_element_type=jnp.float32)
        .astype(jnp.bfloat16)
        .reshape(shard_size, capacity, feature_width)
    )
    returned = lax.all_to_all(expert_out, "shard", split_axis=0, concat_axis=0, tiled=True).reshape(
        experts * capacity, feature_width
    )
    picked_rows = (
        jnp.take(returned, target.reshape(-1), axis=0)
        .reshape(row_count, top_count, feature_width)
        .astype(jnp.float32)
    )
    output_sum = residual + jnp.sum(gate_probs[:, :, None] * picked_rows, axis=1)
    valid_one = valid[0].astype(jnp.float32)
    deviation = output_sum - teacher[0].astype(jnp.float32)
    local_square = jnp.sum(valid_one[:, None] * deviation * deviation)
    total_square, valid_count = lax.psum((local_square, jnp.sum(valid_one)), ("ctx", "shard"))
    loss_value = total_square / (2.0 * feature_width * valid_count)
    everything = float(row_count * ctx_size * shard_size)
    cotangent = everything / valid_count * deviation * valid_one[:, None]
    gate_grad = jnp.sum(cotangent[:, None, :] * picked_rows, axis=-1)
    slot_grad = (gate_probs[:, :, None] * cotangent[:, None, :]).astype(jnp.bfloat16)
    back_send = (
        (
            jnp.dot(pick_first, slot_grad[:, 0], preferred_element_type=jnp.float32)
            + jnp.dot(pick_second, slot_grad[:, 1], preferred_element_type=jnp.float32)
        )
        .astype(jnp.bfloat16)
        .reshape(experts, capacity, feature_width)
    )
    out_grad = lax.all_to_all(back_send, "shard", split_axis=0, concat_axis=0, tiled=True).reshape(
        shard_size * capacity, feature_width
    )
    inner_grad = contract(out_grad, down_w, 1, 1)
    down_w_grad = contract(inner, out_grad, 0, 0)
    gate_pre_grad, up_pre_grad = activation_back(inner_grad)
    gate_low = gate_pre_grad.astype(jnp.bfloat16)
    up_low = up_pre_grad.astype(jnp.bfloat16)
    gate_w_grad = contract(expert_rows, gate_low, 0, 0)
    up_w_grad = contract(expert_rows, up_low, 0, 0)
    rows_grad = (
        (contract(gate_low, gate_w, 1, 1) + contract(up_low, up_w, 1, 1))
        .astype(jnp.bfloat16)
        .reshape(shard_size, capacity, feature_width)
    )
    sent_back = lax.all_to_all(rows_grad, "shard", split_axis=0, concat_axis=0, tiled=True).reshape(
        experts * capacity, feature_width
    )
    ffn_grad = jnp.sum(
        jnp.take(sent_back, target.reshape(-1), axis=0)
        .reshape(row_count, top_count, feature_width)
        .astype(jnp.float32),
        axis=1,
    )
    gate_w_sum, up_w_sum, down_w_sum = (
        lax.psum_scatter(
            gate_w_grad[None].astype(jnp.bfloat16), "ctx", scatter_dimension=1, tiled=True
        ).astype(jnp.float32),
        lax.psum_scatter(
            up_w_grad[None].astype(jnp.bfloat16), "ctx", scatter_dimension=1, tiled=True
        ).astype(jnp.float32),
        lax.psum_scatter(
            down_w_grad[None].astype(jnp.bfloat16), "ctx", scatter_dimension=1, tiled=True
        ).astype(jnp.float32),
    )
    pick_grad = gate_probs * (gate_grad - jnp.sum(gate_probs * gate_grad, axis=-1, keepdims=True))
    logits_grad = jnp.sum(jnp.where(route_hot, pick_grad[:, :, None], 0.0), axis=1)
    router_grad = contract(ffn_in, logits_grad, 0, 0, highest_precision)
    ffn_grad = ffn_grad + contract(logits_grad, router, 1, 1, highest_precision)
    unused, norm_two_back = jax.vjp(rms_norm, residual, gain_two)
    residual_from_norm, gain_two_grad = norm_two_back(ffn_grad)
    residual_grad = cotangent + residual_from_norm
    attn_grad_low = residual_grad.astype(jnp.bfloat16)
    out_w_grad = contract(mixed_low, attn_grad_low, 0, 0)
    mixed_grad = contract(attn_grad_low, full_out, 1, 1).astype(jnp.bfloat16)
    mixed_grad_heads = mixed_grad.reshape(row_count, head_count, head_size)
    delta = jnp.einsum(
        "qhd,qhd->hq",
        mixed_grad_heads.astype(jnp.float32),
        attended_rows,
        precision=highest_precision,
    )
    backward_init = (
        jnp.zeros((row_count, head_count, head_size), jnp.float32),
        jnp.zeros((seq_length, feature_width), jnp.float32),
        jnp.zeros((seq_length, feature_width), jnp.float32),
        jnp.zeros((BUCKETS, head_count), jnp.float32),
    )
    backward_key_piece = lax.all_gather(key_local, "ctx", axis=0, tiled=True)
    backward_value_piece = lax.all_gather(value_local, "ctx", axis=0, tiled=True)
    piece_length = backward_key_piece.shape[0]
    backward_block_size = math.gcd(piece_length, 512)

    def backward_block_step(block_index, carry_state):
        block_begin = block_index * backward_block_size
        key_start = block_begin

        def backward_compute(kept_state):
            query_acc, key_acc, value_acc, table_acc = kept_state
            key_rows, value_rows, allowed, one_hot, scores = block_scores(
                backward_key_piece,
                backward_value_piece,
                block_begin,
                key_start,
                backward_block_size,
            )
            probabilities = jnp.where(allowed[None], jnp.exp(scores - log_total[..., None]), 0.0)
            value_term = jnp.einsum(
                "hqk,qhd->khd",
                probabilities.astype(jnp.bfloat16),
                mixed_grad_heads,
                preferred_element_type=jnp.float32,
            )
            prob_grad = jnp.einsum(
                "qhd,khd->hqk", mixed_grad_heads, value_rows, preferred_element_type=jnp.float32
            )
            score_grad = probabilities * (prob_grad - delta[..., None])
            table_acc = table_acc + jnp.einsum(
                "hqk,qkb->bh", score_grad, one_hot.astype(jnp.float32), precision=highest_precision
            )
            score_low = score_grad.astype(jnp.bfloat16)
            query_acc = (
                query_acc
                + jnp.einsum(
                    "hqk,khd->qhd", score_low, key_rows, preferred_element_type=jnp.float32
                )
                * score_scale
            )
            key_term = (
                jnp.einsum(
                    "hqk,qhd->khd", score_low, query_heads, preferred_element_type=jnp.float32
                )
                * score_scale
            )
            key_old = lax.dynamic_slice_in_dim(key_acc, key_start, backward_block_size, 0)
            key_acc = lax.dynamic_update_slice_in_dim(
                key_acc,
                key_old + key_term.reshape(backward_block_size, feature_width),
                key_start,
                0,
            )
            value_old = lax.dynamic_slice_in_dim(value_acc, key_start, backward_block_size, 0)
            value_acc = lax.dynamic_update_slice_in_dim(
                value_acc,
                value_old + value_term.reshape(backward_block_size, feature_width),
                key_start,
                0,
            )
            return (query_acc, key_acc, value_acc, table_acc)

        return lax.cond(
            key_start > last_query, lambda kept_state: kept_state, backward_compute, carry_state
        )

    query_acc, key_acc, value_acc, table_acc = lax.fori_loop(
        0, piece_length // backward_block_size, backward_block_step, backward_init
    )
    key_sum, value_sum = (
        lax.psum_scatter(
            key_acc.astype(jnp.bfloat16), "ctx", scatter_dimension=0, tiled=True
        ).astype(jnp.float32),
        lax.psum_scatter(
            value_acc.astype(jnp.bfloat16), "ctx", scatter_dimension=0, tiled=True
        ).astype(jnp.float32),
    )
    query_grad = query_acc.reshape(row_count, feature_width).astype(jnp.bfloat16)
    key_grad = key_sum.astype(jnp.bfloat16)
    value_grad = value_sum.astype(jnp.bfloat16)
    query_w_grad = contract(hidden_one, query_grad, 0, 0)
    key_w_grad = contract(hidden_one, key_grad, 0, 0)
    value_w_grad = contract(hidden_one, value_grad, 0, 0)
    hidden_grad = (
        contract(query_grad, full_query, 1, 1)
        + contract(key_grad, full_key, 1, 1)
        + contract(value_grad, full_value, 1, 1)
    )
    unused, norm_one_back = jax.vjp(rms_norm, inputs, gain_one)
    input_from_norm, gain_one_grad = norm_one_back(hidden_grad)
    input_grad = residual_grad + input_from_norm
    summed = (
        lax.psum_scatter(query_w_grad, ("ctx", "shard"), scatter_dimension=0, tiled=True),
        lax.psum_scatter(key_w_grad, ("ctx", "shard"), scatter_dimension=0, tiled=True),
        lax.psum_scatter(value_w_grad, ("ctx", "shard"), scatter_dimension=0, tiled=True),
        lax.psum_scatter(out_w_grad, ("ctx", "shard"), scatter_dimension=0, tiled=True),
        lax.psum_scatter(gain_one_grad, ("ctx", "shard"), scatter_dimension=0, tiled=True),
        lax.psum_scatter(gain_two_grad, ("ctx", "shard"), scatter_dimension=0, tiled=True),
        lax.psum_scatter(router_grad, ("ctx", "shard"), scatter_dimension=0, tiled=True),
        lax.psum_scatter(table_acc.reshape(-1), ("ctx", "shard"), scatter_dimension=0, tiled=True),
    )
    return (
        output_sum.astype(jnp.bfloat16)[None],
        loss_value,
        input_grad[None],
        summed[4],
        summed[0],
        summed[1],
        summed[2],
        summed[3],
        summed[7],
        summed[5],
        summed[6],
        gate_w_sum,
        up_w_sum,
        down_w_sum,
    )


def solution(mesh):
    return jax.shard_map(
        per_device,
        mesh=mesh,
        in_specs=(
            P("shard", "ctx", None),
            P("shard", "ctx"),
            P("shard", "ctx"),
            P("shard", "ctx", None),
            P("shard", "ctx", None),
            P(("ctx", "shard")),
            P(("ctx", "shard"), None),
            P(("ctx", "shard"), None),
            P(("ctx", "shard"), None),
            P(("ctx", "shard"), None),
            P(("ctx", "shard")),
            P(("ctx", "shard")),
            P(("ctx", "shard"), None),
            P("shard", None, None),
            P("shard", None, None),
            P("shard", None, None),
        ),
        out_specs=(
            P("shard", "ctx", None),
            P(),
            P("shard", "ctx", None),
            P(("ctx", "shard")),
            P(("ctx", "shard"), None),
            P(("ctx", "shard"), None),
            P(("ctx", "shard"), None),
            P(("ctx", "shard"), None),
            P(("ctx", "shard")),
            P(("ctx", "shard")),
            P(("ctx", "shard"), None),
            P("shard", "ctx", None),
            P("shard", "ctx", None),
            P("shard", "ctx", None),
        ),
        check_vma=False,
    )
```

profile of v0, /device:TPU:0, one launch (start us, length us, event | category | flops | bytes accessed | tf_op | source)
XLA Modules:
  0.0 1806.5 jit_solution(11447049536100567349)
XLA Ops:
  12.0 42.2 %all-reduce.7 = (bf16[1024]{0:T(1024)(128)(2,1)S(1)}, bf16[512]{0:T(512)(128)(2,1)S(1)}, bf16[1024]{0:T(1024)(128)(2,1)S(1)}) all-reduce(bf16[1024]{0:T(1024)(128)(2,1)S(1)} %dynamic-update-slice, bf16[512]{0:T(512)(128)(2,1)S(1)} %dynamic-update-slice.1, ...), channel_id=1, replica_groups=mesh['ctx'=4,'shard'=8] {'ctx','shard'}, use_global_device_ids=true, to_apply=%add | all-reduce | flops 2560 | bytes 10240
  73.4 54.7 %all-gather.10.cloned.1.call-done = bf16[1024,1024]{1,0:T(8,128)(2,1)} async-done(((bf16[32,1024]{1,0:T(8,128)(2,1)}), bf16[1024,1024]{1,0:T(8,128)(2,1)}) %all-gather.10.cloned.1.call-update) | async-done | bytes 2097168 | tf_op jit(solution)/shard_map/all_gather | solution.py:99
  152.3 34.0 %all-gather.14.cloned.1.call-done = bf16[1024,1024]{1,0:T(8,128)(2,1)} async-done(((bf16[32,1024]{1,0:T(8,128)(2,1)}), bf16[1024,1024]{1,0:T(8,128)(2,1)}) %all-gather.14.cloned.1.call-update) | async-done | bytes 2097168 | tf_op jit(solution)/shard_map/all_gather | solution.py:98
  189.6 43.5 %all-gather.18.cloned.1.call-done = bf16[1024,1024]{1,0:T(8,128)(2,1)} async-done(((bf16[256,1024]{1,0:T(8,128)(2,1)}), bf16[1024,1024]{1,0:T(8,128)(2,1)}) %all-gather.18.cloned.1.call-update) | async-done | bytes 2097168 | tf_op jit(solution)/shard_map/all_gather | solution.py:157
  237.1 42.7 %all-gather.12.cloned.1.call-done = bf16[1024,1024]{1,0:T(8,128)(2,1)} async-done(((bf16[256,1024]{1,0:T(8,128)(2,1)}), bf16[1024,1024]{1,0:T(8,128)(2,1)}) %all-gather.12.cloned.1.call-update) | async-done | bytes 2097168 | tf_op jit(solution)/shard_map/all_gather | solution.py:156
  283.8 32.3 %while.38 = (s32[]{:T(128)}, f32[16,256]{1,0:T(8,128)S(1)}, f32[16,256]{1,0:T(8,128)S(1)}, f32[16,256,64]{1,2,0:T(8,128)S(1)}, s32[]{:T(128)}, /*index=5*/s32[1,...) while((s32[]{:T(128)}, f32[16,256]{1,0:T(8,128)S(1)}, ...), condition=%wide.region_6.7_spmd.clone, body=%wide.region_1.6_spmd.clone.sunk | while | flops 710026496 | bytes 70539632 | solution.py:186
  283.9 31.9 %conditional.6 = (f32[16,256]{1,0:T(8,128)S(1)}, f32[16,256]{1,0:T(8,128)S(1)}, f32[16,256,64]{1,2,0:T(8,128)S(1)}) conditional(s32[]{:T(128)} %convert_element_type.850, (s32[1,256]{1,0:T(1,128)S(1)}, s32[]{:T(128)}, s32[1024]{0:T(1024)S(1)}, s32[]{:T(128)}, s32[1024]{0:T(1024)S(1)}, /*index=5*/bf16[1024,1024]{0,1:T(8,128)(2,1)}, ...), branch_computations={%region_2.4_spmd, %region_5.5_spmd} | conditional | flops 710026496 | bytes 70505544 | solution.py:182
  316.3 21.4 %all-gather.20.cloned.1.call-done = bf16[1024,1024]{1,0:T(8,128)(2,1)} async-done(((bf16[32,1024]{1,0:T(8,128)(2,1)}), bf16[1024,1024]{1,0:T(8,128)(2,1)}) %all-gather.20.cloned.1.call-update) | async-done | bytes 2097168 | tf_op jit(solution)/shard_map/all_gather | solution.py:101
  341.1 21.0 %all_to_all.20 = bf16[8,80,1024]{2,1,0:T(8,128)(2,1)S(1)} all-to-all(bf16[8,80,1024]{2,1,0:T(8,128)(2,1)S(1)} %bitcast.222), channel_id=1, replica_groups=mesh['ctx'=4,'shard'=8] {'shard'}, dimensions={0} | all-to-all | bytes 2621440 | tf_op jit(solution)/shard_map/all_to_all | solution.py:218
  384.6 60.4 %psum.15 = f32[]{:T(128)} all-reduce(f32[]{:T(128)} %convert_reduce_fusion), channel_id=1, replica_groups=mesh['ctx'=4,'shard'=8] {'ctx','shard'}, use_global_device_ids=true, to_apply=%region_18.20 | all-reduce | flops 1 | bytes 8 | tf_op jit(solution)/shard_map/psum | solution.py:248
  445.1 39.9 %all-gather.2 = bf16[32,32,8]{1,2,0:T(8,128)(2,1)S(1)} all-gather(bf16[1,32,8]{1,2,0:T(8,128)(2,1)S(1)} %bitcast.241), channel_id=1, replica_groups=mesh['ctx'=4,'shard'=8] {'ctx','shard'}, dimensions={0}, use_global_device_ids=true | all-gather | bytes 16896 | tf_op jit(solution)/shard_map/all_gather | solution.py:104
  598.1 63.9 %while.39 = (s32[]{:T(128)}, f32[256,16,64]{0,2,1:T(8,128)}, f32[1024,1024]{0,1:T(8,128)}, f32[1024,1024]{0,1:T(8,128)}, f32[32,16]{0,1:T(8,128)S(1)}, /*index=5...) while((s32[]{:T(128)}, f32[256,16,64]{0,2,1:T(8,128)}, ...), condition=%wide.region_27.29_spmd.clone, body=%wide.region_24.28_spmd.clone.sunk | while | flops 2326398720 | bytes 181201520 | solution.py:386
  616.8 37.5 %conditional.7 = ((f32[256,16,64]{0,2,1:T(8,128)}, f32[1024,1024]{0,1:T(8,128)}, f32[1024,1024]{0,1:T(8,128)}, f32[32,16]{0,1:T(8,128)S(1)})) conditional(s32[]{:T(128)} %convert_element_type.851, (s32[]{:T(128)}, bf16[1024,1024]{0,1:T(8,128)(2,1)}, s32[1,256]{1,0:T(1,128)S(1)}, s32[1024]{0:T(1024)S(1)}, s32[]{:T(128)}, ...), branch_computations={%region_25.26_spmd, %region_26.27_spmd} | conditional | flops 2326398720 | bytes 181200128 | solution.py:382
  706.7 35.1 %reduce-scatter.15.cloned.1.call-done = bf16[256,1024]{0,1:T(8,128)(2,1)} async-done(((bf16[1024,1024]{0,1:T(8,128)(2,1)}), bf16[256,1024]{0,1:T(8,128)(2,1)}) %reduce-scatter.15.cloned.1.call-update) | async-done | bytes 524304 | tf_op jit(solution)/shard_map/reduce_scatter | solution.py:393
  746.0 41.9 %reduce-scatter.13.cloned.1.call-done = bf16[256,1024]{0,1:T(8,128)(2,1)} async-done(((bf16[1024,1024]{0,1:T(8,128)(2,1)}), bf16[256,1024]{0,1:T(8,128)(2,1)}) %reduce-scatter.13.cloned.1.call-update) | async-done | bytes 524304 | tf_op jit(solution)/shard_map/reduce_scatter | solution.py:390
  792.6 131.0 %reduce-scatter.31.cloned.1.call-done = f32[32,8]{1,0:T(8,128)} async-done(((f32[1024,8]{1,0:T(8,128)}), f32[32,8]{1,0:T(8,128)}) %reduce-scatter.31.cloned.1.call-update) | async-done | bytes 1040
  931.5 40.8 %all-reduce.6 = (f32[]{:T(128)}, f32[1024]{0:T(1024)S(1)}, f32[512]{0:T(512)S(1)}, f32[1024]{0:T(1024)S(1)}) all-reduce(f32[]{:T(128)} %get-tuple-element.867, f32[1024]{0:T(1024)S(1)} %get-tuple-element.865, f32[512]{0:T(512)S(1)} %reshape.690, f32[1024]{0:T(1024)S(1)} %copy-done.40), channel_id=1, replica_groups=mesh['ctx'=4,'shard'=8] {'ctx','shard'}, use_global_device_ids=true, to_apply=%region_16.18 | all-reduce | flops 2561 | bytes 20488 | tf_op jit(solution)/shard_map/psum | solution.py:248
  976.0 49.0 %reduce-scatter.29.cloned.1.call-done = bf16[1,704,1024]{2,1,0:T(8,128)(2,1)} async-done(((bf16[1,2816,1024]{2,1,0:T(8,128)(2,1)}), bf16[1,704,1024]{2,1,0:T(8,128)(2,1)}) %reduce-scatter.29.cloned.1.call-update) | async-done | bytes 1441808 | tf_op jit(solution)/shard_map/reduce_scatter | solution.py:293
  1028.4 101.8 %reduce-scatter.27.cloned.1.call-done = bf16[1,256,2816]{2,1,0:T(8,128)(2,1)} async-done(((bf16[1,1024,2816]{2,1,0:T(8,128)(2,1)}), bf16[1,256,2816]{2,1,0:T(8,128)(2,1)}) %reduce-scatter.27.cloned.1.call-update) | async-done | bytes 1441808 | tf_op jit(solution)/shard_map/reduce_scatter | solution.py:290
  1133.4 101.9 %reduce-scatter.25.cloned.1.call-done = bf16[1,256,2816]{2,1,0:T(8,128)(2,1)} async-done(((bf16[1,1024,2816]{2,1,0:T(8,128)(2,1)}), bf16[1,256,2816]{2,1,0:T(8,128)(2,1)}) %reduce-scatter.25.cloned.1.call-update) | async-done | bytes 1441808 | tf_op jit(solution)/shard_map/reduce_scatter | solution.py:287
  1238.4 141.2 %reduce-scatter.23.cloned.1.call-done = f32[32,1024]{1,0:T(8,128)} async-done(((f32[1024,1024]{1,0:T(8,128)}), f32[32,1024]{1,0:T(8,128)}) %reduce-scatter.23.cloned.1.call-update) | async-done | bytes 131088 | tf_op jit(solution)/shard_map/reduce_scatter | solution.py:415
  1379.6 139.8 %reduce-scatter.17.cloned.1.call-done = f32[32,1024]{1,0:T(8,128)} async-done(((f32[1024,1024]{1,0:T(8,128)}), f32[32,1024]{1,0:T(8,128)}) %reduce-scatter.17.cloned.1.call-update) | async-done | bytes 131088 | tf_op jit(solution)/shard_map/reduce_scatter | solution.py:412
  1519.4 139.4 %reduce-scatter.21.cloned.1.call-done = f32[32,1024]{1,0:T(8,128)} async-done(((f32[1024,1024]{1,0:T(8,128)}), f32[32,1024]{1,0:T(8,128)}) %reduce-scatter.21.cloned.1.call-update) | async-done | bytes 131088 | tf_op jit(solution)/shard_map/reduce_scatter | solution.py:414
  1658.8 139.8 %reduce-scatter.19.cloned.1.call-done = f32[32,1024]{1,0:T(8,128)} async-done(((f32[1024,1024]{1,0:T(8,128)}), f32[32,1024]{1,0:T(8,128)}) %reduce-scatter.19.cloned.1.call-update) | async-done | bytes 131088 | tf_op jit(solution)/shard_map/reduce_scatter | solution.py:413
  (311 shorter events, 339.7 us)
Async XLA Ops:
  7.2 121.0 %copy-start.13 = (bf16[1,256,1024]{2,1,0:T(8,128)(2,1)S(1)}, bf16[1,256,1024]{2,1,0:T(8,128)(2,1)}, u32[]{:S(2)}) copy-start(bf16[1,256,1024]{2,1,0:T(8,128)(2,1)} %param.26) | copy-start | bytes 1572868
  7.2 62.9 %all-gather.16.cloned.1.call-start = ((), (), s32[]{:S(2)}) async-start(), calls=%async_computation.17 | async-start | bytes 2162688 | tf_op jit(solution)/shard_map/all_gather | solution.py:100
  7.9 120.2 %all-gather.10.cloned.1.call-start = ((), (), s32[]{:S(2)}) async-start(), calls=%async_computation.14 | async-start | bytes 2162688 | tf_op jit(solution)/shard_map/all_gather | solution.py:99
  8.7 177.6 %all-gather.14.cloned.1.call-start = ((), (), s32[]{:S(2)}) async-start(), calls=%async_computation.16 | async-start | bytes 2162688 | tf_op jit(solution)/shard_map/all_gather | solution.py:98
  9.4 223.7 %all-gather.18.cloned.1.call-start = ((), (), s32[]{:S(2)}) async-start(), calls=%async_computation.18 | async-start | bytes 2621440 | tf_op jit(solution)/shard_map/all_gather | solution.py:157
  54.2 132.1 %copy-start.33 = (f32[1024]{0:T(1024)}, f32[1024]{0:T(1024)S(1)}, u32[]{:S(2)}) copy-start(f32[1024]{0:T(1024)S(1)} %convert_element_type.624) | copy-start | bytes 12292
  55.6 130.7 %copy-start.38 = (f32[256]{0:T(256)}, f32[256]{0:T(256)S(1)}, u32[]{:S(2)}) copy-start(f32[256]{0:T(256)S(1)} %fusion.186) | copy-start | bytes 3076
  55.6 88.3 %copy-start.43 = (s32[1,256]{1,0:T(1,128)S(1)}, s32[1,256]{1,0:T(1,128)}, u32[]{:S(2)}) copy-start(s32[1,256]{1,0:T(1,128)} %param.28) | copy-start | bytes 3076
  73.4 206.4 %all-gather.12.cloned.1.call-start = ((), (), s32[]{:S(2)}) async-start(), calls=%async_computation.15 | async-start | bytes 2621440 | tf_op jit(solution)/shard_map/all_gather | solution.py:156
  131.3 206.3 %all-gather.20.cloned.1.call-start = ((), (), s32[]{:S(2)}) async-start(), calls=%async_computation.19 | async-start | bytes 2162688 | tf_op jit(solution)/shard_map/all_gather | solution.py:101
  340.3 145.5 %copy-start.21 = (bf16[256,1024]{1,0:T(8,128)(2,1)}, bf16[256,1024]{1,0:T(8,128)(2,1)S(1)}, u32[]{:S(2)}) copy-start(bf16[256,1024]{1,0:T(8,128)(2,1)S(1)} %multiply_convert_fusion.3) | copy-start | bytes 1572868
  380.5 105.8 %all-to-all-start.1 = ((bf16[8,80,1024]{2,1,0:T(8,128)(2,1)}), bf16[8,80,1024]{2,1,0:T(8,128)(2,1)S(1)}, u32[]{:S(2)}, u32[]{:S(2)}) async-start(bf16[8,80,1024]{2,1,0:T(8,128)(2,1)} %bitcast.36), calls=%async_computation.1 | async-start | bytes 2621440 | tf_op jit(solution)/shard_map/all_to_all | solution.py:236
  548.6 21.7 %all-to-all-start.3 = ((bf16[8,80,1024]{2,1,0:T(8,128)(2,1)}), bf16[8,80,1024]{2,1,0:T(8,128)(2,1)S(1)}, u32[]{:S(2)}, u32[]{:S(2)}) async-start(bf16[8,80,1024]{2,1,0:T(8,128)(2,1)} %bitcast.234), calls=%async_computation.3 | async-start | bytes 2621440 | tf_op jit(solution)/shard_map/all_to_all | solution.py:277
  552.2 189.6 %reduce-scatter.15.cloned.1.call-start = ((), (), s32[]{:S(2)}) async-start(), calls=%async_computation.21 | async-start | bytes 2621440 | tf_op jit(solution)/shard_map/reduce_scatter | solution.py:393
  665.9 122.1 %reduce-scatter.13.cloned.1.call-start = ((), (), s32[]{:S(2)}) async-start(), calls=%async_computation.20 | async-start | bytes 2621440 | tf_op jit(solution)/shard_map/reduce_scatter | solution.py:390
  670.0 253.6 %reduce-scatter.31.cloned.1.call-start = ((), (), s32[]{:S(2)}) async-start(), calls=%async_computation.29 | async-start | bytes 540672
  671.5 353.5 %reduce-scatter.29.cloned.1.call-start = ((), (), s32[]{:S(2)}) async-start(), calls=%async_computation.28 | async-start | bytes 7208960 | tf_op jit(solution)/shard_map/reduce_scatter | solution.py:293
  680.2 450.0 %reduce-scatter.27.cloned.1.call-start = ((), (), s32[]{:S(2)}) async-start(), calls=%async_computation.27 | async-start | bytes 7208960 | tf_op jit(solution)/shard_map/reduce_scatter | solution.py:290
  690.1 545.2 %reduce-scatter.25.cloned.1.call-start = ((), (), s32[]{:S(2)}) async-start(), calls=%async_computation.26 | async-start | bytes 7208960 | tf_op jit(solution)/shard_map/reduce_scatter | solution.py:287
  698.7 680.9 %reduce-scatter.23.cloned.1.call-start = ((), (), s32[]{:S(2)}) async-start(), calls=%async_computation.25 | async-start | bytes 4325376 | tf_op jit(solution)/shard_map/reduce_scatter | solution.py:415
  702.7 816.7 %reduce-scatter.17.cloned.1.call-start = ((), (), s32[]{:S(2)}) async-start(), calls=%async_computation.22 | async-start | bytes 4325376 | tf_op jit(solution)/shard_map/reduce_scatter | solution.py:412
  706.6 952.2 %reduce-scatter.21.cloned.1.call-start = ((), (), s32[]{:S(2)}) async-start(), calls=%async_computation.24 | async-start | bytes 4325376 | tf_op jit(solution)/shard_map/reduce_scatter | solution.py:414
  745.8 1052.8 %reduce-scatter.19.cloned.1.call-start = ((), (), s32[]{:S(2)}) async-start(), calls=%async_computation.23 | async-start | bytes 4325376 | tf_op jit(solution)/shard_map/reduce_scatter | solution.py:413
  791.9 135.7 %copy-start.26 = (bf16[256,1024]{0,1:T(8,128)(2,1)S(1)}, bf16[256,1024]{0,1:T(8,128)(2,1)}, u32[]{:S(2)}) copy-start(bf16[256,1024]{0,1:T(8,128)(2,1)} %reduce-scatter.13.cloned.1.call-done) | copy-start | bytes 1572868
  (51 other events, 739.3 us)
Sparse Core Ops, SparseCore 0:
  10.9 59.1 all-gather.15
  72.9 55.2 all-gather.9
  131.0 55.2 all-gather.13
  188.3 44.7 all-gather.17
  235.1 44.6 all-gather.11
  282.5 55.0 all-gather.19
  666.0 75.7 reduce-scatter.14
  744.8 43.1 reduce-scatter.12
  790.2 133.3 reduce-scatter.30
  925.8 99.1 reduce-scatter.28
  1027.5 102.6 reduce-scatter.26
  1132.5 102.7 reduce-scatter.24
  1238.2 141.2 reduce-scatter.22
  1382.4 136.9 reduce-scatter.16
  1522.2 136.5 reduce-scatter.20
  1661.6 136.9 reduce-scatter.18
where the time goes:
time: 1810 us
  waiting for transfers between devices  1240 us (69%)
  blocking collectives  243 us (13%)
  matrix products  149 us (8%)
  local copies, waits for them, and re-layouts  70.6 us (4%)
  other arithmetic  48.2 us (3%)
  loops' own time  26.9 us (1%)
  between operations  18.2 us (1%)
    reduce_scatter x1, waiting for transfers between devices, per_device(): lax.psum_scatter(out_w_grad, ('ctx', 'shard'), scatter_dimension=0, tiled...  141 us
    reduce_scatter x1, waiting for transfers between devices, per_device(): lax.psum_scatter(key_w_grad, ('ctx', 'shard'), scatter_dimension=0, tiled...  140 us
    reduce_scatter x1, waiting for transfers between devices, per_device(): lax.psum_scatter(query_w_grad, ('ctx', 'shard'), scatter_dimension=0, til...  140 us
    reduce_scatter x1, waiting for transfers between devices, per_device(): lax.psum_scatter(value_w_grad, ('ctx', 'shard'), scatter_dimension=0, til...  139 us
    unnamed x17, waiting for transfers between devices  134 us
    reduce_scatter x1, waiting for transfers between devices, per_device(): lax.psum_scatter(gate_w_grad[None].astype(jnp.bfloat16), 'ctx', scatter_d...  102 us
    reduce_scatter x1, waiting for transfers between devices, per_device(): lax.psum_scatter(up_w_grad[None].astype(jnp.bfloat16), 'ctx', scatter_dim...  102 us
    psum x2, blocking collectives, per_device(): lax.psum((local_square, jnp.sum(valid_one)), ('ctx', 'shard'))  101 us
  transfers between devices with their start and end apart: 18, of which 17 were waited for; matrix products, arithmetic and copies ran while one was open for 7% of the time, Pallas kernels for 0%

commit v1 on v0

v1 whole, which is shorter than its diff:
```python
import math

import jax
import jax.numpy as jnp
from jax import lax
from jax.experimental import pallas as pl
from jax.experimental.pallas import tpu as pltpu
from jax.sharding import PartitionSpec as P

HEADS = 16
HEAD = 64
BUCKETS = 32
MESH = pl.DeviceIdType.MESH
ANY = pl.ANY
VMEM = pltpu.VMEM
SEM = pltpu.SemaphoreType

highest_precision = lax.Precision.HIGHEST
max_distance = 128
epsilon = 1e-06
negative = -1e30
EXTRA = 16


def thresholds(buckets):
    exact_count = buckets // 2
    limits = list(range(1, exact_count))
    for bucket_level in range(exact_count, buckets):
        power = (bucket_level - exact_count) / exact_count
        limits.append(int(math.ceil(exact_count * (max_distance / exact_count) ** power)))
    return limits


def bucket_of(distance, buckets):
    bucket_total = jnp.zeros(distance.shape, jnp.int32)
    for threshold in thresholds(buckets):
        bucket_total = bucket_total + (distance >= threshold).astype(jnp.int32)
    return bucket_total


def rms_norm(values, gain_vector):
    return (
        values
        * lax.rsqrt(jnp.mean(values * values, axis=-1, keepdims=True) + epsilon)
        * gain_vector
    )


def contract(left_side, right_side, left_axis, right_axis, precision_mode=None):
    return lax.dot_general(
        left_side,
        right_side,
        (((left_axis,), (right_axis,)), ((), ())),
        precision=precision_mode,
        preferred_element_type=jnp.float32,
    )


def dot32(left_side, right_side):
    return jnp.dot(left_side, right_side, preferred_element_type=jnp.float32)


def nt(left_side, right_side):
    return contract(left_side, right_side, 1, 1)


def tn(left_side, right_side):
    return contract(left_side, right_side, 0, 0)


class Place:
    def __init__(self, nc, ns):
        self.nc, self.ns, self.nj = nc, ns, ns // 2
        self.c = lax.axis_index("ctx")
        self.s = lax.axis_index("shard")
        self.core = self.s % 2
        self.j = self.s // 2

    def along(self, d):
        return (lax.rem(self.c + d + self.nc, self.nc), self.s)

    def across(self, k):
        return (self.c, self.s ^ (2 * k))

    def twin(self):
        return (self.c, self.s ^ 1)

    def greet(self):
        barrier = pltpu.get_barrier_semaphore()
        partners = (
            [self.along(d) for d in range(1, self.nc)]
            + [self.across(k) for k in range(1, self.nj)]
            + [self.twin()]
        )
        for partner in partners:
            pl.semaphore_signal(barrier, inc=1, device_id=partner, device_id_type=MESH)
        pl.semaphore_wait(barrier, len(partners))


def remote(source, target, send, recv, device):
    return pltpu.make_async_remote_copy(
        src_ref=source,
        dst_ref=target,
        send_sem=send,
        recv_sem=recv,
        device_id=device,
        device_id_type=MESH,
    )


def gather_all(weights, extra, rows, nc, ns):
    n_dev, nj = nc * ns, ns // 2
    parts, piece, width = weights.shape
    count = rows.shape[0]
    spread = piece % 16 == 0
    weight_shape = (parts, n_dev * piece, width) if spread else (n_dev, parts * piece, width)
    if not spread:
        weights = weights.reshape(parts * piece, width)

    def kernel(w_in, e_in, t_in, w_out, e_out, t_out, local, zs, zr, xs, xr, cs, cr, ts, tr):
        me = Place(nc, ns)

        def views(place, device):
            if spread:
                start = pl.multiple_of(device * piece, piece)
                return (w_out.at[:, pl.ds(start, piece), :], e_out.at[device])
            return (w_out.at[device], e_out.at[device])

        def index(d, k):
            return lax.rem(me.c - d + nc, nc) * ns + (me.s ^ (2 * k))

        own = (w_in, e_in)
        mine = me.c * ns + me.s
        locals_ = [
            pltpu.make_async_copy(source, target, local.at[i])
            for i, (source, target) in enumerate(
                zip(own + (t_in,), views(me, mine) + (t_out.at[nc - 1],))
            )
        ]
        for copy in locals_:
            copy.start()
        me.greet()
        sent = []

        def push(sources, targets, send, recv, device):
            for i in range(2):
                copy = remote(sources[i], targets[i], send.at[i], recv.at[i], device)
                copy.start()
                sent.append(copy)

        def arrive(targets, send, recv, device):
            for i in range(2):
                remote(targets[i], targets[i], send.at[i], recv.at[i], device).wait_recv()

        def token_copy(direction, hop, source=None):
            origin_slot = (nc - 1 - hop) if direction > 0 else (hop - 1)
            target_slot = (nc - 2 - hop) if direction > 0 else hop
            lane = 0 if direction > 0 else 1
            return remote(
                t_in if hop == 0 else t_out.at[origin_slot],
                t_out.at[target_slot],
                ts.at[lane, hop],
                tr.at[lane, hop],
                (lax.rem(me.c + direction + nc, nc), me.s),
            )

        def can_send(direction, hop):
            if direction > 0:
                return (me.c >= hop) & (me.c < nc - 1)
            return (me.c <= nc - 1 - hop) & (me.c > 0)

        def can_receive(direction, hop):
            if direction > 0:
                return me.c >= hop + 1
            return me.c <= nc - 2 - hop

        for d in range(1, nc):
            push(own, views(me, mine), zs.at[d], zr.at[d], me.along(d))
        for direction in (1, -1):

            @pl.when(can_send(direction, 0))
            def _():
                token_copy(direction, 0).start()

        for k in range(1, nj):
            push(own, views(me, mine), xs.at[0, k], xr.at[0, k], me.across(k))
        push(own, views(me, mine), cs.at[0, 0], cr.at[0, 0], me.twin())

        for copy in locals_:
            copy.wait()
        for d in range(1, nc):
            here = views(me, index(d, 0))
            arrive(here, zs.at[d], zr.at[d], me.along(-d))
            for k in range(1, nj):
                push(here, here, xs.at[d, k], xr.at[d, k], me.across(k))
            push(here, here, cs.at[d, 0], cr.at[d, 0], me.twin())
            if d < nc - 1:
                for direction in (1, -1):

                    @pl.when(can_receive(direction, d - 1))
                    def _():
                        token_copy(direction, d - 1).wait_recv()

                    @pl.when(can_send(direction, d))
                    def _():
                        token_copy(direction, d).start()

        for d in range(nc):
            for k in range(1, nj):
                here = views(me, index(d, k))
                arrive(here, xs.at[d, k], xr.at[d, k], me.across(k))
                push(here, here, cs.at[d, k], cr.at[d, k], me.twin())
        for d in range(nc):
            for k in range(nj):
                here = views(me, lax.rem(me.c - d + nc, nc) * ns + (me.s ^ 1 ^ (2 * k)))
                arrive(here, cs.at[d, k], cr.at[d, k], me.twin())
        for direction in (1, -1):

            @pl.when(can_receive(direction, nc - 2))
            def _():
                token_copy(direction, nc - 2).wait_recv()

        for copy in sent:
            copy.wait_send()
        for direction in (1, -1):
            for hop in range(nc - 1):

                @pl.when(can_send(direction, hop))
                def _():
                    token_copy(direction, hop).wait_send()

    full, extras, tokens = pl.pallas_call(
        kernel,
        name="gather_all",
        out_shape=(
            jax.ShapeDtypeStruct(weight_shape, weights.dtype),
            jax.ShapeDtypeStruct((n_dev,) + extra.shape, extra.dtype),
            jax.ShapeDtypeStruct((nc,) + rows.shape, rows.dtype),
        ),
        in_specs=[pl.BlockSpec(memory_space=ANY)] * 3,
        out_specs=[pl.BlockSpec(memory_space=ANY)] * 3,
        scratch_shapes=[
            SEM.DMA((3,)),
            SEM.DMA((nc, 2)),
            SEM.DMA((nc, 2)),
            SEM.DMA((nc, nj, 2)),
            SEM.DMA((nc, nj, 2)),
            SEM.DMA((nc, nj, 2)),
            SEM.DMA((nc, nj, 2)),
            SEM.DMA((2, nc)),
            SEM.DMA((2, nc)),
        ],
        compiler_params=pltpu.CompilerParams(collective_id=1, has_side_effects=True),
    )(weights, extra, rows)
    if not spread:
        full = full.reshape(n_dev, parts, piece, width).transpose(1, 0, 2, 3)
        full = full.reshape(parts, n_dev * piece, width)
    return full, extras, tokens.reshape(nc * count, width)


def reduce_all(grads, squares, away, own, nc, ns):
    nj = ns // 2
    piece, width = grads.shape[3:]
    count = own.shape[0]
    tile = squares.shape

    def kernel(g_in, q_in, a_in, o_in, g_out, q_out, o_out, total, cbuf, xbuf, zbuf, abuf,
               qz, qx, qc, qa, qb, cs, cr, xs, xr, zs, zr, as_, ar, q1s, q1r, q2s, q2r, q3s, q3r):
        me = Place(nc, ns)
        me.greet()

        def away_copy(r):
            return remote(
                a_in.at[nc - 1 - r], abuf.at[r - 1], as_.at[r], ar.at[r],
                (lax.rem(me.c - r + nc, nc), me.s),
            )

        def core_copy(d):
            row = lax.rem(me.c + d, nc)
            return remote(
                g_in.at[row, :, 1 - me.core], cbuf.at[d], cs.at[d], cr.at[d], me.twin()
            )

        def cross_copy(d, k):
            return remote(
                total.at[d, me.j ^ k], xbuf.at[d, k - 1], xs.at[d, k], xr.at[d, k], me.across(k)
            )

        def along_copy(d):
            return remote(total.at[d, me.j], zbuf.at[d - 1], zs.at[d], zr.at[d], me.along(d))

        def q_along(d):
            return remote(q_in, qz.at[d - 1], q1s.at[d], q1r.at[d], me.along(d))

        def q_across(k):
            return remote(qa, qx.at[k - 1], q2s.at[k], q2r.at[k], me.across(k))

        q_twin = remote(qb, qc, q3s.at[0], q3r.at[0], me.twin())
        order = list(range(1, nc)) + [0]
        for d in order:
            core_copy(d).start()
        for d in range(1, nc):
            q_along(d).start()
        for r in range(1, nc):

            @pl.when(me.c >= r)
            def _():
                away_copy(r).start()

        step = 16
        for d in order:
            core_copy(d).wait_recv()
            row = lax.rem(me.c + d, nc)

            def add_core(i, carry):
                at = pl.ds(pl.multiple_of(i * step, step), step)
                for k in range(nj):
                    total[d, k, at] = (
                        g_in[row, k, me.core, at].astype(jnp.float32)
                        + cbuf[d, k, at].astype(jnp.float32)
                    ).astype(total.dtype)
                return carry

            lax.fori_loop(0, piece // step, add_core, 0)
            for k in range(1, nj):
                cross_copy(d, k).start()
        for d in range(1, nc):
            q_along(d).wait_recv()
        value = q_in[...]
        for d in range(1, nc):
            value = value + qz[d - 1]
        qa[...] = value
        for k in range(1, nj):
            q_across(k).start()
        for d in order:
            for k in range(1, nj):
                cross_copy(d, k).wait_recv()

            def add_cross(i, carry):
                at = pl.ds(pl.multiple_of(i * step, step), step)
                value = total[d, me.j, at].astype(jnp.float32)
                for k in range(1, nj):
                    value = value + xbuf[d, k - 1, at].astype(jnp.float32)
                if d == 0:
                    g_out[at] = value
                else:
                    total[d, me.j, at] = value.astype(total.dtype)
                return carry

            lax.fori_loop(0, piece // step, add_cross, 0)
            if d:
                along_copy(d).start()
        for k in range(1, nj):
            q_across(k).wait_recv()
        value = qa[...]
        for k in range(1, nj):
            value = value + qx[k - 1]
        qb[...] = value
        q_twin.start()
        for d in range(1, nc):
            along_copy(d).wait_recv()

        def add_along(i, carry):
            at = pl.ds(pl.multiple_of(i * step, step), step)
            value = g_out[at]
            for d in range(1, nc):
                value = value + zbuf[d - 1, at].astype(jnp.float32)
            g_out[at] = value
            return carry

        lax.fori_loop(0, piece // step, add_along, 0)
        o_out[...] = o_in[...]
        for r in range(1, nc):

            @pl.when(me.c < nc - r)
            def _():
                away_copy(r).wait_recv()

                def add_away(i, carry):
                    at = pl.ds(pl.multiple_of(i * step, step), step)
                    o_out[at] = o_out[at] + abuf[r - 1, at].astype(jnp.float32)
                    return carry

                lax.fori_loop(0, count // step, add_away, 0)

        q_twin.wait()
        q_out[...] = qb[...] + qc[...]
        for d in order:
            core_copy(d).wait_send()
            for k in range(1, nj):
                cross_copy(d, k).wait_send()
            if d:
                along_copy(d).wait_send()
                q_along(d).wait_send()
        for k in range(1, nj):
            q_across(k).wait_send()
        for r in range(1, nc):

            @pl.when(me.c >= r)
            def _():
                away_copy(r).wait_send()

    low = grads.dtype
    return pl.pallas_call(
        kernel,
        name="reduce_all",
        out_shape=(
            jax.ShapeDtypeStruct((piece, width), jnp.float32),
            jax.ShapeDtypeStruct(tile, jnp.float32),
            jax.ShapeDtypeStruct(own.shape, jnp.float32),
        ),
        in_specs=[pl.BlockSpec(memory_space=VMEM)] * 4,
        out_specs=[pl.BlockSpec(memory_space=VMEM)] * 3,
        scratch_shapes=[
            VMEM((nc, nj, piece, width), low),
            VMEM((nc, nj, piece, width), low),
            VMEM((nc, nj - 1, piece, width), low),
            VMEM((nc - 1, piece, width), low),
            VMEM((nc - 1,) + own.shape, low),
            VMEM((nc - 1,) + tile, jnp.float32),
            VMEM((nj - 1,) + tile, jnp.float32),
            VMEM(tile, jnp.float32),
            VMEM(tile, jnp.float32),
            VMEM(tile, jnp.float32),
            SEM.DMA((nc,)),
            SEM.DMA((nc,)),
            SEM.DMA((nc, nj)),
            SEM.DMA((nc, nj)),
            SEM.DMA((nc,)),
            SEM.DMA((nc,)),
            SEM.DMA((nc,)),
            SEM.DMA((nc,)),
            SEM.DMA((nc,)),
            SEM.DMA((nc,)),
            SEM.DMA((nj,)),
            SEM.DMA((nj,)),
            SEM.DMA((1,)),
            SEM.DMA((1,)),
        ],
        compiler_params=pltpu.CompilerParams(
            collective_id=2, has_side_effects=True, vmem_limit_bytes=56 * 1024 * 1024
        ),
    )(grads, squares, away, own)


CHUNK = 16
QUAD = 256


def fill_mask(mask, query_seg, key_code, count, length):
    near = length - count
    seen = query_seg[...] == key_code[:, :near]
    mask[:, :near] = jnp.where(seen, 0.0, negative)
    row = lax.broadcasted_iota(jnp.int32, (count, count), 0)
    column = lax.broadcasted_iota(jnp.int32, (count, count), 1)
    seen = ((query_seg[...] == key_code[:, near:]) & (row >= column)) | (row == column)
    mask[:, near:] = jnp.where(seen, 0.0, negative)


def attend_forward(tokens, weights, gain, query_seg, key_code, slopes):
    length, width = tokens.shape
    count = query_seg.shape[0]
    band = slopes.shape[2]
    far = length - band
    heads_in = QUAD // HEAD

    def kernel(t_in, w_in, gain_in, qseg, kcode, toe, first, q_out, k_out, v_out, o_out, lse_out, x_out, sbuf, pbuf, mask, lsum):
        fill_mask(mask, qseg, kcode, count, length)

        def norm(i, carry):
            at = pl.ds(pl.multiple_of(i * 64, 64), 64)
            x = t_in[at].astype(jnp.float32)
            rate = lax.rsqrt(jnp.mean(x * x, axis=-1, keepdims=True) + epsilon)
            first[at] = (x * rate * gain_in[...]).astype(jnp.bfloat16)
            return carry

        lax.fori_loop(0, length // 64, norm, 0)
        lane = lax.broadcasted_iota(jnp.int32, (count, 2 * HEAD), 1)
        lse_out[...] = jnp.zeros_like(lse_out)

        def quad(n, carry):
            columns = pl.ds(pl.multiple_of(n * QUAD, QUAD), QUAD)
            own = pl.ds(length - count, count)
            q_out[:, columns] = dot32(first[own], w_in[0, :, columns]).astype(jnp.bfloat16)

            def project(i, inner):
                at = pl.ds(pl.multiple_of(i * count, count), count)
                block = first[at]
                k_out[at, columns] = dot32(block, w_in[1, :, columns]).astype(jnp.bfloat16)
                v_out[at, columns] = dot32(block, w_in[2, :, columns]).astype(jnp.bfloat16)
                return inner

            lax.fori_loop(0, length // count, project, 0)
            for pair in range(heads_in // 2):
                two = pl.ds(pl.multiple_of(n * QUAD + pair * 2 * HEAD, 2 * HEAD), 2 * HEAD)
                q_pair = q_out[:, two] * jnp.bfloat16(1.0 / math.sqrt(HEAD))
                k_pair = k_out[:, two]
                v_pair = v_out[:, two]
                parts = []
                for half in range(2):
                    head = n * heads_in + pair * 2 + half
                    inside = (lane >= HEAD) if half else (lane < HEAD)
                    q_one = jnp.where(inside, q_pair, jnp.bfloat16(0))
                    sbuf[...] = nt(q_one, k_pair)
                    slope = toe[head]

                    def soft(i, inner):
                        at = pl.ds(pl.multiple_of(i * CHUNK, CHUNK), CHUNK)
                        wide = sbuf[at, :far] + mask[at, :far]
                        tight = (
                            sbuf[at, far:] + mask[at, far:]
                            + pltpu.roll(slope, i * CHUNK, 1)
                        )
                        top = jnp.maximum(
                            jnp.max(wide, axis=1, keepdims=True), jnp.max(tight, axis=1, keepdims=True)
                        )
                        wide = jnp.exp(wide - top)
                        tight = jnp.exp(tight - top)
                        total = jnp.sum(wide, axis=1, keepdims=True) + jnp.sum(
                            tight, axis=1, keepdims=True
                        )
                        pbuf[at, :far] = wide.astype(jnp.bfloat16)
                        pbuf[at, far:] = tight.astype(jnp.bfloat16)
                        lsum[at] = jnp.broadcast_to(1.0 / total, (CHUNK, 2 * HEAD))
                        spot = lax.broadcasted_iota(jnp.int32, (CHUNK, 128), 1)
                        lse_out[at] = jnp.where(spot == head, top + jnp.log(total), lse_out[at])
                        return inner

                    lax.fori_loop(0, count // CHUNK, soft, 0, unroll=2)
                    parts.append(dot32(pbuf[...], v_pair) * lsum[...])
                o_out[:, two] = jnp.where(lane < HEAD, parts[0], parts[1]).astype(jnp.bfloat16)
            return carry

        lax.fori_loop(0, width // QUAD, quad, 0)

        def finish(n, carry):
            columns = pl.ds(pl.multiple_of(n * QUAD, QUAD), QUAD)
            x = t_in[pl.ds(length - count, count), columns].astype(jnp.float32)
            x_out[:, columns] = x + dot32(o_out[...], w_in[3, :, columns])
            return carry

        lax.fori_loop(0, width // QUAD, finish, 0)

    low = jnp.bfloat16
    return pl.pallas_call(
        kernel,
        name="attend_forward",
        out_shape=(
            jax.ShapeDtypeStruct((length, width), low),
            jax.ShapeDtypeStruct((count, width), low),
            jax.ShapeDtypeStruct((length, width), low),
            jax.ShapeDtypeStruct((length, width), low),
            jax.ShapeDtypeStruct((count, width), low),
            jax.ShapeDtypeStruct((count, 128), jnp.float32),
            jax.ShapeDtypeStruct((count, width), jnp.float32),
        ),
        in_specs=[pl.BlockSpec(memory_space=VMEM)] * 6,
        out_specs=[pl.BlockSpec(memory_space=VMEM)] * 7,
        scratch_shapes=[
            VMEM((count, length), jnp.float32),
            VMEM((count, length), low),
            VMEM((count, length), jnp.float32),
            VMEM((count, 2 * HEAD), jnp.float32),
        ],
        compiler_params=pltpu.CompilerParams(vmem_limit_bytes=56 * 1024 * 1024),
    )(tokens, weights, gain, query_seg, key_code, slopes)


def attend_backward(q_all, k_all, v_all, do_all, lse, query_seg, key_code, slopes):
    length, width = k_all.shape
    count = q_all.shape[0]
    band = slopes.shape[2]
    far = length - band
    heads = width // HEAD

    def kernel(q_in, k_in, v_in, do_in, lse_in, qseg, kcode, toe, dq_out, dk_out, dv_out, near_out, far_out, sbuf, dbuf, pbuf, gbuf, mask):
        fill_mask(mask, qseg, kcode, count, length)
        lane = lax.broadcasted_iota(jnp.int32, (count, 2 * HEAD), 1)

        def pair_step(n, carry):
            two = pl.ds(pl.multiple_of(n * 2 * HEAD, 2 * HEAD), 2 * HEAD)
            q_pair = q_in[:, two] * jnp.bfloat16(1.0 / math.sqrt(HEAD))
            do_pair = do_in[:, two]
            k_pair = k_in[:, two]
            v_pair = v_in[:, two]
            dq_parts, dk, dv = [], None, None
            for half in range(2):
                head = n * 2 + half
                inside = (lane >= HEAD) if half else (lane < HEAD)
                q_one = jnp.where(inside, q_pair, jnp.bfloat16(0))
                do_one = jnp.where(inside, do_pair, jnp.bfloat16(0))
                sbuf[...] = nt(q_one, k_pair)
                dbuf[...] = nt(do_one, v_pair)
                slope = toe[head]
                near_out[head] = jnp.zeros((CHUNK, band), jnp.float32)
                far_out[head] = jnp.zeros((CHUNK, 128), jnp.float32)

                def soft(i, inner):
                    at = pl.ds(pl.multiple_of(i * CHUNK, CHUNK), CHUNK)
                    spot = lax.broadcasted_iota(jnp.int32, (CHUNK, 128), 1)
                    level = jnp.sum(
                        jnp.where(spot == head, lse_in[at], 0.0), axis=1, keepdims=True
                    )
                    wide = jnp.exp(sbuf[at, :far] + mask[at, :far] - level)
                    tight = jnp.exp(
                        sbuf[at, far:] + mask[at, far:] + pltpu.roll(slope, i * CHUNK, 1) - level
                    )
                    pbuf[at, :far] = wide.astype(jnp.bfloat16)
                    pbuf[at, far:] = tight.astype(jnp.bfloat16)
                    d_wide = wide * dbuf[at, :far]
                    d_tight = tight * dbuf[at, far:]
                    delta = jnp.sum(d_wide, axis=1, keepdims=True) + jnp.sum(
                        d_tight, axis=1, keepdims=True
                    )
                    d_wide = d_wide - wide * delta
                    d_tight = d_tight - tight * delta
                    gbuf[at, :far] = d_wide.astype(jnp.bfloat16)
                    gbuf[at, far:] = d_tight.astype(jnp.bfloat16)
                    near_out[head] = near_out[head] + pltpu.roll(
                        d_tight, lax.rem(band - i * CHUNK, band), 1
                    )
                    summed = d_wide[:, :128]
                    for piece in range(1, far // 128):
                        summed = summed + d_wide[:, piece * 128 : (piece + 1) * 128]
                    far_out[head] = far_out[head] + summed
                    return inner

                lax.fori_loop(0, count // CHUNK, soft, 0, unroll=2)
                grads, probs = gbuf[...], pbuf[...]
                dq_parts.append(dot32(grads, k_pair))
                dk_half = tn(grads, q_one)
                dv_half = tn(probs, do_one)
                dk = dk_half if dk is None else dk + dk_half
                dv = dv_half if dv is None else dv + dv_half
            dq = jnp.where(lane < HEAD, dq_parts[0], dq_parts[1]) * (1.0 / math.sqrt(HEAD))
            dq_out[:, two] = dq.astype(jnp.bfloat16)
            dk_out[:, two] = dk.astype(jnp.bfloat16)
            dv_out[:, two] = dv.astype(jnp.bfloat16)
            return carry

        lax.fori_loop(0, width // (2 * HEAD), pair_step, 0)

    low = jnp.bfloat16
    return pl.pallas_call(
        kernel,
        name="attend_backward",
        out_shape=(
            jax.ShapeDtypeStruct((count, width), low),
            jax.ShapeDtypeStruct((length, width), low),
            jax.ShapeDtypeStruct((length, width), low),
            jax.ShapeDtypeStruct((heads, CHUNK, band), jnp.float32),
            jax.ShapeDtypeStruct((heads, CHUNK, 128), jnp.float32),
        ),
        in_specs=[pl.BlockSpec(memory_space=VMEM)] * 8,
        out_specs=[pl.BlockSpec(memory_space=VMEM)] * 5,
        scratch_shapes=[
            VMEM((count, length), jnp.float32),
            VMEM((count, length), jnp.float32),
            VMEM((count, length), low),
            VMEM((count, length), low),
            VMEM((count, length), jnp.float32),
        ],
        compiler_params=pltpu.CompilerParams(vmem_limit_bytes=56 * 1024 * 1024),
    )(q_all, k_all, v_all, do_all, lse, query_seg, key_code, slopes)


def per_device(
    tokens,
    segments,
    valid,
    routes,
    teacher,
    norm_attn,
    w_query,
    w_key,
    w_value,
    output_weight,
    rel_bias,
    norm_ffn,
    w_router,
    w_gate,
    w_up,
    w_down,
):
    nc = lax.axis_size("ctx")
    ns = lax.axis_size("shard")
    c, s = lax.axis_index("ctx"), lax.axis_index("shard")
    n_dev, nj = nc * ns, ns // 2
    row_count, width = tokens.shape[1:]
    top_count = routes.shape[2]
    experts = w_router.shape[1]
    capacity = (5 * row_count * top_count + 4 * experts - 1) // (4 * experts)
    length = row_count * nc
    low = jnp.bfloat16
    f32 = jnp.float32
    piece = w_query.shape[0]
    band = 2 * row_count

    smalls = (norm_attn, norm_ffn, rel_bias, w_router.reshape(-1))
    sizes = [x.shape[0] for x in smalls]
    head_row = jnp.concatenate(smalls + (jnp.zeros((width - sum(sizes),), low),))
    marks = jnp.concatenate(
        (
            segments[0].astype(low),
            valid[0].astype(low),
            jnp.zeros((width - 2 * row_count,), low),
        )
    )
    extra = jnp.concatenate(
        (head_row[None], marks[None], jnp.zeros((EXTRA - 2, width), low)), axis=0
    )
    weights, extras, tokens_all = gather_all(
        jnp.stack((w_query, w_key, w_value, output_weight)), extra, tokens[0], nc, ns
    )
    starts = [sum(sizes[:i]) for i in range(len(sizes))]
    gain_attn, gain_ffn, full_bias, full_router = (
        extras[:, 0, begin : begin + size].reshape(-1) for begin, size in zip(starts, sizes)
    )
    full_router = full_router.reshape(width, experts)
    table = full_bias.reshape(BUCKETS, HEADS).astype(f32)
    line_marks = lax.dynamic_slice_in_dim(extras.reshape(nc, ns, EXTRA, width), s, 1, 1)[:, 0, 1]
    line_marks = jnp.roll(line_marks, -(c + 1), axis=0)
    slot = jnp.arange(nc, dtype=jnp.int32)[:, None]
    past = slot >= nc - 1 - c
    line_seg = line_marks[:, :row_count].astype(jnp.int32)
    line_valid = line_marks[:, row_count : 2 * row_count] > 0
    key_code = jnp.where(line_valid & past, line_seg, -1).reshape(1, length)
    query_seg = segments[0][:, None]
    valid_count = jnp.sum(extras[:, 1, row_count : 2 * row_count].astype(f32))

    spot = (jnp.arange(band)[None, :] - jnp.arange(CHUNK)[:, None]) % band
    distance = jnp.where(spot <= row_count, row_count - spot, 3 * row_count - spot)
    level = bucket_of(distance, BUCKETS)
    level_hot = (level[:, :, None] == jnp.arange(BUCKETS)[None, None, :]).astype(f32)
    slopes = jnp.einsum(
        "ixb,bh->hix", level_hot, table - table[BUCKETS - 1 :], precision=highest_precision
    )

    gain_one = gain_attn.astype(f32)
    first_all, queries, keys, values, mixed_low, log_total, residual = attend_forward(
        tokens_all, weights, gain_one[None], query_seg, key_code, slopes
    )
    gain_two = gain_ffn.astype(f32)
    ffn_low = rms_norm(residual, gain_two).astype(low)
    ffn_in = ffn_low.astype(f32)
    router = full_router.astype(f32)
    logits = jnp.dot(ffn_in, router, precision=highest_precision)
    route_local = routes[0]
    expert_ids = jnp.arange(experts, dtype=jnp.int32)
    route_hot = route_local[:, :, None] == expert_ids[None, None, :]
    picked = jnp.sum(jnp.where(route_hot, logits[:, None, :], 0.0), axis=-1)
    gate_probs = jax.nn.softmax(picked, axis=-1)
    flat_routes = route_local.reshape(row_count * top_count)
    route_hits = (flat_routes[:, None] == expert_ids[None, :]).astype(jnp.int32)
    before = jnp.cumsum(route_hits, axis=0) - route_hits
    slot_rank = jnp.sum(before * route_hits, axis=1)
    target = (flat_routes * capacity + slot_rank).reshape(row_count, top_count)
    slot_ids = jnp.arange(experts * capacity, dtype=jnp.int32)
    pick_first = (slot_ids[:, None] == target[None, :, 0]).astype(low)
    pick_second = (slot_ids[:, None] == target[None, :, 1]).astype(low)

    def exchange(rows):
        return lax.all_to_all(
            rows.reshape(experts, capacity, width), "shard", split_axis=0, concat_axis=0, tiled=True
        ).reshape(experts * capacity, width)

    expert_rows = exchange(dot32(pick_first + pick_second, ffn_low).astype(low))
    gate_w, up_w, down_w = w_gate[0], w_up[0], w_down[0]
    gate_pre = dot32(expert_rows, gate_w)
    up_pre = dot32(expert_rows, up_w)

    def activation(gate_values, up_values):
        return jax.nn.gelu(gate_values) * up_values

    inner_value, activation_back = jax.vjp(activation, gate_pre, up_pre)
    inner = inner_value.astype(low)
    returned = exchange(dot32(inner, down_w).astype(low))
    picked_one, picked_two = tn(pick_first, returned), tn(pick_second, returned)
    output_sum = residual + gate_probs[:, :1] * picked_one + gate_probs[:, 1:] * picked_two
    valid_one = valid[0].astype(f32)
    deviation = output_sum - teacher[0].astype(f32)
    local_square = jnp.sum(valid_one[:, None] * deviation * deviation)
    everything = float(row_count * nc * ns)
    cotangent = everything / valid_count * deviation * valid_one[:, None]
    gate_grad = jnp.stack(
        (jnp.sum(cotangent * picked_one, axis=-1), jnp.sum(cotangent * picked_two, axis=-1)), axis=1
    )
    back_send = dot32(pick_first, (gate_probs[:, :1] * cotangent).astype(low)) + dot32(
        pick_second, (gate_probs[:, 1:] * cotangent).astype(low)
    )
    out_grad = exchange(back_send.astype(low))
    inner_grad = nt(out_grad, down_w)
    gate_pre_grad, up_pre_grad = activation_back(inner_grad)
    gate_low = gate_pre_grad.astype(low)
    up_low = up_pre_grad.astype(low)
    sent_back = exchange((nt(gate_low, gate_w) + nt(up_low, up_w)).astype(low))
    down_w_grad = tn(inner, out_grad).astype(low)
    gate_w_grad = tn(expert_rows, gate_low).astype(low)
    up_w_grad = tn(expert_rows, up_low).astype(low)
    gate_w_sum, up_w_sum, down_w_sum = (
        lax.psum_scatter(x[None], "ctx", scatter_dimension=1, tiled=True).astype(f32)
        for x in (gate_w_grad, up_w_grad, down_w_grad)
    )
    ffn_grad = tn(pick_first + pick_second, sent_back)
    pick_grad = gate_probs * (gate_grad - jnp.sum(gate_probs * gate_grad, axis=-1, keepdims=True))
    logits_grad = jnp.sum(jnp.where(route_hot, pick_grad[:, :, None], 0.0), axis=1)
    router_grad = contract(ffn_in, logits_grad, 0, 0, highest_precision)
    ffn_grad = ffn_grad + contract(logits_grad, router, 1, 1, highest_precision)
    unused, norm_two_back = jax.vjp(rms_norm, residual, gain_two)
    residual_from_norm, gain_two_grad = norm_two_back(ffn_grad)
    residual_grad = cotangent + residual_from_norm
    attn_grad_low = residual_grad.astype(low)
    out_w_grad = tn(mixed_low, attn_grad_low)
    mixed_grad = nt(attn_grad_low, weights[3]).astype(low)

    query_grad, key_grad, value_grad, near_sum, far_sum = attend_backward(
        queries, keys, values, mixed_grad, log_total, query_seg, key_code, slopes
    )
    bias_grad = jnp.einsum("hix,ixb->bh", near_sum, level_hot, precision=highest_precision)
    last_bucket = (jnp.arange(BUCKETS) == BUCKETS - 1).astype(f32)
    bias_grad = bias_grad + last_bucket[:, None] * jnp.sum(far_sum, axis=(1, 2))[None, :]
    first_own = first_all[length - row_count :]
    query_w_grad = tn(first_own, query_grad)
    key_w_grad = tn(first_all, key_grad)
    value_w_grad = tn(first_all, value_grad)
    hidden_grad = nt(key_grad, weights[1]) + nt(value_grad, weights[2])
    hidden_own = hidden_grad[length - row_count :] + nt(query_grad, weights[0])
    hidden_terms = jnp.concatenate((hidden_grad[: length - row_count], hidden_own), axis=0)
    inputs_all = tokens_all.astype(f32)
    rates_all = lax.rsqrt(jnp.mean(inputs_all * inputs_all, axis=-1, keepdims=True) + epsilon)
    gain_one_grad = jnp.sum(hidden_terms * inputs_all * rates_all, axis=0)

    small_grads = jnp.concatenate(
        [
            x.reshape(n_dev, -1).astype(low)
            for x in (gain_one_grad, gain_two_grad, bias_grad, router_grad)
        ],
        axis=1,
    )
    small_grads = jnp.pad(small_grads, ((0, 0), (0, width - small_grads.shape[1])))
    stacked = jnp.concatenate(
        [
            x.astype(low).reshape(n_dev, piece, width)
            for x in (query_w_grad, key_w_grad, value_w_grad, out_w_grad)
        ]
        + [jnp.pad(small_grads[:, None], ((0, 0), (0, EXTRA - 1), (0, 0)))],
        axis=1,
    ).reshape(nc, nj, 2, 4 * piece + EXTRA, width)
    squares = jnp.full((8, 128), local_square, f32)
    summed, square_sum, hidden_sum = reduce_all(
        stacked, squares, hidden_grad.astype(low).reshape(nc, row_count, width), hidden_own, nc, ns
    )
    loss_value = square_sum[0, 0] / (2.0 * width * valid_count)
    inputs = inputs_all[length - row_count :]
    rate = rates_all[length - row_count :]
    scaled = hidden_sum * gain_one
    input_grad = (
        residual_grad
        + rate * scaled
        - inputs * (rate * rate * rate) * jnp.mean(scaled * inputs, axis=-1, keepdims=True)
    )
    tail = summed[4 * piece]
    tails = [tail[begin : begin + size] for begin, size in zip(starts, sizes)]
    return (
        output_sum.astype(low)[None],
        loss_value,
        input_grad[None],
        tails[0],
        summed[:piece],
        summed[piece : 2 * piece],
        summed[2 * piece : 3 * piece],
        summed[3 * piece : 4 * piece],
        tails[2],
        tails[1],
        tails[3].reshape(w_router.shape),
        gate_w_sum,
        up_w_sum,
        down_w_sum,
    )


def solution(mesh):
    return jax.shard_map(
        per_device,
        mesh=mesh,
        in_specs=(
            P("shard", "ctx", None),
            P("shard", "ctx"),
            P("shard", "ctx"),
            P("shard", "ctx", None),
            P("shard", "ctx", None),
            P(("ctx", "shard")),
            P(("ctx", "shard"), None),
            P(("ctx", "shard"), None),
            P(("ctx", "shard"), None),
            P(("ctx", "shard"), None),
            P(("ctx", "shard")),
            P(("ctx", "shard")),
            P(("ctx", "shard"), None),
            P("shard", None, None),
            P("shard", None, None),
            P("shard", None, None),
        ),
        out_specs=(
            P("shard", "ctx", None),
            P(),
            P("shard", "ctx", None),
            P(("ctx", "shard")),
            P(("ctx", "shard"), None),
            P(("ctx", "shard"), None),
            P(("ctx", "shard"), None),
            P(("ctx", "shard"), None),
            P(("ctx", "shard")),
            P(("ctx", "shard")),
            P(("ctx", "shard"), None),
            P("shard", "ctx", None),
            P("shard", "ctx", None),
            P("shard", "ctx", None),
        ),
        check_vma=False,
    )
```

time: 1810 us -> 651 us (0.36)
  waiting for transfers between devices: 1240 us -> 74.3 us
  Pallas kernels: 0 us -> 329 us
  blocking collectives: 243 us -> 20.9 us
  matrix products: 149 us -> 115 us
  local copies, waits for them, and re-layouts: 70.6 us -> 38.2 us
  loops' own time: 26.9 us -> 0 us
    reduce_scatter x9 -> x3, waiting for transfers between devices: 890 us -> 29.2 us  [per_device(): lax.psum_scatter(x[None], 'ctx', scatter_dimension=1, tiled=True)]
    pallas_call x0 -> x4, Pallas kernels: none -> 329 us  [the longest x1 137 us: reduce_all(): pl.pallas_call(kernel, name='reduce_all', out_shape=(jax.ShapeDtypeStruct...]
    all_gather x6 -> x0, waiting for transfers between devices: 211 us -> none  [the longest x1 54.7 us: per_device(): lax.all_gather(w_key, ('ctx', 'shard'), axis=0, tiled=True)]
    unnamed x17 -> x3, waiting for transfers between devices: 134 us -> 0.05 us
    psum x2 -> x0, blocking collectives: 101 us -> none  [per_device(): lax.psum((local_square, jnp.sum(valid_one)), ('ctx', 'shard'))]
    all_gather x3 -> x0, blocking collectives: 57.7 us -> none  [the longest x1 39.9 us: per_device(): lax.all_gather(w_router, ('ctx', 'shard'), axis=0, tiled=True)]
    dot_general x20 -> x8, matrix products: 71.1 us -> 28.7 us  [the longest x6 26.3 us: dot32(): return jnp.dot(left_side, right_side, preferred_element_type=jnp.float32)]
    unnamed x1 -> x0, blocking collectives: 42.2 us -> none
  transfers between devices with their start and end apart: 18 -> 6, of which waited for: 17 -> 4; matrix products, arithmetic and copies ran while one was open for 7% -> 18% of each run, Pallas kernels for 0% -> 30%
where the time goes in v1:
time: 651 us; the launch traced here: 639 us
  Pallas kernels  329 us (51%)
  matrix products  115 us (18%)
  waiting for transfers between devices  74.3 us (11%)
  local copies, waits for them, and re-layouts  38.2 us (6%)
  other arithmetic  30.8 us (5%)
  blocking collectives  20.9 us (3%)
  between operations  18 us (3%)
  starting transfers between devices  12.4 us (2%)
    pallas_call x1, Pallas kernels, reduce_all(): pl.pallas_call(kernel, name='reduce_all', out_shape=(jax.ShapeDtypeStruct...  137 us
    dot_general x19, matrix products, contract(): lax.dot_general(left_side, right_side, (((left_axis,), (right_axis,)), ((...  86.4 us
    pallas_call x1, Pallas kernels, gather_all(): pl.pallas_call(kernel, name='gather_all', out_shape=(jax.ShapeDtypeStruct...  73.9 us
    pallas_call x1, Pallas kernels, attend_forward(): pl.pallas_call(kernel, name='attend_forward', out_shape=(jax.ShapeDtypeSt...  61.5 us
    pallas_call x1, Pallas kernels, attend_backward(): pl.pallas_call(kernel, name='attend_backward', out_shape=(jax.ShapeDtypeS...  57.3 us
    all_to_all x3, waiting for transfers between devices, exchange(): lax.all_to_all(rows.reshape(experts, capacity, width), 'shard', split_axi...  45 us
    reduce_scatter x3, waiting for transfers between devices, per_device(): lax.psum_scatter(x[None], 'ctx', scatter_dimension=1, tiled=True)  29.2 us
    dot_general x6, matrix products, dot32(): return jnp.dot(left_side, right_side, preferred_element_type=jnp.float32)  26.3 us
  transfers between devices with their start and end apart: 6, of which 4 were waited for; matrix products, arithmetic and copies ran while one was open for 18% of the time, Pallas kernels for 30%

profile of v1, /device:TPU:0, one launch (start us, length us, event | category | flops | bytes accessed | tf_op | source)
XLA Modules:
  0.0 639.3 jit_solution(6492585665616673831)
XLA Ops:
  14.6 73.9 %gather_all.1 = (bf16[4,1024,1024]{2,1,0:T(8,128)(2,1)}, bf16[32,16,1024]{2,1,0:T(8,128)(2,1)}, bf16[4,256,1024]{2,1,0:T(8,128)(2,1)}) custom-call(bf16[4,32,1024]{2,1,0:T(8,128)(2,1)} %pad_maximum_fusion.1.w_in, bf16[16,1024]{1,0:T(8,128)(2,1)} %maximum_maximum_fusion.e_in, bf16[256,1024]{1,0:T(8,128)(2,1)} %bitcast.184), custom_call_target="tpu_custom_call" | custom-call | tf_op jit(solution)/shard_map/gather_all/pallas_call | solution.py:232
  97.8 61.5 %attend_forward.1 = (bf16[1024,1024]{1,0:T(8,128)(2,1)}, bf16[256,1024]{1,0:T(8,128)(2,1)}, bf16[1024,1024]{1,0:T(8,128)(2,1)}, bf16[1024,1024]{1,0:T(8,128)(2,1...) custom-call(bf16[1024,1024]{1,0:T(8,128)(2,1)} %bitcast.165, ...), custom_call_target="tpu_custom_call" | custom-call | tf_op jit(solution)/shard_map/attend_forward/pallas_call | solution.py:545
  163.8 4.1 all-to-all-start
  168.0 18.0 %all-to-all-done = bf16[8,80,1024]{2,1,0:T(8,128)(2,1)S(1)} async-done(((bf16[8,80,1024]{2,1,0:T(8,128)(2,1)}), bf16[8,80,1024]{2,1,0:T(8,128)(2,1)S(1)}, u32[]{:S(2)}, u32[]{:S(2)}) %all-to-all-start) | async-done | bytes 1310752 | tf_op jit(solution)/shard_map/all_to_all | solution.py:763
  186.0 7.0 %fusion.17 = f32[640,2816]{1,0:T(8,128)S(1)} fusion(bf16[640,1024]{1,0:T(8,128)(2,1)S(1)} %bitcast.176, bf16[1,1024,2816]{2,1,0:T(8,128)(2,1)} %param.29), kind=kOutput, calls=%fused_computation.22 | convolution fusion | flops 3690987520 | bytes 14286848 | tf_op jit(solution)/shard_map/dot_general | solution.py:60
  193.1 11.5 %multiply_convert_fusion.1 = (bf16[640,2816]{1,0:T(8,128)(2,1)S(1)}, f32[640,2816]{1,0:T(8,128)}) fusion(f32[640,2816]{1,0:T(8,128)S(1)} %fusion.17, bf16[640,1024]{1,0:T(8,128)(2,1)S(1)} %bitcast.177, bf16[1,1024,2816]{2,1,0:T(8,128)(2,1)} %param.30), kind=kOutput, calls=%fused_computation.10 | convolution fusion | flops 3709009920 | bytes 25100288 | tf_op jit(solution)/shard_map/dot_general | solution.py:60
  204.6 5.0 fusion.39
  209.6 3.7 all-to-all-start.1
  217.4 14.0 %all-to-all-done.1 = bf16[8,80,1024]{2,1,0:T(8,128)(2,1)S(1)} async-done(((bf16[8,80,1024]{2,1,0:T(8,128)(2,1)}), bf16[8,80,1024]{2,1,0:T(8,128)(2,1)S(1)}, u32[]{:S(2)}, u32[]{:S(2)}) %all-to-all-start.1) | async-done | bytes 1310752 | tf_op jit(solution)/shard_map/all_to_all | solution.py:763
  237.1 20.9 %all_to_all.20 = bf16[8,80,1024]{2,1,0:T(8,128)(2,1)S(1)} all-to-all(bf16[8,80,1024]{2,1,0:T(8,128)(2,1)S(1)} %bitcast.170), channel_id=1, replica_groups=mesh['ctx'=4,'shard'=8] {'shard'}, dimensions={0} | all-to-all | bytes 2621440 | tf_op jit(solution)/shard_map/all_to_all | solution.py:763
  259.1 6.6 %convert_bitcast_fusion = bf16[1,2816,1024]{2,1,0:T(8,128)(2,1)} fusion(bf16[640,2816]{1,0:T(8,128)(2,1)S(1)} %copy-done.20, bf16[640,1024]{1,0:T(8,128)(2,1)S(1)} %bitcast.182), kind=kOutput, calls=%fused_computation.24 | convolution fusion | flops 3693871104 | bytes 10682368 | tf_op jit(solution)/shard_map/dot_general | solution.py:50
  265.7 16.7 %fusion.6 = (bf16[640,2816]{1,0:T(8,128)(2,1)}, bf16[640,2816]{1,0:T(8,128)(2,1)S(1)}) fusion(f32[640,2816]{1,0:T(8,128)} %copy-done.18, f32[640,2816]{1,0:T(8,128)} %get-tuple-element.129, bf16[640,1024]{1,0:T(8,128)(2,1)} %bitcast.183, bf16[1,2816,1024]{2,1,0:T(8,128)(2,1)} %param.31), kind=kOutput, calls=%fused_computation.8 | convolution fusion | flops 3734241280 | bytes 28704768 | tf_op jit(solution)/shard_map/dot_general | solution.py:50
  284.3 6.6 %convert_bitcast_fusion.1 = bf16[1,1024,2816]{2,1,0:T(8,128)(2,1)} fusion(bf16[640,1024]{1,0:T(8,128)(2,1)S(1)} %bitcast.178, bf16[640,2816]{1,0:T(8,128)(2,1)S(1)} %get-tuple-element.118), kind=kOutput, calls=%fused_computation.25 | convolution fusion | flops 3693871104 | bytes 10682368 | tf_op jit(solution)/shard_map/dot_general | solution.py:50
  291.1 8.6 %convert_bitcast_fusion.2 = bf16[1,1024,2816]{2,1,0:T(8,128)(2,1)} fusion(bf16[640,1024]{1,0:T(8,128)(2,1)S(1)} %bitcast.179, bf16[640,2816]{1,0:T(8,128)(2,1)} %get-tuple-element.117), kind=kOutput, calls=%fused_computation.26 | convolution fusion | flops 3693871104 | bytes 10682368 | tf_op jit(solution)/shard_map/dot_general | solution.py:50
  303.4 7.2 %fusion.11 = f32[640,1024]{1,0:T(8,128)S(1)} fusion(bf16[640,2816]{1,0:T(8,128)(2,1)} %copy-done.22, bf16[1,1024,2816]{2,1,0:T(8,128)(2,1)} %param.30), kind=kOutput, calls=%fused_computation.16 | convolution fusion | flops 3690987520 | bytes 11993088 | tf_op jit(solution)/shard_map/dot_general | solution.py:50
  310.6 7.6 %add_convert_fusion = bf16[640,1024]{1,0:T(8,128)(2,1)} fusion(f32[640,1024]{1,0:T(8,128)S(1)} %fusion.11, bf16[640,2816]{1,0:T(8,128)(2,1)S(1)} %copy-done.21, bf16[1,1024,2816]{2,1,0:T(8,128)(2,1)} %param.29), kind=kOutput, calls=%fused_computation.33 | convolution fusion | flops 3692298240 | bytes 13303808 | tf_op jit(solution)/shard_map/dot_general | solution.py:50
  318.2 4.3 all-to-all-start.3
  327.7 13.0 %all-to-all-done.3 = bf16[8,80,1024]{2,1,0:T(8,128)(2,1)} async-done(((bf16[8,80,1024]{2,1,0:T(8,128)(2,1)}), bf16[8,80,1024]{2,1,0:T(8,128)(2,1)}, u32[]{:S(2)}, u32[]{:S(2)}) %all-to-all-start.3) | async-done | bytes 1310752 | tf_op jit(solution)/shard_map/all_to_all | solution.py:763
  340.7 3.4 multiply_reduce_fusion
  350.2 57.3 %attend_backward.1 = (bf16[256,1024]{1,0:T(8,128)(2,1)}, bf16[1024,1024]{1,0:T(8,128)(2,1)}, bf16[1024,1024]{1,0:T(8,128)(2,1)}, f32[16,16,512]{2,1,0:T(8,128)}, f32[16,16,128]{2,1,0:T(8,128)}) custom-call(bf16[256,1024]{1,0:T(8,128)(2,1)} %get-tuple-element.37.q_in, bf16[1024,1024]{1,0:T(8,128)(2,1)} %get-tuple-element.38.k_in, ...), custom_call_target="tpu_custom_call" | custom-call | tf_op jit(solution)/shard_map/attend_backward/pallas_call | solution.py:644
  410.6 4.7 fusion.24
  415.3 5.3 fusion.106
  443.7 136.7 %reduce_all.1 = (f32[144,1024]{1,0:T(8,128)}, f32[8,128]{1,0:T(8,128)}, f32[256,1024]{1,0:T(8,128)}) custom-call(bf16[4,4,2,144,1024]{4,3,2,1,0:T(8,128)(2,1)} %constant_dynamic-update-slice_fusion.g_in, f32[8,128]{1,0:T(8,128)} %broadcast_in_dim.103.q_in, bf16[4,256,1024]{2,1,0:T(8,128)(2,1)} %bitcast.175, f32[256,1024]{1,0:T(8,128)} %copy-done.5), custom_call_target="tpu_custom_call" | custom-call | tf_op jit(solution)/shard_map/reduce_all/pallas_call | solution.py:404
  598.9 29.2 %reduce-scatter.4.cloned.1.call-done = bf16[1,256,2816]{2,1,0:T(8,128)(2,1)} async-done(((bf16[1,1024,2816]{2,1,0:T(8,128)(2,1)}), bf16[1,256,2816]{2,1,0:T(8,128)(2,1)}) %reduce-scatter.4.cloned.1.call-update) | async-done | bytes 1441808 | tf_op jit(solution)/shard_map/reduce_scatter | solution.py:801
  (170 shorter events, 94.5 us)
Async XLA Ops:
  159.3 8.6 %copy-start.14 = (s32[1,256]{1,0:T(1,128)S(1)}, s32[1,256]{1,0:T(1,128)}, u32[]{:S(2)}) copy-start(s32[1,256]{1,0:T(1,128)} %param.18) | copy-start | bytes 3076
  162.1 55.0 %copy-start.6 = (bf16[256,1024]{1,0:T(8,128)(2,1)}, bf16[256,1024]{1,0:T(8,128)(2,1)S(1)}, u32[]{:S(2)}) copy-start(bf16[256,1024]{1,0:T(8,128)(2,1)S(1)} %multiply_convert_fusion.4) | copy-start | bytes 1572868
  163.8 22.2 %all-to-all-start = ((bf16[8,80,1024]{2,1,0:T(8,128)(2,1)}), bf16[8,80,1024]{2,1,0:T(8,128)(2,1)S(1)}, u32[]{:S(2)}, u32[]{:S(2)}) async-start(bf16[8,80,1024]{2,1,0:T(8,128)(2,1)} %bitcast.16), calls=%async_computation | async-start | bytes 2621440 | tf_op jit(solution)/shard_map/all_to_all | solution.py:763
  186.0 7.1 %copy-start.9 = (bf16[8,80,1024]{2,1,0:T(8,128)(2,1)}, bf16[8,80,1024]{2,1,0:T(8,128)(2,1)S(1)}, u32[]{:S(2)}) copy-start(bf16[8,80,1024]{2,1,0:T(8,128)(2,1)S(1)} %all-to-all-done) | copy-start | bytes 3932164
  186.0 18.6 %slice-start = ((s8[5767168]{0:T(1024)(128)(4,1)}), s8[4194304]{0:T(1024)(128)(4,1)S(1)}, s32[]{:S(2)}) async-start(s8[5767168]{0:T(1024)(128)(4,1)} %bitcast.208), calls=%async_computation.10 | async-start | bytes 8388608
  193.1 11.5 %copy-start.18 = (f32[640,2816]{1,0:T(8,128)}, f32[640,2816]{1,0:T(8,128)S(1)}, u32[]{:S(2)}) copy-start(f32[640,2816]{1,0:T(8,128)S(1)} %fusion.17) | copy-start | bytes 21626884
  193.1 11.5 %slice-start.1 = ((s8[5767168]{0:T(1024)(128)(4,1)}), s8[1572864]{0:T(1024)(128)(4,1)S(1)}, s32[]{:S(2)}) async-start(s8[5767168]{0:T(1024)(128)(4,1)} %bitcast.208), calls=%async_computation.11 | async-start | bytes 3145728
  204.6 5.0 copy-start.19
  209.6 22.5 %copy-start = (f32[256,1024]{1,0:T(8,128)S(1)}, f32[256,1024]{1,0:T(8,128)}, u32[]{:S(2)}) copy-start(f32[256,1024]{1,0:T(8,128)} %get-tuple-element.35) | copy-start | bytes 3145732
  209.6 21.9 %all-to-all-start.1 = ((bf16[8,80,1024]{2,1,0:T(8,128)(2,1)}), bf16[8,80,1024]{2,1,0:T(8,128)(2,1)S(1)}, u32[]{:S(2)}, u32[]{:S(2)}) async-start(bf16[8,80,1024]{2,1,0:T(8,128)(2,1)} %bitcast.181), calls=%async_computation.1 | async-start | bytes 2621440 | tf_op jit(solution)/shard_map/all_to_all | solution.py:763
  213.3 379.0 %reduce-scatter.8.cloned.1.call-start = ((), (), s32[]{:S(2)}) async-start(), calls=%async_computation.9 | async-start | bytes 7208960 | tf_op jit(solution)/shard_map/reduce_scatter | solution.py:801
  232.1 2.6 copy-start.8
  236.5 22.6 %copy-start.20 = (bf16[640,2816]{1,0:T(8,128)(2,1)S(1)}, bf16[640,2816]{1,0:T(8,128)(2,1)}, u32[]{:S(2)}) copy-start(bf16[640,2816]{1,0:T(8,128)(2,1)} %copy-done.19) | copy-start | bytes 10813444
  265.7 330.0 %reduce-scatter.6.cloned.1.call-start = ((), (), s32[]{:S(2)}) async-start(), calls=%async_computation.8 | async-start | bytes 7208960 | tf_op jit(solution)/shard_map/reduce_scatter | solution.py:801
  265.7 18.5 %copy-start.10 = (bf16[8,80,1024]{2,1,0:T(8,128)(2,1)S(1)}, bf16[8,80,1024]{2,1,0:T(8,128)(2,1)}, u32[]{:S(2)}) copy-start(bf16[8,80,1024]{2,1,0:T(8,128)(2,1)} %copy-done.9) | copy-start | bytes 3932164
  282.5 1.8 copy-start.22
  290.9 337.2 %reduce-scatter.4.cloned.1.call-start = ((), (), s32[]{:S(2)}) async-start(), calls=%async_computation.7 | async-start | bytes 7208960 | tf_op jit(solution)/shard_map/reduce_scatter | solution.py:801
  303.4 7.2 %copy-start.21 = (bf16[640,2816]{1,0:T(8,128)(2,1)S(1)}, bf16[640,2816]{1,0:T(8,128)(2,1)}, u32[]{:S(2)}) copy-start(bf16[640,2816]{1,0:T(8,128)(2,1)} %get-tuple-element.117) | copy-start | bytes 10813444
  318.2 22.5 %all-to-all-start.3 = ((bf16[8,80,1024]{2,1,0:T(8,128)(2,1)}), bf16[8,80,1024]{2,1,0:T(8,128)(2,1)}, u32[]{:S(2)}, u32[]{:S(2)}) async-start(bf16[8,80,1024]{2,1,0:T(8,128)(2,1)} %bitcast.180), calls=%async_computation.3 | async-start | bytes 2621440 | tf_op jit(solution)/shard_map/all_to_all | solution.py:763
  410.6 4.8 copy-start.16
  426.1 3.4 copy-start.13
  426.1 3.4 copy-start.17
  432.0 2.3 copy-start.15
  436.8 2.1 copy-start.12
  (7 other events, 8.5 us)
Sparse Core Ops, SparseCore 0:
  265.8 99.5 reduce-scatter.7
  367.7 117.4 reduce-scatter.5
  487.5 140.4 reduce-scatter.3

commit v2 on v1

v2 whole, which is shorter than its diff:
```python
import math

import jax
import jax.numpy as jnp
from jax import lax
from jax.experimental import pallas as pl
from jax.experimental.pallas import tpu as pltpu
from jax.sharding import PartitionSpec as P

HEADS = 16
HEAD = 64
BUCKETS = 32
MESH = pl.DeviceIdType.MESH
ANY = pl.ANY
VMEM = pltpu.VMEM
SEM = pltpu.SemaphoreType

highest_precision = lax.Precision.HIGHEST
max_distance = 128
epsilon = 1e-06
negative = -1e30
EXTRA = 16


def thresholds(buckets):
    exact_count = buckets // 2
    limits = list(range(1, exact_count))
    for bucket_level in range(exact_count, buckets):
        power = (bucket_level - exact_count) / exact_count
        limits.append(int(math.ceil(exact_count * (max_distance / exact_count) ** power)))
    return limits


def bucket_of(distance, buckets):
    bucket_total = jnp.zeros(distance.shape, jnp.int32)
    for threshold in thresholds(buckets):
        bucket_total = bucket_total + (distance >= threshold).astype(jnp.int32)
    return bucket_total


def rms_norm(values, gain_vector):
    return (
        values
        * lax.rsqrt(jnp.mean(values * values, axis=-1, keepdims=True) + epsilon)
        * gain_vector
    )


def contract(left_side, right_side, left_axis, right_axis, precision_mode=None):
    return lax.dot_general(
        left_side,
        right_side,
        (((left_axis,), (right_axis,)), ((), ())),
        precision=precision_mode,
        preferred_element_type=jnp.float32,
    )


def dot32(left_side, right_side):
    return jnp.dot(left_side, right_side, preferred_element_type=jnp.float32)


def nt(left_side, right_side):
    return contract(left_side, right_side, 1, 1)


def tn(left_side, right_side):
    return contract(left_side, right_side, 0, 0)


class Place:
    def __init__(self, nc, ns):
        self.nc, self.ns, self.nj = nc, ns, ns // 2
        self.c = lax.axis_index("ctx")
        self.s = lax.axis_index("shard")
        self.core = self.s % 2
        self.j = self.s // 2

    def along(self, d):
        return (lax.rem(self.c + d + self.nc, self.nc), self.s)

    def across(self, k):
        return (self.c, self.s ^ (2 * k))

    def twin(self):
        return (self.c, self.s ^ 1)

    def greet(self):
        barrier = pltpu.get_barrier_semaphore()
        partners = (
            [self.along(d) for d in range(1, self.nc)]
            + [self.across(k) for k in range(1, self.nj)]
            + [self.twin()]
        )
        for partner in partners:
            pl.semaphore_signal(barrier, inc=1, device_id=partner, device_id_type=MESH)
        pl.semaphore_wait(barrier, len(partners))


def remote(source, target, send, recv, device):
    return pltpu.make_async_remote_copy(
        src_ref=source,
        dst_ref=target,
        send_sem=send,
        recv_sem=recv,
        device_id=device,
        device_id_type=MESH,
    )


def gather_all(weights, extra, rows, nc, ns):
    n_dev, nj = nc * ns, ns // 2
    share = weights.shape[1:]
    full_shape = (share[0], nc, ns) + share[1:]

    def kernel(w_in, e_in, t_in, w_out, e_out, t_out, local, zs, zr, xs, xr, cs, cr, ts, tr):
        me = Place(nc, ns)

        def views(row, column):
            return (w_out.at[:, row, column], e_out.at[row, column])

        def piece(d, k):
            return views(lax.rem(me.c - d + nc, nc), me.s ^ (2 * k))

        mine = (w_in.at[me.c], e_in)
        locals_ = [
            pltpu.make_async_copy(source, target, local.at[i])
            for i, (source, target) in enumerate(
                zip(mine + (t_in,), views(me.c, me.s) + (t_out.at[me.c],))
            )
        ]
        for copy in locals_:
            copy.start()
        me.greet()
        sent = []

        def push(sources, targets, send, recv, device):
            for i in range(2):
                copy = remote(sources[i], targets[i], send.at[i], recv.at[i], device)
                copy.start()
                sent.append(copy)

        def arrive(targets, send, recv, device):
            for i in range(2):
                remote(targets[i], targets[i], send.at[i], recv.at[i], device).wait_recv()

        def token_copy(direction, hop):
            lane = 0 if direction > 0 else 1
            origin = lax.rem(me.c - direction * hop + nc, nc)
            return remote(
                t_in if hop == 0 else t_out.at[origin],
                t_out.at[origin],
                ts.at[lane, hop],
                tr.at[lane, hop],
                (lax.rem(me.c + direction + nc, nc), me.s),
            )

        def token_landing(direction, hop):
            lane = 0 if direction > 0 else 1
            origin = lax.rem(me.c - direction * (hop + 1) + nc, nc)
            landing = t_out.at[origin]
            return remote(landing, landing, ts.at[lane, hop], tr.at[lane, hop], me.along(1))

        def can_send(direction, hop):
            if direction > 0:
                return (me.c >= hop) & (me.c < nc - 1)
            return (me.c <= nc - 1 - hop) & (me.c > 0)

        def can_receive(direction, hop):
            if direction > 0:
                return me.c >= hop + 1
            return me.c <= nc - 2 - hop

        for d in range(1, nc):
            target = lax.rem(me.c + d, nc)
            push(
                (w_in.at[target], e_in), views(me.c, me.s), zs.at[d], zr.at[d], (target, me.s)
            )
        for direction in (1, -1):

            @pl.when(can_send(direction, 0))
            def _():
                token_copy(direction, 0).start()

        for k in range(1, nj):
            push(mine, views(me.c, me.s), xs.at[0, k], xr.at[0, k], me.across(k))
        push(mine, views(me.c, me.s), cs.at[0, 0], cr.at[0, 0], me.twin())

        for copy in locals_:
            copy.wait()
        for d in range(1, nc):
            here = piece(d, 0)
            arrive(here, zs.at[d], zr.at[d], me.along(-d))
            for k in range(1, nj):
                push(here, here, xs.at[d, k], xr.at[d, k], me.across(k))
            push(here, here, cs.at[d, 0], cr.at[d, 0], me.twin())
        for d in range(nc):
            for k in range(1, nj):
                here = piece(d, k)
                arrive(here, xs.at[d, k], xr.at[d, k], me.across(k))
                push(here, here, cs.at[d, k], cr.at[d, k], me.twin())
            if d < nc - 2:
                for direction in (1, -1):

                    @pl.when(can_receive(direction, d))
                    def _():
                        token_landing(direction, d).wait_recv()

                    @pl.when(can_send(direction, d + 1))
                    def _():
                        token_copy(direction, d + 1).start()

        for d in range(nc):
            for k in range(nj):
                here = views(lax.rem(me.c - d + nc, nc), me.s ^ 1 ^ (2 * k))
                arrive(here, cs.at[d, k], cr.at[d, k], me.twin())
        for direction in (1, -1):

            @pl.when(can_receive(direction, nc - 2))
            def _():
                token_landing(direction, nc - 2).wait_recv()

        for copy in sent:
            copy.wait_send()
        for direction in (1, -1):
            for hop in range(nc - 1):

                @pl.when(can_send(direction, hop))
                def _():
                    token_copy(direction, hop).wait_send()

    full, extras, tokens = pl.pallas_call(
        kernel,
        name="gather_all",
        out_shape=(
            jax.ShapeDtypeStruct(full_shape, weights.dtype),
            jax.ShapeDtypeStruct((nc, ns) + extra.shape, extra.dtype),
            jax.ShapeDtypeStruct((nc,) + rows.shape, rows.dtype),
        ),
        in_specs=[pl.BlockSpec(memory_space=ANY)] * 3,
        out_specs=[pl.BlockSpec(memory_space=ANY)] * 3,
        scratch_shapes=[
            SEM.DMA((3,)),
            SEM.DMA((nc, 2)),
            SEM.DMA((nc, 2)),
            SEM.DMA((nc, nj, 2)),
            SEM.DMA((nc, nj, 2)),
            SEM.DMA((nc, nj, 2)),
            SEM.DMA((nc, nj, 2)),
            SEM.DMA((2, nc)),
            SEM.DMA((2, nc)),
        ],
        compiler_params=pltpu.CompilerParams(collective_id=1, has_side_effects=True),
    )(weights, extra, rows)
    return (
        full.reshape(share[0], n_dev * share[1], share[2]),
        extras,
        tokens.reshape(nc * rows.shape[0], rows.shape[1]),
    )


def reduce_all(grads, small, squares, nc, ns, kept):
    nj = ns // 2
    parts, piece, width = grads.shape[0], grads.shape[4], grads.shape[5]
    low = grads.dtype
    tile = squares.shape

    def kernel(g_in, e_in, q_in, k_out, g_out, e_out, q_out,
               gt, et, gc, ec, gx, ex, gz, ez, qz, qx, qc, qa, qb,
               cs, cr, xs, xr, zs, zr, q1s, q1r, q2s, q2r, q3s, q3r):
        me = Place(nc, ns)
        me.greet()

        def both(pairs, send, recv, device):
            return [
                remote(source, target, send.at[i], recv.at[i], device)
                for i, (source, target) in enumerate(pairs)
            ]

        def core_copy(d):
            row = lax.rem(me.c + d, nc)
            other = 1 - me.core
            return both(
                ((g_in.at[:, row, :, other], gc.at[d]), (e_in.at[row, :, other], ec.at[d])),
                cs.at[d], cr.at[d], me.twin(),
            )

        def cross_copy(d, k):
            return both(
                ((gt.at[d, :, me.j ^ k], gx.at[d, k - 1]), (et.at[d, me.j ^ k], ex.at[d, k - 1])),
                xs.at[d, k], xr.at[d, k], me.across(k),
            )

        def along_copy(d):
            return both(
                ((gt.at[d, :, me.j], gz.at[d - 1]), (et.at[d, me.j], ez.at[d - 1])),
                zs.at[d], zr.at[d], me.along(d),
            )

        def start(copies):
            for copy in copies:
                copy.start()

        def landed(copies):
            for copy in copies:
                copy.wait_recv()

        def q_along(d):
            return remote(q_in, qz.at[d - 1], q1s.at[d], q1r.at[d], me.along(d))

        def q_across(k):
            return remote(qa, qx.at[k - 1], q2s.at[k], q2r.at[k], me.across(k))

        q_twin = remote(qb, qc, q3s.at[0], q3r.at[0], me.twin())
        order = list(range(1, nc)) + [0]
        for d in order:
            start(core_copy(d))
        for d in range(1, nc):
            q_along(d).start()

        for d in order:
            landed(core_copy(d))
            row = lax.rem(me.c + d, nc)

            def add_core(i, carry):
                for k in range(nj):
                    gt[d, i, k] = (
                        g_in[i, row, k, me.core].astype(jnp.float32)
                        + gc[d, i, k].astype(jnp.float32)
                    ).astype(low)
                return carry

            lax.fori_loop(0, parts, add_core, 0)
            for k in range(nj):
                et[d, k] = (
                    e_in[row, k, me.core].astype(jnp.float32) + ec[d, k].astype(jnp.float32)
                ).astype(low)
            for k in range(1, nj):
                start(cross_copy(d, k))
        for d in range(1, nc):
            q_along(d).wait_recv()
        value = q_in[...]
        for d in range(1, nc):
            value = value + qz[d - 1]
        qa[...] = value
        for k in range(1, nj):
            q_across(k).start()
        for d in order:
            for k in range(1, nj):
                landed(cross_copy(d, k))

            def add_cross(i, carry):
                value = gt[d, i, me.j].astype(jnp.float32)
                for k in range(1, nj):
                    value = value + gx[d, k - 1, i].astype(jnp.float32)
                if d == 0:
                    g_out[i] = value
                else:
                    gt[d, i, me.j] = value.astype(low)
                return carry

            lax.fori_loop(0, parts, add_cross, 0)
            value = et[d, me.j].astype(jnp.float32)
            for k in range(1, nj):
                value = value + ex[d, k - 1].astype(jnp.float32)
            if d:
                et[d, me.j] = value.astype(low)
                start(along_copy(d))
            else:
                e_out[...] = value
        for k in range(1, nj):
            q_across(k).wait_recv()
        value = qa[...]
        for k in range(1, nj):
            value = value + qx[k - 1]
        qb[...] = value
        q_twin.start()
        for i in range(kept):
            k_out[i, me.c] = g_out[i]
        for d in range(1, nc):
            landed(along_copy(d))
            row = lax.rem(me.c - d + nc, nc)
            for i in range(kept):
                k_out[i, row] = gz[d - 1, i].astype(jnp.float32)
            e_out[...] = e_out[...] + ez[d - 1].astype(jnp.float32)

        def add_along(i, carry):
            value = g_out[i]
            for d in range(1, nc):
                value = value + gz[d - 1, i].astype(jnp.float32)
            g_out[i] = value
            return carry

        lax.fori_loop(kept, parts, add_along, 0)
        q_twin.wait()
        q_out[...] = qb[...] + qc[...]
        for d in order:
            started = core_copy(d) + [copy for k in range(1, nj) for copy in cross_copy(d, k)]
            if d:
                started = started + along_copy(d) + [q_along(d)]
            for copy in started:
                copy.wait_send()
        for k in range(1, nj):
            q_across(k).wait_send()

    f32 = jnp.float32
    one, extra = (parts, piece, width), small.shape[3:]
    return pl.pallas_call(
        kernel,
        name="reduce_all",
        out_shape=(
            jax.ShapeDtypeStruct((kept, nc, piece, width), f32),
            jax.ShapeDtypeStruct(one, f32),
            jax.ShapeDtypeStruct(extra, f32),
            jax.ShapeDtypeStruct(tile, f32),
        ),
        in_specs=[pl.BlockSpec(memory_space=VMEM)] * 3,
        out_specs=[pl.BlockSpec(memory_space=VMEM)] * 4,
        scratch_shapes=[
            VMEM((nc, parts, nj, piece, width), low),
            VMEM((nc, nj) + extra, low),
            VMEM((nc, parts, nj, piece, width), low),
            VMEM((nc, nj) + extra, low),
            VMEM((nc, nj - 1) + one, low),
            VMEM((nc, nj - 1) + extra, low),
            VMEM((nc - 1,) + one, low),
            VMEM((nc - 1,) + extra, low),
            VMEM((nc - 1,) + tile, f32),
            VMEM((nj - 1,) + tile, f32),
            VMEM(tile, f32),
            VMEM(tile, f32),
            VMEM(tile, f32),
            SEM.DMA((nc, 2)),
            SEM.DMA((nc, 2)),
            SEM.DMA((nc, nj, 2)),
            SEM.DMA((nc, nj, 2)),
            SEM.DMA((nc, 2)),
            SEM.DMA((nc, 2)),
            SEM.DMA((nc,)),
            SEM.DMA((nc,)),
            SEM.DMA((nj,)),
            SEM.DMA((nj,)),
            SEM.DMA((1,)),
            SEM.DMA((1,)),
        ],
        compiler_params=pltpu.CompilerParams(
            collective_id=2, has_side_effects=True, vmem_limit_bytes=56 * 1024 * 1024
        ),
    )(grads, small, squares)


CHUNK = 16


def fill_mask(mask, query_code, key_code, block, count):
    near = block * count
    query = query_code[pl.ds(near, count)]
    if block:
        mask[:, :near] = jnp.where(query == key_code[:, :near], 0.0, negative)
    row = lax.broadcasted_iota(jnp.int32, (count, count), 0)
    column = lax.broadcasted_iota(jnp.int32, (count, count), 1)
    seen = ((query == key_code[:, near : near + count]) & (row >= column)) | (row == column)
    mask[:, near : near + count] = jnp.where(seen, 0.0, negative)


def fill_slopes(bank, slopes, head, count):
    for i in range(count // CHUNK):
        row = slopes[head]
        bank[head, i * CHUNK : (i + 1) * CHUNK] = pltpu.roll(row, i * CHUNK, 1) if i else row


def biased(scores, mask, slope, block, count):
    end = (block + 1) * count
    band = 2 * count
    if end < band:
        return scores + mask[:, :end] + slope[:, band - end :]
    if end == band:
        return scores + mask[:, :end] + slope[...]
    wide = scores[:, : end - band] + mask[:, : end - band]
    tight = scores[:, end - band :] + mask[:, end - band : end] + slope[...]
    return jnp.concatenate((wide, tight), axis=1)


def attend_forward(tokens, weights, gain, gain_next, query_code, key_code, slopes, nc, ns):
    length, width = tokens.shape
    count = length // nc
    part = width // nc
    heads, _, band = slopes.shape
    low, f32 = jnp.bfloat16, jnp.float32

    def kernel(t_in, w_in, gain_in, next_in, qcode, kcode, toe, first, q_out, k_out, v_out, o_out, lse_out, x_out, y_out,
               mask, bank, osend, ss, rs):
        me = Place(nc, ns)
        barrier = pltpu.get_barrier_semaphore()
        for d in range(1, nc):
            pl.semaphore_signal(barrier, inc=1, device_id=me.along(d), device_id_type=MESH)
        pl.semaphore_wait(barrier, nc - 1)

        def norm(i, carry):
            at = pl.ds(pl.multiple_of(i * 64, 64), 64)
            x = t_in[at].astype(f32)
            rate = lax.rsqrt(jnp.mean(x * x, axis=-1, keepdims=True) + epsilon)
            first[at] = (x * rate * gain_in[...]).astype(low)
            return carry

        lax.fori_loop(0, length // 64, norm, 0)

        def project(i, carry):
            at = pl.ds(pl.multiple_of(i * count, count), count)
            block = first[at]
            q_out[at] = dot32(block, w_in[0]).astype(low)
            k_out[at] = dot32(block, w_in[1]).astype(low)
            v_out[at] = dot32(block, w_in[2]).astype(low)
            return carry

        lax.fori_loop(0, nc, project, 0)
        for head in range(heads):
            fill_slopes(bank, toe, head, count)
        lane = lax.broadcasted_iota(jnp.int32, (count, 2 * HEAD), 1)
        spot = lax.broadcasted_iota(jnp.int32, (count, 128), 1)
        own_copy = [
            remote(osend.at[b], o_out.at[me.c], ss.at[b], rs.at[me.c], (b, me.s)) for b in range(nc)
        ]
        for b in reversed(range(nc)):
            end = (b + 1) * count
            rows = pl.ds(b * count, count)
            fill_mask(mask, qcode, kcode, b, count)
            level = jnp.zeros((count, 128), f32)
            for pair in range(heads // 2):
                two = slice(pair * 2 * HEAD, (pair + 1) * 2 * HEAD)
                q_pair = q_out[rows, two] * low(1.0 / math.sqrt(HEAD))
                k_pair = k_out[:end, two]
                v_pair = v_out[:end, two]
                halves = []
                for half in range(2):
                    head = pair * 2 + half
                    inside = (lane >= HEAD) if half else (lane < HEAD)
                    scores = nt(jnp.where(inside, q_pair, low(0)), k_pair)
                    scores = biased(scores, mask, bank.at[head], b, count)
                    top = jnp.max(scores, axis=1, keepdims=True)
                    scores = jnp.exp(scores - top)
                    total = jnp.sum(scores, axis=1, keepdims=True)
                    halves.append(dot32(scores.astype(low), v_pair) * (1.0 / total))
                    level = jnp.where(spot == head, top + jnp.log(total), level)
                osend[b, :, two] = jnp.where(lane < HEAD, halves[0], halves[1]).astype(low)
            lse_out[rows] = level

            @pl.when(me.c == b)
            def _():
                o_out[me.c] = osend[b]

            @pl.when(me.c != b)
            def _():
                own_copy[b].start()

        for d in range(1, nc):
            origin = lax.rem(me.c + d, nc)
            remote(
                osend.at[0], o_out.at[origin], ss.at[0], rs.at[origin], me.along(d)
            ).wait_recv()
        own = pl.ds(pl.multiple_of(me.c * count, count), count)
        squares = jnp.zeros((count, 1), f32)
        for n in range(nc):
            columns = slice(n * part, (n + 1) * part)
            x = t_in[own, columns].astype(f32)
            for origin in range(nc):
                x = x + dot32(o_out[origin], w_in[3 + n, origin * part : (origin + 1) * part])
            x_out[:, columns] = x
            squares = squares + jnp.sum(x * x, axis=1, keepdims=True)
        rate = lax.rsqrt(squares * (1.0 / width) + epsilon)
        for n in range(nc):
            columns = slice(n * part, (n + 1) * part)
            y_out[:, columns] = (x_out[:, columns] * rate * next_in[:, columns]).astype(low)
        for b in range(nc):

            @pl.when(me.c != b)
            def _():
                own_copy[b].wait_send()

    return pl.pallas_call(
        kernel,
        name="attend_forward",
        out_shape=(
            jax.ShapeDtypeStruct((length, width), low),
            jax.ShapeDtypeStruct((length, part), low),
            jax.ShapeDtypeStruct((length, part), low),
            jax.ShapeDtypeStruct((length, part), low),
            jax.ShapeDtypeStruct((nc, count, part), low),
            jax.ShapeDtypeStruct((length, 128), f32),
            jax.ShapeDtypeStruct((count, width), f32),
            jax.ShapeDtypeStruct((count, width), low),
        ),
        in_specs=[pl.BlockSpec(memory_space=VMEM)] * 7,
        out_specs=[pl.BlockSpec(memory_space=VMEM)] * 8,
        scratch_shapes=[
            VMEM((count, length), f32),
            VMEM((heads, count, band), f32),
            VMEM((nc, count, part), low),
            SEM.DMA((nc,)),
            SEM.DMA((nc,)),
        ],
        compiler_params=pltpu.CompilerParams(
            collective_id=3, has_side_effects=True, vmem_limit_bytes=56 * 1024 * 1024
        ),
    )(tokens, weights, gain, gain_next, query_code, key_code, slopes)


def attend_backward(
    dattn, dh, o_all, tokens, first, q_all, k_all, v_all, lse, weights, gain, query_code, key_code, slopes, nc, ns
):
    length, width = tokens.shape
    count = length // nc
    part = width // nc
    heads, _, band = slopes.shape
    low, f32 = jnp.bfloat16, jnp.float32
    scale = 1.0 / math.sqrt(HEAD)

    def kernel(a_in, dh_in, o_in, t_in, first_in, q_in, k_in, v_in, lse_in, w_in, gain_in, qcode, kcode, toe,
               x_out, w_out, gain_out, near_out, far_out,
               mask, bank, dsend, dall, dq, dk, dv, fsend, frecv, fown, ss, rs, fs, fr):
        me = Place(nc, ns)
        barrier = pltpu.get_barrier_semaphore()
        for d in range(1, nc):
            pl.semaphore_signal(barrier, inc=1, device_id=me.along(d), device_id_type=MESH)
        pl.semaphore_wait(barrier, nc - 1)

        def do_copy(d):
            return remote(dsend.at[d], dall.at[me.c], ss.at[d], rs.at[d], me.along(d))

        for d in list(range(1, nc)) + [0]:
            target = lax.rem(me.c + d, nc)
            at = pl.ds(pl.multiple_of(target * part, part), part)
            value = nt(a_in[:, :part], w_in[3, at])
            for n in range(1, nc):
                value = value + nt(a_in[:, n * part : (n + 1) * part], w_in[3 + n, at])
            if d:
                dsend[d] = value.astype(low)
                do_copy(d).start()
            else:
                dall[me.c] = value.astype(low)
        for n in range(nc):
            for origin in range(nc):
                w_out[3 + n, origin * part : (origin + 1) * part] = tn(
                    o_in[origin], a_in[:, n * part : (n + 1) * part]
                ).astype(low)
        for head in range(heads):
            fill_slopes(bank, toe, head, count)
        lane = lax.broadcasted_iota(jnp.int32, (count, 2 * HEAD), 1)
        spot = lax.broadcasted_iota(jnp.int32, (count, 128), 1)
        dk[...] = jnp.zeros_like(dk)
        dv[...] = jnp.zeros_like(dv)
        near_out[...] = jnp.zeros_like(near_out)
        far_out[...] = jnp.zeros_like(far_out)
        gain_out[...] = jnp.zeros_like(gain_out)
        for d in range(1, nc):
            origin = lax.rem(me.c - d + nc, nc)
            remote(dsend.at[d], dall.at[origin], ss.at[d], rs.at[d], me.along(d)).wait_recv()
        out_copy = [
            remote(fsend.at[b], frecv.at[me.c], fs.at[b], fr.at[me.c], (b, me.s)) for b in range(nc)
        ]
        for b in reversed(range(nc)):
            end = (b + 1) * count
            rows = pl.ds(b * count, count)
            fill_mask(mask, qcode, kcode, b, count)
            level = lse_in[rows]
            for pair in range(heads // 2):
                two = slice(pair * 2 * HEAD, (pair + 1) * 2 * HEAD)
                q_pair = q_in[rows, two] * low(scale)
                do_pair = dall[b, :, two]
                k_pair = k_in[:end, two]
                v_pair = v_in[:end, two]
                parts = []
                for half in range(2):
                    head = pair * 2 + half
                    inside = (lane >= HEAD) if half else (lane < HEAD)
                    q_one = jnp.where(inside, q_pair, low(0))
                    do_one = jnp.where(inside, do_pair, low(0))
                    own_level = jnp.sum(
                        jnp.where(spot == head, level, 0.0), axis=1, keepdims=True
                    )
                    probs = jnp.exp(
                        biased(nt(q_one, k_pair), mask, bank.at[head], b, count) - own_level
                    )
                    grads = probs * nt(do_one, v_pair)
                    grads = grads - probs * jnp.sum(grads, axis=1, keepdims=True)
                    low_grads = grads.astype(low)
                    parts.append(dot32(low_grads, k_pair))
                    dk[:end, two] += tn(low_grads, q_one)
                    dv[:end, two] += tn(probs.astype(low), do_one)
                    near = grads[:, max(end - band, 0) :]
                    if end < band:
                        near = jnp.concatenate((jnp.zeros((count, band - end), f32), near), axis=1)
                    height = count
                    while height > CHUNK:
                        height = height // 2
                        near = near[:height] + pltpu.roll(near[height:], band - height, 1)
                    near_out[head] += near
                    if end > band:
                        far = grads[:, : end - band]
                        total = far[:, :128]
                        for piece in range(1, (end - band) // 128):
                            total = total + far[:, piece * 128 : (piece + 1) * 128]
                        height = count
                        while height > 8:
                            height = height // 2
                            total = total[:height] + total[height:]
                        far_out[head] += total
                dq[rows, two] = (jnp.where(lane < HEAD, parts[0], parts[1]) * scale).astype(low)
            dq_low, dk_low, dv_low = dq[rows], dk[rows].astype(low), dv[rows].astype(low)
            for n in range(nc):
                columns = slice(n * part, (n + 1) * part)
                at = pl.ds(n * part, part)
                value = nt(dq_low, w_in[0, at]) + nt(dk_low, w_in[1, at]) + nt(dv_low, w_in[2, at])
                fown[:, columns] = value
            x = t_in[rows].astype(f32)
            rate = lax.rsqrt(jnp.mean(x * x, axis=-1, keepdims=True) + epsilon)
            gain_out[...] += jnp.sum(fown[...] * x * rate, axis=0, keepdims=True)
            fsend[b] = fown[...].astype(low)

            @pl.when(me.c == b)
            def _():
                x_out[...] = fown[...]

            @pl.when(me.c != b)
            def _():
                out_copy[b].start()

        for i, grads in enumerate((dq, dk, dv)):
            for n in range(nc):
                at = slice(n * part, (n + 1) * part)
                w_out[i, at] = tn(first_in[:, at], grads[...].astype(low)).astype(low)
        for d in range(1, nc):
            origin = lax.rem(me.c + d, nc)
            remote(
                fsend.at[0], frecv.at[origin], fs.at[0], fr.at[origin], me.along(d)
            ).wait_recv()
            x_out[...] += frecv[origin].astype(f32)
        own = pl.ds(pl.multiple_of(me.c * count, count), count)
        x = t_in[own].astype(f32)
        rate = lax.rsqrt(jnp.mean(x * x, axis=-1, keepdims=True) + epsilon)
        scaled = x_out[...] * gain_in[...]
        pull = jnp.mean(scaled * x, axis=-1, keepdims=True)
        x_out[...] = dh_in[...] + rate * scaled - x * (rate * rate * rate * pull)
        for d in range(1, nc):
            do_copy(d).wait_send()
        for b in range(nc):

            @pl.when(me.c != b)
            def _():
                out_copy[b].wait_send()

    return pl.pallas_call(
        kernel,
        name="attend_backward",
        out_shape=(
            jax.ShapeDtypeStruct((count, width), f32),
            jax.ShapeDtypeStruct((3 + nc, width, part), low),
            jax.ShapeDtypeStruct((1, width), f32),
            jax.ShapeDtypeStruct((heads, CHUNK, band), f32),
            jax.ShapeDtypeStruct((heads, 8, 128), f32),
        ),
        in_specs=[pl.BlockSpec(memory_space=VMEM)] * 14,
        out_specs=[pl.BlockSpec(memory_space=VMEM)] * 5,
        scratch_shapes=[
            VMEM((count, length), f32),
            VMEM((heads, count, band), f32),
            VMEM((nc, count, part), low),
            VMEM((nc, count, part), low),
            VMEM((length, part), low),
            VMEM((length, part), f32),
            VMEM((length, part), f32),
            VMEM((nc, count, width), low),
            VMEM((nc, count, width), low),
            VMEM((count, width), f32),
            SEM.DMA((nc,)),
            SEM.DMA((nc,)),
            SEM.DMA((nc,)),
            SEM.DMA((nc,)),
        ],
        compiler_params=pltpu.CompilerParams(
            collective_id=4, has_side_effects=True, vmem_limit_bytes=56 * 1024 * 1024
        ),
    )(dattn, dh, o_all, tokens, first, q_all, k_all, v_all, lse, weights, gain, query_code, key_code, slopes)


def activation(gate_values, up_values):
    return jax.nn.gelu(gate_values) * up_values


def per_device(
    tokens,
    segments,
    valid,
    routes,
    teacher,
    norm_attn,
    w_query,
    w_key,
    w_value,
    output_weight,
    rel_bias,
    norm_ffn,
    w_router,
    w_gate,
    w_up,
    w_down,
):
    nc = lax.axis_size("ctx")
    ns = lax.axis_size("shard")
    c, s = lax.axis_index("ctx"), lax.axis_index("shard")
    n_dev, nj = nc * ns, ns // 2
    row_count, width = tokens.shape[1:]
    top_count = routes.shape[2]
    experts = w_router.shape[1]
    capacity = (5 * row_count * top_count + 4 * experts - 1) // (4 * experts)
    length = row_count * nc
    low = jnp.bfloat16
    f32 = jnp.float32
    piece = w_query.shape[0]
    band = 2 * row_count

    part = width // nc
    smalls = (norm_attn, norm_ffn, rel_bias, w_router.reshape(-1), segments[0].astype(low), valid[0].astype(low))
    sizes = [x.shape[0] for x in smalls]
    starts = [sum(sizes[:i]) for i in range(len(sizes))]
    extra = jnp.concatenate(smalls + (jnp.zeros((EXTRA * part - sum(sizes),), low),))
    shares = [w.reshape(piece, nc, part).transpose(1, 0, 2) for w in (w_query, w_key, w_value, output_weight)]
    shares = jnp.concatenate(
        [x[:, None] for x in shares[:3]] + [jnp.broadcast_to(shares[3][None], (nc, nc, piece, part))], axis=1
    )
    weights, extras, tokens_all = gather_all(
        shares, extra.reshape(EXTRA, part), tokens[0], nc, ns
    )
    extras = extras.reshape(nc, ns, EXTRA * part)
    gain_attn, gain_ffn, full_bias, full_router = (
        extras[:, :, begin : begin + size].reshape(-1)
        for begin, size in zip(starts[:4], sizes[:4])
    )
    full_router = full_router.reshape(width, experts)
    table = full_bias.reshape(BUCKETS, HEADS).astype(f32)
    line = lax.dynamic_slice_in_dim(extras, s, 1, 1)[:, 0]
    line_seg = line[:, starts[4] : starts[4] + row_count].reshape(length).astype(jnp.int32)
    line_valid = line[:, starts[5] : starts[5] + row_count].reshape(length) > 0
    key_code = jnp.where(line_valid, line_seg, -1)[None]
    query_code = line_seg[:, None]
    valid_count = jnp.sum(extras[:, :, starts[5] : starts[5] + row_count].astype(f32))

    spot = (jnp.arange(band)[None, :] - jnp.arange(CHUNK)[:, None]) % band
    distance = jnp.where(spot <= row_count, row_count - spot, 3 * row_count - spot)
    level = bucket_of(distance, BUCKETS)
    level_hot = (level[:, :, None] == jnp.arange(BUCKETS)[None, None, :]).astype(f32)
    heads = HEADS // nc
    own_table = lax.dynamic_slice_in_dim(table, c * heads, heads, 1)
    slopes = jnp.einsum(
        "ixb,bh->hix", level_hot, own_table - own_table[BUCKETS - 1 :], precision=highest_precision
    )

    gain_one, gain_two = gain_attn.astype(f32), gain_ffn.astype(f32)
    first_all, queries, keys, values, mixed, log_total, residual, ffn_low = attend_forward(
        tokens_all, weights, gain_one[None], gain_two[None], query_code, key_code, slopes, nc, ns
    )
    ffn_in = ffn_low.astype(f32)
    router = full_router.astype(f32)
    logits = jnp.dot(ffn_in, router, precision=highest_precision)
    route_local = routes[0]
    expert_ids = jnp.arange(experts, dtype=jnp.int32)
    route_hot = route_local[:, :, None] == expert_ids[None, None, :]
    picked = jnp.sum(jnp.where(route_hot, logits[:, None, :], 0.0), axis=-1)
    gate_probs = jax.nn.softmax(picked, axis=-1)
    flat_routes = route_local.reshape(row_count * top_count)
    route_hits = (flat_routes[:, None] == expert_ids[None, :]).astype(jnp.int32)
    before = jnp.cumsum(route_hits, axis=0) - route_hits
    slot_rank = jnp.sum(before * route_hits, axis=1)
    target = (flat_routes * capacity + slot_rank).reshape(row_count, top_count)
    slot_ids = jnp.arange(experts * capacity, dtype=jnp.int32)
    pick_first = (slot_ids[:, None] == target[None, :, 0]).astype(low)
    pick_second = (slot_ids[:, None] == target[None, :, 1]).astype(low)

    def exchange(rows):
        return lax.all_to_all(
            rows.reshape(experts, capacity, width), "shard", split_axis=0, concat_axis=0, tiled=True
        ).reshape(experts * capacity, width)

    expert_rows = exchange(dot32(pick_first + pick_second, ffn_low).astype(low))
    gate_w, up_w, down_w = w_gate[0], w_up[0], w_down[0]
    gate_pre = dot32(expert_rows, gate_w)
    up_pre = dot32(expert_rows, up_w)

    inner_value, activation_back = jax.vjp(activation, gate_pre, up_pre)
    inner = inner_value.astype(low)
    returned = exchange(dot32(inner, down_w).astype(low))
    picked_one, picked_two = tn(pick_first, returned), tn(pick_second, returned)
    output_sum = residual + gate_probs[:, :1] * picked_one + gate_probs[:, 1:] * picked_two
    valid_one = valid[0].astype(f32)
    deviation = output_sum - teacher[0].astype(f32)
    local_square = jnp.sum(valid_one[:, None] * deviation * deviation)
    everything = float(row_count * nc * ns)
    cotangent = everything / valid_count * deviation * valid_one[:, None]
    gate_grad = jnp.stack(
        (jnp.sum(cotangent * picked_one, axis=-1), jnp.sum(cotangent * picked_two, axis=-1)), axis=1
    )
    back_send = dot32(pick_first, (gate_probs[:, :1] * cotangent).astype(low)) + dot32(
        pick_second, (gate_probs[:, 1:] * cotangent).astype(low)
    )
    out_grad = exchange(back_send.astype(low))
    inner_grad = nt(out_grad, down_w)
    gate_pre_grad, up_pre_grad = activation_back(inner_grad)
    gate_low = gate_pre_grad.astype(low)
    up_low = up_pre_grad.astype(low)
    sent_back = exchange((nt(gate_low, gate_w) + nt(up_low, up_w)).astype(low))
    down_w_grad = tn(inner, out_grad).astype(low)
    gate_w_grad = tn(expert_rows, gate_low).astype(low)
    up_w_grad = tn(expert_rows, up_low).astype(low)
    gate_w_sum, up_w_sum, down_w_sum = (
        lax.psum_scatter(x[None], "ctx", scatter_dimension=1, tiled=True).astype(f32)
        for x in (gate_w_grad, up_w_grad, down_w_grad)
    )
    ffn_grad = tn(pick_first + pick_second, sent_back)
    pick_grad = gate_probs * (gate_grad - jnp.sum(gate_probs * gate_grad, axis=-1, keepdims=True))
    logits_grad = jnp.sum(jnp.where(route_hot, pick_grad[:, :, None], 0.0), axis=1)
    router_grad = contract(ffn_in, logits_grad, 0, 0, highest_precision)
    ffn_grad = ffn_grad + contract(logits_grad, router, 1, 1, highest_precision)
    unused, norm_two_back = jax.vjp(rms_norm, residual, gain_two)
    residual_from_norm, gain_two_grad = norm_two_back(ffn_grad)
    residual_grad = cotangent + residual_from_norm
    attn_grad_low = residual_grad.astype(low)
    input_grad, w_grads, gain_one_grad, near_sum, far_sum = attend_backward(
        attn_grad_low, residual_grad, mixed, tokens_all, first_all, queries, keys, values, log_total, weights,
        gain_one[None], query_code, key_code, slopes, nc, ns,
    )
    own_bias = jnp.einsum("hix,ixb->bh", near_sum, level_hot, precision=highest_precision)
    last_bucket = (jnp.arange(BUCKETS) == BUCKETS - 1).astype(f32)
    own_bias = own_bias + last_bucket[:, None] * jnp.sum(far_sum, axis=(1, 2))[None, :]
    bias_grad = lax.dynamic_update_slice_in_dim(
        jnp.zeros((BUCKETS, HEADS), f32), own_bias, c * heads, 1
    )
    small_grads = jnp.concatenate(
        [
            x.reshape(n_dev, -1).astype(low)
            for x in (gain_one_grad, gain_two_grad, bias_grad, router_grad)
        ],
        axis=1,
    )
    small_grads = jnp.pad(small_grads, ((0, 0), (0, EXTRA * part - small_grads.shape[1])))
    kept_sum, w_sum, small_sum, square_sum = reduce_all(
        w_grads.reshape(3 + nc, nc, nj, 2, piece, part),
        small_grads.reshape(nc, nj, 2, EXTRA, part),
        jnp.full((8, 128), local_square, f32),
        nc,
        ns,
        3,
    )
    loss_value = square_sum[0, 0] / (2.0 * width * valid_count)
    kept_sum = kept_sum.transpose(0, 2, 1, 3).reshape(3, piece, width)
    out_sum = w_sum[3:].transpose(1, 0, 2).reshape(piece, width)
    small_sum = small_sum.reshape(-1)
    tails = [small_sum[begin : begin + size] for begin, size in zip(starts[:4], sizes[:4])]
    return (
        output_sum.astype(low)[None],
        loss_value,
        input_grad[None],
        tails[0],
        kept_sum[0],
        kept_sum[1],
        kept_sum[2],
        out_sum,
        tails[2],
        tails[1],
        tails[3].reshape(w_router.shape),
        gate_w_sum,
        up_w_sum,
        down_w_sum,
    )


def solution(mesh):
    return jax.shard_map(
        per_device,
        mesh=mesh,
        in_specs=(
            P("shard", "ctx", None),
            P("shard", "ctx"),
            P("shard", "ctx"),
            P("shard", "ctx", None),
            P("shard", "ctx", None),
            P(("ctx", "shard")),
            P(("ctx", "shard"), None),
            P(("ctx", "shard"), None),
            P(("ctx", "shard"), None),
            P(("ctx", "shard"), None),
            P(("ctx", "shard")),
            P(("ctx", "shard")),
            P(("ctx", "shard"), None),
            P("shard", None, None),
            P("shard", None, None),
            P("shard", None, None),
        ),
        out_specs=(
            P("shard", "ctx", None),
            P(),
            P("shard", "ctx", None),
            P(("ctx", "shard")),
            P(("ctx", "shard"), None),
            P(("ctx", "shard"), None),
            P(("ctx", "shard"), None),
            P(("ctx", "shard"), None),
            P(("ctx", "shard")),
            P(("ctx", "shard")),
            P(("ctx", "shard"), None),
            P("shard", "ctx", None),
            P("shard", "ctx", None),
            P("shard", "ctx", None),
        ),
        check_vma=False,
    )
```

time: 651 us -> 592 us (0.909)
  Pallas kernels: 329 us -> 239 us
  waiting for transfers between devices: 74.3 us -> 142 us
  matrix products: 115 us -> 81.3 us
  blocking collectives: 20.9 us -> 43.4 us
  other arithmetic: 30.8 us -> 19.2 us
  local copies, waits for them, and re-layouts: 38.2 us -> 31.3 us
    pallas_call x1, Pallas kernels: 137 us -> 35.8 us  [reduce_all(): pl.pallas_call(kernel, name='reduce_all', out_shape=(jax.ShapeDtypeStruct...]
    reduce_scatter x3, waiting for transfers between devices: 29.2 us -> 112 us  [per_device(): lax.psum_scatter(x[None], 'ctx', scatter_dimension=1, tiled=True)]
    pallas_call x1, Pallas kernels: 57.3 us -> 121 us  [attend_backward(): pl.pallas_call(kernel, name='attend_backward', out_shape=(jax.ShapeDtypeS...]
    pallas_call x1, Pallas kernels: 61.5 us -> 29.1 us  [attend_forward(): pl.pallas_call(kernel, name='attend_forward', out_shape=(jax.ShapeDtypeSt...]
    dot_general x19 -> x11, matrix products: 86.4 us -> 61.3 us  [contract(): lax.dot_general(left_side, right_side, (((left_axis,), (right_axis,)), ((...]
    all_to_all x1 -> x2, blocking collectives: 20.9 us -> 43.4 us  [exchange(): lax.all_to_all(rows.reshape(experts, capacity, width), 'shard', split_axi...]
    pallas_call x1, Pallas kernels: 73.9 us -> 53.8 us  [gather_all(): pl.pallas_call(kernel, name='gather_all', out_shape=(jax.ShapeDtypeStruct...]
    all_to_all x3 -> x2, waiting for transfers between devices: 45 us -> 29.4 us  [exchange(): lax.all_to_all(rows.reshape(experts, capacity, width), 'shard', split_axi...]
  transfers between devices with their start and end apart: 6 -> 5, of which waited for: 4 -> 4; matrix products, arithmetic and copies ran while one was open for 18% -> 14% of each run, Pallas kernels for 30% -> 27%
where the time goes in v2:
time: 592 us; the launch traced here: 583 us
  Pallas kernels  239 us (40%)
  waiting for transfers between devices  142 us (24%)
  matrix products  81.3 us (14%)
  blocking collectives  43.4 us (7%)
  local copies, waits for them, and re-layouts  31.3 us (5%)
  other arithmetic  19.2 us (3%)
  between operations  18 us (3%)
  starting transfers between devices  8.61 us (1%)
    pallas_call x1, Pallas kernels, attend_backward(): pl.pallas_call(kernel, name='attend_backward', out_shape=(jax.ShapeDtypeS...  121 us
    reduce_scatter x3, waiting for transfers between devices, per_device(): lax.psum_scatter(x[None], 'ctx', scatter_dimension=1, tiled=True)  112 us
    dot_general x11, matrix products, contract(): lax.dot_general(left_side, right_side, (((left_axis,), (right_axis,)), ((...  61.3 us
    pallas_call x1, Pallas kernels, gather_all(): pl.pallas_call(kernel, name='gather_all', out_shape=(jax.ShapeDtypeStruct...  53.8 us
    all_to_all x2, blocking collectives, exchange(): lax.all_to_all(rows.reshape(experts, capacity, width), 'shard', split_axi...  43.4 us
    pallas_call x1, Pallas kernels, reduce_all(): pl.pallas_call(kernel, name='reduce_all', out_shape=(jax.ShapeDtypeStruct...  35.8 us
    all_to_all x2, waiting for transfers between devices, exchange(): lax.all_to_all(rows.reshape(experts, capacity, width), 'shard', split_axi...  29.4 us
    pallas_call x1, Pallas kernels, attend_forward(): pl.pallas_call(kernel, name='attend_forward', out_shape=(jax.ShapeDtypeSt...  29.1 us
  transfers between devices with their start and end apart: 5, of which 4 were waited for; matrix products, arithmetic and copies ran while one was open for 14% of the time, Pallas kernels for 27%

profile of v2, /device:TPU:0, one launch (start us, length us, event | category | flops | bytes accessed | tf_op | source)
XLA Modules:
  0.0 582.8 jit_solution(14754065793413158707)
XLA Ops:
  15.0 53.8 %gather_all.1 = (bf16[7,4,8,32,256]{4,3,2,1,0:T(8,128)(2,1)}, bf16[4,8,16,256]{3,2,1,0:T(8,128)(2,1)}, bf16[4,256,1024]{2,1,0:T(8,128)(2,1)}) custom-call(bf16[4,7,32,256]{3,2,1,0:T(8,128)(2,1)} %pad_maximum_fusion.w_in, bf16[16,256]{1,0:T(8,128)(2,1)} %reshape.431.e_in, bf16[256,1024]{1,0:T(8,128)(2,1)} %bitcast.186), custom_call_target="tpu_custom_call" | custom-call | tf_op jit(solution)/shard_map/gather_all/pallas_call | solution.py:232
  77.2 29.1 %attend_forward.1 = (bf16[1024,1024]{1,0:T(8,128)(2,1)}, bf16[1024,256]{1,0:T(8,128)(2,1)}, bf16[1024,256]{1,0:T(8,128)(2,1)}, bf16[1024,256]{1,0:T(8,128)(2,1)}...) custom-call(bf16[1024,1024]{1,0:T(8,128)(2,1)} %bitcast.164, ...), custom_call_target="tpu_custom_call" | custom-call | tf_op jit(solution)/shard_map/attend_forward/pallas_call | solution.py:580
  107.9 22.2 %all_to_all.20 = bf16[8,80,1024]{2,1,0:T(8,128)(2,1)S(1)} all-to-all(bf16[8,80,1024]{2,1,0:T(8,128)(2,1)S(1)} %bitcast.166), channel_id=1, replica_groups=mesh['ctx'=4,'shard'=8] {'shard'}, dimensions={0} | all-to-all | bytes 2621440 | tf_op jit(solution)/shard_map/all_to_all | solution.py:880
  130.1 3.9 fusion.17
  134.1 6.2 %multiply_convert_fusion.1 = (bf16[640,2816]{1,0:T(8,128)(2,1)S(1)}, f32[640,2816]{1,0:T(8,128)}) fusion(f32[640,2816]{1,0:T(8,128)S(1)} %fusion.17, bf16[640,1024]{1,0:T(8,128)(2,1)S(1)} %bitcast.173, bf16[1,1024,2816]{2,1,0:T(8,128)(2,1)S(1)} %bitcast.219), kind=kOutput, calls=%fused_computation.10 | convolution fusion | flops 3709009920 | bytes 25100288 | tf_op jit(solution)/shard_map/dot_general | solution.py:60
  140.3 4.9 fusion.21
  145.3 3.7 all-to-all-start.1
  154.4 12.7 %all-to-all-done.1 = bf16[8,80,1024]{2,1,0:T(8,128)(2,1)S(1)} async-done(((bf16[8,80,1024]{2,1,0:T(8,128)(2,1)}), bf16[8,80,1024]{2,1,0:T(8,128)(2,1)S(1)}, u32[]{:S(2)}, u32[]{:S(2)}) %all-to-all-start.1) | async-done | bytes 1310752 | tf_op jit(solution)/shard_map/all_to_all | solution.py:880
  173.6 21.1 %all_to_all.21 = bf16[8,80,1024]{2,1,0:T(8,128)(2,1)S(1)} all-to-all(bf16[8,80,1024]{2,1,0:T(8,128)(2,1)S(1)} %bitcast.167), channel_id=1, replica_groups=mesh['ctx'=4,'shard'=8] {'shard'}, dimensions={0} | all-to-all | bytes 2621440 | tf_op jit(solution)/shard_map/all_to_all | solution.py:880
  195.8 6.5 %convert_bitcast_fusion = bf16[1,2816,1024]{2,1,0:T(8,128)(2,1)} fusion(bf16[640,2816]{1,0:T(8,128)(2,1)S(1)} %copy-done.21, bf16[640,1024]{1,0:T(8,128)(2,1)S(1)} %bitcast.178), kind=kOutput, calls=%fused_computation.24 | convolution fusion | flops 3693871104 | bytes 10682368 | tf_op jit(solution)/shard_map/dot_general | solution.py:50
  202.4 16.7 %fusion.6 = (bf16[640,2816]{1,0:T(8,128)(2,1)}, bf16[640,2816]{1,0:T(8,128)(2,1)S(1)}) fusion(f32[640,2816]{1,0:T(8,128)} %copy-done.19, f32[640,2816]{1,0:T(8,128)} %get-tuple-element.149, bf16[640,1024]{1,0:T(8,128)(2,1)} %bitcast.179, bf16[1,2816,1024]{2,1,0:T(8,128)(2,1)} %param.31), kind=kOutput, calls=%fused_computation.8 | convolution fusion | flops 3734241280 | bytes 28704768 | tf_op jit(solution)/shard_map/dot_general | solution.py:50
  221.0 6.7 %convert_bitcast_fusion.1 = bf16[1,1024,2816]{2,1,0:T(8,128)(2,1)} fusion(bf16[640,1024]{1,0:T(8,128)(2,1)S(1)} %bitcast.175, bf16[640,2816]{1,0:T(8,128)(2,1)S(1)} %get-tuple-element.136), kind=kOutput, calls=%fused_computation.25 | convolution fusion | flops 3693871104 | bytes 10682368 | tf_op jit(solution)/shard_map/dot_general | solution.py:50
  227.9 9.6 %convert_bitcast_fusion.2 = bf16[1,1024,2816]{2,1,0:T(8,128)(2,1)} fusion(bf16[640,1024]{1,0:T(8,128)(2,1)} %bitcast.174, bf16[640,2816]{1,0:T(8,128)(2,1)} %get-tuple-element.135), kind=kOutput, calls=%fused_computation.26 | convolution fusion | flops 3693871104 | bytes 10682368 | tf_op jit(solution)/shard_map/dot_general | solution.py:50
  238.3 7.2 %fusion.11 = f32[640,1024]{1,0:T(8,128)S(1)} fusion(bf16[640,2816]{1,0:T(8,128)(2,1)} %copy-done.23, bf16[1,1024,2816]{2,1,0:T(8,128)(2,1)} %param.30), kind=kOutput, calls=%fused_computation.16 | convolution fusion | flops 3690987520 | bytes 11993088 | tf_op jit(solution)/shard_map/dot_general | solution.py:50
  245.5 7.6 %add_convert_fusion = bf16[640,1024]{1,0:T(8,128)(2,1)} fusion(f32[640,1024]{1,0:T(8,128)S(1)} %fusion.11, bf16[640,2816]{1,0:T(8,128)(2,1)S(1)} %copy-done.22, bf16[1,1024,2816]{2,1,0:T(8,128)(2,1)} %param.29), kind=kOutput, calls=%fused_computation.27 | convolution fusion | flops 3692298240 | bytes 13303808 | tf_op jit(solution)/shard_map/dot_general | solution.py:50
  253.1 4.6 all-to-all-start.3
  259.3 16.7 %all-to-all-done.3 = bf16[8,80,1024]{2,1,0:T(8,128)(2,1)} async-done(((bf16[8,80,1024]{2,1,0:T(8,128)(2,1)}), bf16[8,80,1024]{2,1,0:T(8,128)(2,1)}, u32[]{:S(2)}, u32[]{:S(2)}) %all-to-all-start.3) | async-done | bytes 1310752 | tf_op jit(solution)/shard_map/all_to_all | solution.py:880
  279.6 120.6 %attend_backward.1 = (f32[256,1024]{1,0:T(8,128)}, bf16[7,1024,256]{2,1,0:T(8,128)(2,1)}, f32[1,1024]{1,0:T(1,128)}, f32[4,16,512]{2,1,0:T(8,128)}, f32[4,8,128]{2,1,0:T(8,128)}) custom-call(bf16[256,1024]{1,0:T(8,128)(2,1)} %get-tuple-element.132.a_in, f32[256,1024]{1,0:T(8,128)} %get-tuple-element.133.dh_in, bf16[4,256,256]{2,1,0:T(8,128)(2,1)} %get-tuple-element.39.o_in, ...), custom_call_target="tpu_custom_call" | custom-call | tf_op jit(solution)/shard_map/attend_backward/pallas_call | solution.py:752
  405.8 35.8 %reduce_all.1 = (f32[3,4,32,256]{3,2,1,0:T(8,128)}, f32[7,32,256]{2,1,0:T(8,128)}, f32[16,256]{1,0:T(8,128)}, f32[8,128]{1,0:T(8,128)}) custom-call(bf16[7,4,4,2,32,256]{5,4,3,2,1,0:T(8,128)(2,1)} %bitcast.170, bf16[4,4,2,16,256]{4,3,2,1,0:T(8,128)(2,1)} %bitcast.180, f32[8,128]{1,0:T(8,128)} %broadcast_in_dim.104.q_in), custom_call_target="tpu_custom_call" | custom-call | tf_op jit(solution)/shard_map/reduce_all/pallas_call | solution.py:408
  451.9 3.3 convert_element_type.547
  455.2 7.2 %reduce-scatter.6.cloned.1.call-done = bf16[1,256,2816]{2,1,0:T(8,128)(2,1)} async-done(((bf16[1,1024,2816]{2,1,0:T(8,128)(2,1)}), bf16[1,256,2816]{2,1,0:T(8,128)(2,1)}) %reduce-scatter.6.cloned.1.call-update) | async-done | bytes 1441808 | tf_op jit(solution)/shard_map/reduce_scatter | solution.py:915
  462.4 3.1 convert_element_type.545
  465.6 104.9 %reduce-scatter.4.cloned.1.call-done = bf16[1,256,2816]{2,1,0:T(8,128)(2,1)} async-done(((bf16[1,1024,2816]{2,1,0:T(8,128)(2,1)}), bf16[1,256,2816]{2,1,0:T(8,128)(2,1)}) %reduce-scatter.4.cloned.1.call-update) | async-done | bytes 1441808 | tf_op jit(solution)/shard_map/reduce_scatter | solution.py:915
  570.5 3.1 convert_element_type.543
  (169 shorter events, 53.3 us)
Async XLA Ops:
  7.2 63.2 %copy-start.18 = (s32[1,256,2]{1,2,0:T(2,128)S(1)}, s32[1,256,2]{1,2,0:T(2,128)}, u32[]{:S(2)}) copy-start(s32[1,256,2]{1,2,0:T(2,128)} %param.19) | copy-start | bytes 6148
  7.3 99.0 %copy-start.9 = (s32[16,512]{1,0:T(8,128)}, s32[16,512]{1,0:T(8,128)S(1)}, u32[]{:S(2)}) copy-start(s32[16,512]{1,0:T(8,128)S(1)} %convert_add_fusion) | copy-start | bytes 98308
  77.1 30.7 %copy-start.11 = (s32[256]{0:T(256)}, s32[256]{0:T(256)S(1)}, u32[]{:S(2)}) copy-start(s32[256]{0:T(256)S(1)} %get-tuple-element.128) | copy-start | bytes 3076
  77.1 30.7 %copy-start.13 = (s32[256]{0:T(256)}, s32[256]{0:T(256)S(1)}, u32[]{:S(2)}) copy-start(s32[256]{0:T(256)S(1)} %get-tuple-element.129) | copy-start | bytes 3076
  77.2 52.9 %slice-start.4 = ((s8[5767168]{0:T(1024)(128)(4,1)}), s8[4194304]{0:T(1024)(128)(4,1)S(1)}, s32[]{:S(2)}) async-start(s8[5767168]{0:T(1024)(128)(4,1)} %bitcast.220), calls=%async_computation.14 | async-start | bytes 8388608
  77.2 52.9 %slice-start.5 = ((s8[5767168]{0:T(1024)(128)(4,1)}), s8[1572864]{0:T(1024)(128)(4,1)S(1)}, s32[]{:S(2)}) async-start(s8[5767168]{0:T(1024)(128)(4,1)} %bitcast.220), calls=%async_computation.15 | async-start | bytes 3145728
  107.9 26.2 %slice-start.2 = ((s8[5767168]{0:T(1024)(128)(4,1)}), s8[4194304]{0:T(1024)(128)(4,1)S(1)}, s32[]{:S(2)}) async-start(s8[5767168]{0:T(1024)(128)(4,1)} %bitcast.218), calls=%async_computation.12 | async-start | bytes 8388608
  130.1 10.2 %slice-start = ((s8[5767168]{0:T(1024)(128)(4,1)}), s8[4194304]{0:T(1024)(128)(4,1)S(1)}, s32[]{:S(2)}) async-start(s8[5767168]{0:T(1024)(128)(4,1)} %bitcast.216), calls=%async_computation.10 | async-start | bytes 8388608
  134.1 6.2 %copy-start.19 = (f32[640,2816]{1,0:T(8,128)}, f32[640,2816]{1,0:T(8,128)S(1)}, u32[]{:S(2)}) copy-start(f32[640,2816]{1,0:T(8,128)S(1)} %fusion.17) | copy-start | bytes 21626884
  140.3 9.4 %copy-start.17 = (s32[1,256]{1,0:T(1,128)S(1)}, s32[1,256]{1,0:T(1,128)}, u32[]{:S(2)}) copy-start(s32[1,256]{1,0:T(1,128)} %param.18) | copy-start | bytes 3076
  140.3 11.7 %copy-start.1 = (bf16[256,1024]{1,0:T(8,128)(2,1)S(1)}, bf16[256,1024]{1,0:T(8,128)(2,1)}, u32[]{:S(2)}) copy-start(bf16[256,1024]{1,0:T(8,128)(2,1)} %get-tuple-element.38) | copy-start | bytes 1572868
  145.3 23.2 %copy-start = (f32[256,1024]{1,0:T(8,128)S(1)}, f32[256,1024]{1,0:T(8,128)}, u32[]{:S(2)}) copy-start(f32[256,1024]{1,0:T(8,128)} %get-tuple-element.37) | copy-start | bytes 3145732
  145.3 21.9 %all-to-all-start.1 = ((bf16[8,80,1024]{2,1,0:T(8,128)(2,1)}), bf16[8,80,1024]{2,1,0:T(8,128)(2,1)S(1)}, u32[]{:S(2)}, u32[]{:S(2)}) async-start(bf16[8,80,1024]{2,1,0:T(8,128)(2,1)} %bitcast.176), calls=%async_computation.1 | async-start | bytes 2621440 | tf_op jit(solution)/shard_map/all_to_all | solution.py:880
  149.0 302.9 %reduce-scatter.8.cloned.1.call-start = ((), (), s32[]{:S(2)}) async-start(), calls=%async_computation.9 | async-start | bytes 7208960 | tf_op jit(solution)/shard_map/reduce_scatter | solution.py:915
  151.3 19.8 %copy-start.2 = (bf16[1024,8]{1,0:T(8,128)(2,1)}, bf16[1024,8]{1,0:T(8,128)(2,1)S(1)}, u32[]{:S(2)}) copy-start(bf16[1024,8]{1,0:T(8,128)(2,1)S(1)} %reshape_reshape.4) | copy-start | bytes 49156
  173.0 22.8 %copy-start.21 = (bf16[640,2816]{1,0:T(8,128)(2,1)S(1)}, bf16[640,2816]{1,0:T(8,128)(2,1)}, u32[]{:S(2)}) copy-start(bf16[640,2816]{1,0:T(8,128)(2,1)} %copy-done.20) | copy-start | bytes 10813444
  202.4 260.1 %reduce-scatter.6.cloned.1.call-start = ((), (), s32[]{:S(2)}) async-start(), calls=%async_computation.8 | async-start | bytes 7208960 | tf_op jit(solution)/shard_map/reduce_scatter | solution.py:915
  202.4 18.6 %copy-start.6 = (bf16[8,80,1024]{2,1,0:T(8,128)(2,1)S(1)}, bf16[8,80,1024]{2,1,0:T(8,128)(2,1)}, u32[]{:S(2)}) copy-start(bf16[8,80,1024]{2,1,0:T(8,128)(2,1)} %copy-done.5) | copy-start | bytes 3932164
  227.7 342.8 %reduce-scatter.4.cloned.1.call-start = ((), (), s32[]{:S(2)}) async-start(), calls=%async_computation.7 | async-start | bytes 7208960 | tf_op jit(solution)/shard_map/reduce_scatter | solution.py:915
  238.3 7.2 %copy-start.22 = (bf16[640,2816]{1,0:T(8,128)(2,1)S(1)}, bf16[640,2816]{1,0:T(8,128)(2,1)}, u32[]{:S(2)}) copy-start(bf16[640,2816]{1,0:T(8,128)(2,1)} %get-tuple-element.135) | copy-start | bytes 10813444
  245.5 12.3 %copy-start.15 = (s32[256,2]{0,1:T(2,128)S(1)}, s32[256,2]{0,1:T(2,128)}, u32[]{:S(2)}) copy-start(s32[256,2]{0,1:T(2,128)} %copy.138) | copy-start | bytes 6148
  253.1 22.9 %all-to-all-start.3 = ((bf16[8,80,1024]{2,1,0:T(8,128)(2,1)}), bf16[8,80,1024]{2,1,0:T(8,128)(2,1)}, u32[]{:S(2)}, u32[]{:S(2)}) async-start(bf16[8,80,1024]{2,1,0:T(8,128)(2,1)} %bitcast.177), calls=%async_computation.3 | async-start | bytes 2621440 | tf_op jit(solution)/shard_map/all_to_all | solution.py:880
  279.6 121.5 %copy-start.10 = (s32[16,512]{1,0:T(8,128)S(1)}, s32[16,512]{1,0:T(8,128)}, u32[]{:S(2)}) copy-start(s32[16,512]{1,0:T(8,128)} %copy-done.9) | copy-start | bytes 98308
  455.2 118.4 %copy-start.8 = (f32[256,1024]{1,0:T(8,128)S(1)}, f32[256,1024]{1,0:T(8,128)}, u32[]{:S(2)}) copy-start(f32[256,1024]{1,0:T(8,128)} %get-tuple-element.50) | copy-start | bytes 3145732
  (11 other events, 38.7 us)
Sparse Core Ops, SparseCore 0:
  202.5 106.9 reduce-scatter.7
  311.8 150.5 reduce-scatter.5
  464.8 105.6 reduce-scatter.3

commit v3 on v2

--- a/solution.py
+++ b/solution.py
@@ -232,6 +232,7 @@
     full, extras, tokens = pl.pallas_call(
         kernel,
         name="gather_all",
+        cost_estimate=pl.CostEstimate(flops=50 * 10**9, bytes_accessed=10**7, transcendentals=0),
         out_shape=(
             jax.ShapeDtypeStruct(full_shape, weights.dtype),
             jax.ShapeDtypeStruct((nc, ns) + extra.shape, extra.dtype),
@@ -259,13 +260,15 @@
     )
 
 
-def reduce_all(grads, small, squares, nc, ns, kept):
+def reduce_all(grads, small, squares, slices, hidden, nc, ns, kept):
     nj = ns // 2
     parts, piece, width = grads.shape[0], grads.shape[4], grads.shape[5]
     low = grads.dtype
     tile = squares.shape
-
-    def kernel(g_in, e_in, q_in, k_out, g_out, e_out, q_out,
+    begins, wide = slice_plan(hidden, nc)
+    height = slices[0].shape[1]
+
+    def kernel(g_in, e_in, q_in, sa_in, sb_in, k_out, g_out, e_out, q_out, sa_out, sb_out, srecv, ss, sr,
                gt, et, gc, ec, gx, ex, gz, ez, qz, qx, qc, qa, qb,
                cs, cr, xs, xr, zs, zr, q1s, q1r, q2s, q2r, q3s, q3r):
         me = Place(nc, ns)
@@ -311,8 +314,15 @@
         def q_across(k):
             return remote(qa, qx.at[k - 1], q2s.at[k], q2r.at[k], me.across(k))
 
+        def slice_copy(i, d):
+            source = (sa_in, sb_in)[i].at[lax.rem(me.c + d, nc)]
+            return remote(source, srecv.at[i, me.c], ss.at[i, d], sr.at[i, d], me.along(d))
+
         q_twin = remote(qb, qc, q3s.at[0], q3r.at[0], me.twin())
         order = list(range(1, nc)) + [0]
+        for i in range(2):
+            for d in range(1, nc):
+                slice_copy(i, d).start()
         for d in order:
             start(core_copy(d))
         for d in range(1, nc):
@@ -376,28 +386,36 @@
         qb[...] = value
         q_twin.start()
         for i in range(kept):
-            k_out[i, me.c] = g_out[i]
+            k_out[i, :, pl.ds(pl.multiple_of(me.c * width, width), width)] = g_out[i]
         for d in range(1, nc):
             landed(along_copy(d))
             row = lax.rem(me.c - d + nc, nc)
             for i in range(kept):
-                k_out[i, row] = gz[d - 1, i].astype(jnp.float32)
+                at = pl.ds(pl.multiple_of(row * width, width), width)
+                k_out[i, :, at] = gz[d - 1, i].astype(jnp.float32)
             e_out[...] = e_out[...] + ez[d - 1].astype(jnp.float32)
 
-        def add_along(i, carry):
+        for i in range(kept, parts):
             value = g_out[i]
             for d in range(1, nc):
                 value = value + gz[d - 1, i].astype(jnp.float32)
-            g_out[i] = value
-            return carry
-
-        lax.fori_loop(kept, parts, add_along, 0)
+            k_out[kept, :, (i - kept) * width : (i - kept + 1) * width] = value
         q_twin.wait()
         q_out[...] = qb[...] + qc[...]
+        srecv[0, me.c] = sa_in[me.c]
+        srecv[1, me.c] = sb_in[me.c]
+        for i, target in enumerate((sa_out, sb_out)):
+            for d in range(1, nc):
+                origin = lax.rem(me.c - d + nc, nc)
+                landing = srecv.at[i, origin]
+                remote(landing, landing, ss.at[i, d], sr.at[i, d], me.along(-d)).wait_recv()
+            for origin in range(nc):
+                at = slice(begins[origin], begins[origin] + wide)
+                target[:, at] = srecv[i, origin].astype(jnp.float32)
         for d in order:
             started = core_copy(d) + [copy for k in range(1, nj) for copy in cross_copy(d, k)]
             if d:
-                started = started + along_copy(d) + [q_along(d)]
+                started = started + along_copy(d) + [q_along(d), slice_copy(0, d), slice_copy(1, d)]
             for copy in started:
                 copy.wait_send()
         for k in range(1, nj):
@@ -408,15 +426,21 @@
     return pl.pallas_call(
         kernel,
         name="reduce_all",
+        cost_estimate=pl.CostEstimate(flops=45 * 10**9, bytes_accessed=10**7, transcendentals=0),
         out_shape=(
-            jax.ShapeDtypeStruct((kept, nc, piece, width), f32),
+            jax.ShapeDtypeStruct((kept + 1, piece, nc * width), f32),
             jax.ShapeDtypeStruct(one, f32),
             jax.ShapeDtypeStruct(extra, f32),
             jax.ShapeDtypeStruct(tile, f32),
+            jax.ShapeDtypeStruct((height, hidden), f32),
+            jax.ShapeDtypeStruct((height, hidden), f32),
         ),
-        in_specs=[pl.BlockSpec(memory_space=VMEM)] * 3,
-        out_specs=[pl.BlockSpec(memory_space=VMEM)] * 4,
+        in_specs=[pl.BlockSpec(memory_space=VMEM)] * 5,
+        out_specs=[pl.BlockSpec(memory_space=VMEM)] * 6,
         scratch_shapes=[
+            VMEM((2, nc, height, wide), low),
+            SEM.DMA((2, nc)),
+            SEM.DMA((2, nc)),
             VMEM((nc, parts, nj, piece, width), low),
             VMEM((nc, nj) + extra, low),
             VMEM((nc, parts, nj, piece, width), low),
@@ -446,7 +470,7 @@
         compiler_params=pltpu.CompilerParams(
             collective_id=2, has_side_effects=True, vmem_limit_bytes=56 * 1024 * 1024
         ),
-    )(grads, small, squares)
+    )(grads, small, squares, *slices)
 
 
 CHUNK = 16
@@ -580,6 +604,7 @@
     return pl.pallas_call(
         kernel,
         name="attend_forward",
+        cost_estimate=pl.CostEstimate(flops=25 * 10**9, bytes_accessed=10**7, transcendentals=0),
         out_shape=(
             jax.ShapeDtypeStruct((length, width), low),
             jax.ShapeDtypeStruct((length, part), low),
@@ -606,7 +631,8 @@
 
 
 def attend_backward(
-    dattn, dh, o_all, tokens, first, q_all, k_all, v_all, lse, weights, gain, query_code, key_code, slopes, nc, ns
+    dattn, dh, o_all, tokens, first, q_all, k_all, v_all, lse, weights, gain, query_code, key_code, slopes,
+    picks, weighted, normed, cotangents, nc, ns,
 ):
     length, width = tokens.shape
     count = length // nc
@@ -614,15 +640,19 @@
     heads, _, band = slopes.shape
     low, f32 = jnp.bfloat16, jnp.float32
     scale = 1.0 / math.sqrt(HEAD)
+    more = normed.shape[0]
+    exchange = picks.shape[1:3] + (width,)
 
     def kernel(a_in, dh_in, o_in, t_in, first_in, q_in, k_in, v_in, lse_in, w_in, gain_in, qcode, kcode, toe,
-               x_out, w_out, gain_out, near_out, far_out,
-               mask, bank, dsend, dall, dq, dk, dv, fsend, frecv, fown, ss, rs, fs, fr):
+               p_in, pw_in, n_in, c_in,
+               x_out, w_out, gain_out, near_out, far_out, n_out, c_out,
+               mask, bank, dsend, dall, dq, dk, dv, fsend, frecv, fown, nsend, ss, rs, fs, fr, ns_, nr):
         me = Place(nc, ns)
         barrier = pltpu.get_barrier_semaphore()
-        for d in range(1, nc):
-            pl.semaphore_signal(barrier, inc=1, device_id=me.along(d), device_id_type=MESH)
-        pl.semaphore_wait(barrier, nc - 1)
+        partners = [me.along(d) for d in range(1, nc)] + [(me.c, me.s ^ m) for m in range(1, ns)]
+        for partner in partners:
+            pl.semaphore_signal(barrier, inc=1, device_id=partner, device_id_type=MESH)
+        pl.semaphore_wait(barrier, len(partners))
 
         def do_copy(d):
             return remote(dsend.at[d], dall.at[me.c], ss.at[d], rs.at[d], me.along(d))
@@ -638,6 +668,11 @@
                 do_copy(d).start()
             else:
                 dall[me.c] = value.astype(low)
+        jobs = [(pw_in.at[d], c_in.at[me.c ^ (d + 1)], c_out.at[d]) for d in range(nc - 1)]
+        jobs = jobs + [(p_in.at[d], n_in.at[d], n_out.at[d]) for d in range(more)]
+        spread = Spread(me, jobs, nsend, ns_, nr)
+        for i in range(len(jobs)):
+            spread.start(i)
         for n in range(nc):
             for origin in range(nc):
                 w_out[3 + n, origin * part : (origin + 1) * part] = tn(
@@ -741,6 +776,7 @@
         scaled = x_out[...] * gain_in[...]
         pull = jnp.mean(scaled * x, axis=-1, keepdims=True)
         x_out[...] = dh_in[...] + rate * scaled - x * (rate * rate * rate * pull)
+        spread.finish()
         for d in range(1, nc):
             do_copy(d).wait_send()
         for b in range(nc):
@@ -752,15 +788,18 @@
     return pl.pallas_call(
         kernel,
         name="attend_backward",
+        cost_estimate=pl.CostEstimate(flops=50 * 10**9, bytes_accessed=10**7, transcendentals=0),
         out_shape=(
             jax.ShapeDtypeStruct((count, width), f32),
             jax.ShapeDtypeStruct((3 + nc, width, part), low),
             jax.ShapeDtypeStruct((1, width), f32),
             jax.ShapeDtypeStruct((heads, CHUNK, band), f32),
             jax.ShapeDtypeStruct((heads, 8, 128), f32),
+            jax.ShapeDtypeStruct((more,) + exchange, low),
+            jax.ShapeDtypeStruct((nc - 1,) + exchange, low),
         ),
-        in_specs=[pl.BlockSpec(memory_space=VMEM)] * 14,
-        out_specs=[pl.BlockSpec(memory_space=VMEM)] * 5,
+        in_specs=[pl.BlockSpec(memory_space=VMEM)] * 18,
+        out_specs=[pl.BlockSpec(memory_space=VMEM)] * 5 + [pl.BlockSpec(memory_space=ANY)] * 2,
         scratch_shapes=[
             VMEM((count, length), f32),
             VMEM((heads, count, band), f32),
@@ -772,19 +811,491 @@
             VMEM((nc, count, width), low),
             VMEM((nc, count, width), low),
             VMEM((count, width), f32),
+            VMEM((4,) + exchange, low),
             SEM.DMA((nc,)),
             SEM.DMA((nc,)),
             SEM.DMA((nc,)),
             SEM.DMA((nc,)),
+            SEM.DMA((nc - 1 + more, ns)),
+            SEM.DMA((nc - 1 + more, ns)),
         ],
         compiler_params=pltpu.CompilerParams(
             collective_id=4, has_side_effects=True, vmem_limit_bytes=56 * 1024 * 1024
         ),
-    )(dattn, dh, o_all, tokens, first, q_all, k_all, v_all, lse, weights, gain, query_code, key_code, slopes)
+    )(dattn, dh, o_all, tokens, first, q_all, k_all, v_all, lse, weights, gain, query_code, key_code, slopes,
+      picks, weighted, normed, cotangents)
 
 
 def activation(gate_values, up_values):
     return jax.nn.gelu(gate_values) * up_values
+
+
+def gelu_parts(x):
+    c, a = math.sqrt(2.0 / math.pi), 0.044715
+    square = x * x
+    t = jnp.tanh(c * x * (1.0 + a * square))
+    half = 0.5 * (1.0 + t)
+    return x * half, half + (0.5 * c) * x * (1.0 - t * t) * (1.0 + (3.0 * a) * square)
+
+
+class Chain:
+    def __init__(self, me, pairs, send, recv):
+        self.me, self.pairs, self.send, self.recv, self.nc = me, pairs, send, recv, me.nc
+
+    def copies(self, direction, hop, landing):
+        me, nc = self.me, self.nc
+        lane = 0 if direction > 0 else 1
+        origin = lax.rem(me.c - direction * (hop + 1 if landing else hop) + 2 * nc, nc)
+        result = []
+        for i, (own, every) in enumerate(self.pairs):
+            target = every.at[origin]
+            source = own if hop == 0 and not landing else target
+            result.append(
+                remote(
+                    source, target, self.send.at[lane, hop, i], self.recv.at[lane, hop, i],
+                    me.along(direction),
+                )
+            )
+        return result
+
+    def sends(self, direction, hop):
+        c, nc = self.me.c, self.nc
+        if direction > 0:
+            return (c >= hop) & (c < nc - 1)
+        return (c <= nc - 1 - hop) & (c > 0)
+
+    def lands(self, direction, hop):
+        c, nc = self.me.c, self.nc
+        if direction > 0:
+            return c >= hop + 1
+        return c <= nc - 2 - hop
+
+    def start(self, hop):
+        for direction in (1, -1):
+            if hop:
+
+                @pl.when(self.lands(direction, hop - 1))
+                def _():
+                    for copy in self.copies(direction, hop - 1, True):
+                        copy.wait_recv()
+
+            if hop < self.nc - 1:
+
+                @pl.when(self.sends(direction, hop))
+                def _():
+                    for copy in self.copies(direction, hop, False):
+                        copy.start()
+
+    def finish(self):
+        for direction in (1, -1):
+            for hop in range(self.nc - 1):
+
+                @pl.when(self.sends(direction, hop))
+                def _():
+                    for copy in self.copies(direction, hop, False):
+                        copy.wait_send()
+
+
+def greet_experts(me):
+    barrier = pltpu.get_barrier_semaphore()
+    partners = [(me.c, me.s ^ m) for m in range(1, me.ns)] + [me.along(1), me.along(-1)]
+    for partner in partners:
+        pl.semaphore_signal(barrier, inc=1, device_id=partner, device_id_type=MESH)
+    pl.semaphore_wait(barrier, len(partners))
+
+
+TILE = 256
+
+
+class Spread:
+    def __init__(self, me, jobs, send, send_sem, recv_sem):
+        self.me, self.jobs, self.send = me, jobs, send
+        self.send_sem, self.recv_sem = send_sem, recv_sem
+        self.order = list(range(2, me.ns)) + [1]
+        self.turns = send.shape[0]
+
+    def copy(self, i, m):
+        return remote(
+            self.send.at[i % self.turns, m], self.jobs[i][2].at[m],
+            self.send_sem.at[i, m], self.recv_sem.at[i, m], (self.me.c, self.me.s ^ m),
+        )
+
+    def own(self, i):
+        return pltpu.make_async_copy(
+            self.send.at[i % self.turns, 0], self.jobs[i][2].at[0], self.send_sem.at[i, 0]
+        )
+
+    def left(self, i):
+        for m in self.order:
+            self.copy(i, m).wait_send()
+        self.own(i).wait()
+
+    def start(self, i):
+        if i >= self.turns:
+            self.left(i - self.turns)
+        picks, tokens = self.jobs[i][:2]
+        for m in self.order + [0]:
+            self.send[i % self.turns, m] = dot32(picks[m], tokens[...]).astype(self.send.dtype)
+            if m:
+                self.copy(i, m).start()
+            else:
+                self.own(i).start()
+
+    def finish(self):
+        for i in range(len(self.jobs)):
+            for m in self.order:
+                self.copy(i, m).wait_recv()
+            if i >= len(self.jobs) - self.turns:
+                self.left(i)
+
+
+def moe_forward(pick, pick_next, tokens, gates, gate_w, up_w, down_w, nc, ns):
+    cap, count = pick.shape[1:]
+    width, hidden = gate_w.shape
+    low, f32 = jnp.bfloat16, jnp.float32
+    half = ns // 2
+    rows_in_half = half * cap
+
+    def kernel(p_in, n_in, t_in, s_in, g_hbm, u_hbm, d_hbm, r_out, y_out, t_all, s_all, n_out,
+               wg, wu, wd, send, yield_, nsend, inner, ws, ss, rs, ys, yr, ts, tr, ls, ns_, nr):
+        me = Place(nc, ns)
+        loads = [
+            pltpu.make_async_copy(source, target, ws.at[i])
+            for i, (source, target) in enumerate(((g_hbm, wg), (u_hbm, wu), (d_hbm, wd)))
+        ]
+        for load in loads:
+            load.start()
+        keep = [
+            pltpu.make_async_copy(t_in, t_all.at[me.c], ls.at[0]),
+            pltpu.make_async_copy(s_in, s_all.at[me.c], ls.at[1]),
+        ]
+        for copy in keep:
+            copy.start()
+        greet_experts(me)
+
+        def there(m):
+            return (me.c, me.s ^ m)
+
+        def out_copy(m):
+            return remote(send.at[m], r_out.at[m], ss.at[m], rs.at[m], there(m))
+
+        def back_copy(m):
+            return remote(yield_.at[m], y_out.at[m], ys.at[m], yr.at[m], there(m))
+
+        order = list(range(2, ns)) + [1]
+        for m in order:
+            send[m] = dot32(p_in[m], t_in[...]).astype(low)
+            out_copy(m).start()
+        chain = Chain(me, ((t_in, t_all), (s_in, s_all)), ts, tr)
+        chain.start(0)
+        r_out[0] = dot32(p_in[0], t_in[...]).astype(low)
+        for load in loads:
+            load.wait()
+        for part in range(2):
+            for m in range(part * half, (part + 1) * half):
+                if m:
+                    out_copy(m).wait_recv()
+
+            def up(n, carry):
+                rows = r_out[part * half : (part + 1) * half].reshape(rows_in_half, width)
+                at = pl.ds(pl.multiple_of(n * TILE, TILE), TILE)
+                value = activation(dot32(rows, wg[:, at]), dot32(rows, wu[:, at]))
+                inner[:, at] = value.astype(low)
+                return carry
+
+            lax.fori_loop(0, hidden // TILE, up, 0)
+
+            def down(n, carry):
+                at = pl.ds(pl.multiple_of(n * TILE, TILE), TILE)
+                value = dot32(inner[...], wd[:, at]).astype(low).reshape(half, cap, TILE)
+                yield_[part * half : (part + 1) * half, :, at] = value
+                return carry
+
+            lax.fori_loop(0, width // TILE, down, 0)
+            for m in range(part * half, (part + 1) * half):
+                if m:
+                    back_copy(m).start()
+            if part == 0:
+                chain.start(1)
+                spread = Spread(me, [(n_in, t_all.at[me.c ^ 1], n_out)], nsend, ns_, nr)
+                spread.start(0)
+        y_out[0] = yield_[0]
+        for hop in range(2, nc):
+            chain.start(hop)
+        for m in order:
+            back_copy(m).wait_recv()
+        for copy in keep:
+            copy.wait()
+        for m in order:
+            out_copy(m).wait_send()
+            back_copy(m).wait_send()
+        spread.finish()
+        chain.finish()
+
+    exchange = (ns, cap, width)
+    return pl.pallas_call(
+        kernel,
+        name="moe_forward",
+        cost_estimate=pl.CostEstimate(flops=45 * 10**9, bytes_accessed=10**7, transcendentals=0),
+        out_shape=(
+            jax.ShapeDtypeStruct(exchange, low),
+            jax.ShapeDtypeStruct(exchange, low),
+            jax.ShapeDtypeStruct((nc,) + tokens.shape, low),
+            jax.ShapeDtypeStruct((nc,) + gates.shape, f32),
+            jax.ShapeDtypeStruct(exchange, low),
+        ),
+        in_specs=[pl.BlockSpec(memory_space=VMEM)] * 4 + [pl.BlockSpec(memory_space=ANY)] * 3,
+        out_specs=[pl.BlockSpec(memory_space=VMEM)] * 4 + [pl.BlockSpec(memory_space=ANY)],
+        scratch_shapes=[
+            VMEM((width, hidden), low),
+            VMEM((width, hidden), low),
+            VMEM((hidden, width), low),
+            VMEM(exchange, low),
+            VMEM(exchange, low),
+            VMEM((1,) + exchange, low),
+            VMEM((rows_in_half, hidden), low),
+            SEM.DMA((3,)),
+            SEM.DMA((ns,)),
+            SEM.DMA((ns,)),
+            SEM.DMA((ns,)),
+            SEM.DMA((ns,)),
+            SEM.DMA((2, nc, 2)),
+            SEM.DMA((2, nc, 2)),
+            SEM.DMA((2,)),
+            SEM.DMA((1, ns)),
+            SEM.DMA((1, ns)),
+        ],
+        compiler_params=pltpu.CompilerParams(
+            collective_id=5, has_side_effects=True, vmem_limit_bytes=56 * 1024 * 1024
+        ),
+    )(pick, pick_next, tokens, gates, gate_w, up_w, down_w)
+
+
+def moe_backward(grads, rows, cotangents, pick_next, tokens, gate_w, up_w, down_w, nc, ns):
+    cap = rows.shape[1]
+    width, hidden = gate_w.shape
+    low, f32 = jnp.bfloat16, jnp.float32
+    half = ns // 2
+    rows_in_half = half * cap
+    more = tokens.shape[0]
+
+    def kernel(g_in, r_in, t_in, n_in, f_in, g_hbm, u_hbm, d_hbm, g_out, x_out, t_all, n_out,
+               wg, wu, wd, yield_, nsend, slope_g, slope_u, dg, du, ws, ss, rs, ys, yr, ts, tr, ls, ns_, nr):
+        me = Place(nc, ns)
+        loads = [
+            pltpu.make_async_copy(source, target, ws.at[i])
+            for i, (source, target) in enumerate(((g_hbm, wg), (u_hbm, wu), (d_hbm, wd)))
+        ]
+        for load in loads:
+            load.start()
+        keep = pltpu.make_async_copy(t_in, t_all.at[me.c], ls.at[0])
+        keep.start()
+        greet_experts(me)
+
+        def there(m):
+            return (me.c, me.s ^ m)
+
+        def out_copy(m):
+            return remote(g_in.at[m], g_out.at[m], ss.at[m], rs.at[m], there(m))
+
+        def back_copy(m):
+            return remote(yield_.at[m], x_out.at[m], ys.at[m], yr.at[m], there(m))
+
+        order = list(range(2, ns)) + [1]
+        for m in order:
+            out_copy(m).start()
+        chain = Chain(me, ((t_in, t_all),), ts, tr)
+        chain.start(0)
+        g_out[0] = g_in[0]
+        for load in loads:
+            load.wait()
+
+        def again(n, carry):
+            every = r_in[...].reshape(ns * cap, width)
+            at = pl.ds(pl.multiple_of(n * TILE, TILE), TILE)
+            value, slope = gelu_parts(dot32(every, wg[:, at]))
+            slope_g[:, at] = (slope * dot32(every, wu[:, at])).astype(slope_g.dtype)
+            slope_u[:, at] = value.astype(slope_u.dtype)
+            return carry
+
+        lax.fori_loop(0, hidden // TILE, again, 0)
+        chain.start(1)
+        jobs = [(n_in.at[i], f_in.at[i], n_out.at[i]) for i in range(more)]
+        spread = Spread(me, jobs, nsend, ns_, nr)
+        for i in range(more):
+            spread.start(i)
+        for part in range(2):
+            for m in range(part * half, (part + 1) * half):
+                if m:
+                    out_copy(m).wait_recv()
+            here = slice(part * rows_in_half, (part + 1) * rows_in_half)
+
+            def up(n, carry):
+                taken = g_out[part * half : (part + 1) * half].reshape(rows_in_half, width)
+                at = pl.ds(pl.multiple_of(n * TILE, TILE), TILE)
+                value = nt(taken, wd[at])
+                dg[:, at] = (value * slope_g[here, at].astype(f32)).astype(low)
+                du[:, at] = (value * slope_u[here, at].astype(f32)).astype(low)
+                return carry
+
+            lax.fori_loop(0, hidden // TILE, up, 0)
+
+            def down(n, carry):
+                at = pl.ds(pl.multiple_of(n * TILE, TILE), TILE)
+                value = nt(dg[...], wg[at]) + nt(du[...], wu[at])
+                yield_[part * half : (part + 1) * half, :, at] = value.astype(low).reshape(
+                    half, cap, TILE
+                )
+                return carry
+
+            lax.fori_loop(0, width // TILE, down, 0)
+            for m in range(part * half, (part + 1) * half):
+                if m:
+                    back_copy(m).start()
+            if part == 0:
+                chain.start(2)
+        x_out[0] = yield_[0]
+        for hop in range(3, nc):
+            chain.start(hop)
+        for m in order:
+            back_copy(m).wait_recv()
+        keep.wait()
+        for m in order:
+            out_copy(m).wait_send()
+            back_copy(m).wait_send()
+        spread.finish()
+        chain.finish()
+
+    exchange = (ns, cap, width)
+    return pl.pallas_call(
+        kernel,
+        name="moe_backward",
+        cost_estimate=pl.CostEstimate(flops=45 * 10**9, bytes_accessed=10**7, transcendentals=0),
+        out_shape=(
+            jax.ShapeDtypeStruct(exchange, low),
+            jax.ShapeDtypeStruct(exchange, low),
+            jax.ShapeDtypeStruct((nc,) + cotangents.shape, low),
+            jax.ShapeDtypeStruct((more,) + exchange, low),
+        ),
+        in_specs=[pl.BlockSpec(memory_space=VMEM)] * 5 + [pl.BlockSpec(memory_space=ANY)] * 3,
+        out_specs=[pl.BlockSpec(memory_space=VMEM)] * 2 + [pl.BlockSpec(memory_space=ANY)] * 2,
+        scratch_shapes=[
+            VMEM((width, hidden), low),
+            VMEM((width, hidden), low),
+            VMEM((hidden, width), low),
+            VMEM(exchange, low),
+            VMEM((1,) + exchange, low),
+            VMEM((ns * cap, hidden), low),
+            VMEM((ns * cap, hidden), low),
+            VMEM((rows_in_half, hidden), low),
+            VMEM((rows_in_half, hidden), low),
+            SEM.DMA((3,)),
+            SEM.DMA((ns,)),
+            SEM.DMA((ns,)),
+            SEM.DMA((ns,)),
+            SEM.DMA((ns,)),
+            SEM.DMA((2, nc, 1)),
+            SEM.DMA((2, nc, 1)),
+            SEM.DMA((1,)),
+            SEM.DMA((more, ns)),
+            SEM.DMA((more, ns)),
+        ],
+        compiler_params=pltpu.CompilerParams(
+            collective_id=6, has_side_effects=True, vmem_limit_bytes=60 * 1024 * 1024
+        ),
+    )(grads, rows, cotangents, pick_next, tokens, gate_w, up_w, down_w)
+
+
+def slice_plan(hidden, nc):
+    exact, tiles = hidden // nc, hidden // 128
+    wide = max(-(-((c + 1) * exact) // 128) - (c * exact) // 128 for c in range(nc))
+    return [min((c * exact) // 128, tiles - wide) * 128 for c in range(nc)], wide * 128
+
+
+def slice_grads(rows, grads, gate_w, up_w, down_w, nc):
+    width, hidden = gate_w.shape
+    exact = hidden // nc
+    starts, wide = slice_plan(hidden, nc)
+    low, f32 = jnp.bfloat16, jnp.float32
+    row_at = [(i, n) for i, x in enumerate(rows) for n in range(x.shape[0])]
+    grad_at = [(len(rows) + i, n) for i, x in enumerate(grads) for n in range(x.shape[0])]
+    count, block = len(rows) + len(grads), rows[0].shape[1]
+    cuts = [(i, min(i + TILE, wide)) for i in range(0, wide, TILE)]
+
+    def kernel(*refs):
+        g_hbm, u_hbm, d_hbm, wg_out, wu_out, wd_out, xs, ys, wg, wu, wd, inner, dg, du, ag, au, ad, ws, rs = refs[count:]
+        c = lax.axis_index("ctx")
+        exact_tile = (c * exact) // 128
+        begin = pl.multiple_of(jnp.minimum(exact_tile, (hidden - wide) // 128) * 128, 128)
+
+        def fetch(i):
+            (a, n), (b, k) = row_at[i], grad_at[i]
+            return [
+                pltpu.make_async_copy(refs[a].at[n], xs.at[i % 2], rs.at[i % 2, 0]),
+                pltpu.make_async_copy(refs[b].at[k], ys.at[i % 2], rs.at[i % 2, 1]),
+            ]
+
+        loads = fetch(0) + [
+            pltpu.make_async_copy(g_hbm.at[:, pl.ds(begin, wide)], wg, ws.at[0]),
+            pltpu.make_async_copy(u_hbm.at[:, pl.ds(begin, wide)], wu, ws.at[1]),
+            pltpu.make_async_copy(d_hbm.at[pl.ds(begin, wide)], wd, ws.at[2]),
+        ]
+        for load in loads:
+            load.start()
+        for load in loads:
+            load.wait()
+        for i in range(len(row_at)):
+            if i:
+                for load in fetch(i):
+                    load.wait()
+            if i + 1 < len(row_at):
+                for load in fetch(i + 1):
+                    load.start()
+            x, dy = xs.at[i % 2], ys.at[i % 2]
+            for left, right in cuts:
+                value, slope = gelu_parts(dot32(x[...], wg[:, left:right]))
+                linear = dot32(x[...], wu[:, left:right])
+                down = nt(dy[...], wd[left:right])
+                inner[:, left:right] = (value * linear).astype(low)
+                dg[:, left:right] = (down * linear * slope).astype(low)
+                du[:, left:right] = (down * value).astype(low)
+            for total, one, other in ((ag, x, dg), (au, x, du), (ad, inner, dy)):
+                if i:
+                    total[...] += tn(one[...], other[...])
+                else:
+                    total[...] = tn(one[...], other[...])
+        wg_out[...] = ag[...].astype(low)
+        wu_out[...] = au[...].astype(low)
+        wd_out[...] = ad[pl.ds(pl.multiple_of(c * exact - begin, 16), exact)]
+
+    return pl.pallas_call(
+        kernel,
+        name="slice_grads",
+        cost_estimate=pl.CostEstimate(flops=38 * 10**9, bytes_accessed=10**7, transcendentals=0),
+        out_shape=(
+            jax.ShapeDtypeStruct((width, wide), low),
+            jax.ShapeDtypeStruct((width, wide), low),
+            jax.ShapeDtypeStruct((exact, width), f32),
+        ),
+        in_specs=[pl.BlockSpec(memory_space=ANY)] * (count + 3),
+        out_specs=[pl.BlockSpec(memory_space=VMEM)] * 3,
+        scratch_shapes=[
+            VMEM((2, block, width), low),
+            VMEM((2, block, width), low),
+            VMEM((width, wide), low),
+            VMEM((width, wide), low),
+            VMEM((wide, width), low),
+            VMEM((block, wide), low),
+            VMEM((block, wide), low),
+            VMEM((block, wide), low),
+            VMEM((width, wide), f32),
+            VMEM((width, wide), f32),
+            VMEM((wide, width), f32),
+            SEM.DMA((3,)),
+            SEM.DMA((2, 2)),
+        ],
+        compiler_params=pltpu.CompilerParams(vmem_limit_bytes=60 * 1024 * 1024),
+    )(*rows, *grads, gate_w, up_w, down_w)
 
 
 def per_device(
@@ -819,8 +1330,19 @@
     piece = w_query.shape[0]
     band = 2 * row_count
 
+    route_local = routes[0]
+    expert_ids = jnp.arange(experts, dtype=jnp.int32)
+    route_hot = route_local[:, :, None] == expert_ids[None, None, :]
+    flat_routes = route_local.reshape(row_count * top_count)
+    route_hits = (flat_routes[:, None] == expert_ids[None, :]).astype(jnp.int32)
+    before = jnp.cumsum(route_hits, axis=0) - route_hits
+    slot_rank = jnp.sum(before * route_hits, axis=1).reshape(row_count, top_count)
+
     part = width // nc
-    smalls = (norm_attn, norm_ffn, rel_bias, w_router.reshape(-1), segments[0].astype(low), valid[0].astype(low))
+    smalls = (
+        norm_attn, norm_ffn, rel_bias, w_router.reshape(-1), segments[0].astype(low), valid[0].astype(low),
+        route_local.astype(low).T.reshape(-1), slot_rank.astype(low).T.reshape(-1),
+    )
     sizes = [x.shape[0] for x in smalls]
     starts = [sum(sizes[:i]) for i in range(len(sizes))]
     extra = jnp.concatenate(smalls + (jnp.zeros((EXTRA * part - sum(sizes),), low),))
@@ -862,33 +1384,34 @@
     ffn_in = ffn_low.astype(f32)
     router = full_router.astype(f32)
     logits = jnp.dot(ffn_in, router, precision=highest_precision)
-    route_local = routes[0]
-    expert_ids = jnp.arange(experts, dtype=jnp.int32)
-    route_hot = route_local[:, :, None] == expert_ids[None, None, :]
     picked = jnp.sum(jnp.where(route_hot, logits[:, None, :], 0.0), axis=-1)
     gate_probs = jax.nn.softmax(picked, axis=-1)
-    flat_routes = route_local.reshape(row_count * top_count)
-    route_hits = (flat_routes[:, None] == expert_ids[None, :]).astype(jnp.int32)
-    before = jnp.cumsum(route_hits, axis=0) - route_hits
-    slot_rank = jnp.sum(before * route_hits, axis=1)
-    target = (flat_routes * capacity + slot_rank).reshape(row_count, top_count)
-    slot_ids = jnp.arange(experts * capacity, dtype=jnp.int32)
+
+    slots = -(-capacity // 16) * 16
+    target = (route_local ^ s) * slots + slot_rank
+    slot_ids = jnp.arange(experts * slots, dtype=jnp.int32)
     pick_first = (slot_ids[:, None] == target[None, :, 0]).astype(low)
     pick_second = (slot_ids[:, None] == target[None, :, 1]).astype(low)
-
-    def exchange(rows):
-        return lax.all_to_all(
-            rows.reshape(experts, capacity, width), "shard", split_axis=0, concat_axis=0, tiled=True
-        ).reshape(experts * capacity, width)
-
-    expert_rows = exchange(dot32(pick_first + pick_second, ffn_low).astype(low))
+    pick_both = pick_first + pick_second
     gate_w, up_w, down_w = w_gate[0], w_up[0], w_down[0]
-    gate_pre = dot32(expert_rows, gate_w)
-    up_pre = dot32(expert_rows, up_w)
-
-    inner_value, activation_back = jax.vjp(activation, gate_pre, up_pre)
-    inner = inner_value.astype(low)
-    returned = exchange(dot32(inner, down_w).astype(low))
+    gate_rows = jnp.concatenate((gate_probs.T, jnp.zeros((8 - top_count, row_count), f32)), axis=0)
+    other_line = line[c ^ jnp.arange(1, nc)]
+    other_routes, other_slots = (
+        other_line[:, starts[i] : starts[i] + top_count * row_count]
+        .astype(jnp.int32)
+        .reshape(nc - 1, top_count, row_count)
+        for i in (6, 7)
+    )
+    other_target = (other_routes ^ s) * slots + other_slots
+    other_first, other_second = (
+        slot_ids[None, :, None] == other_target[:, m, None, :] for m in range(2)
+    )
+    other_picks = (other_first | other_second).astype(low).reshape(nc - 1, experts, slots, row_count)
+    expert_rows, returned, ffn_all, gates_all, rows_next = moe_forward(
+        pick_both.reshape(experts, slots, row_count), other_picks[0], ffn_low, gate_rows,
+        gate_w, up_w, down_w, nc, ns,
+    )
+    returned = returned.reshape(experts * slots, width)
     picked_one, picked_two = tn(pick_first, returned), tn(pick_second, returned)
     output_sum = residual + gate_probs[:, :1] * picked_one + gate_probs[:, 1:] * picked_two
     valid_one = valid[0].astype(f32)
@@ -902,20 +1425,16 @@
     back_send = dot32(pick_first, (gate_probs[:, :1] * cotangent).astype(low)) + dot32(
         pick_second, (gate_probs[:, 1:] * cotangent).astype(low)
     )
-    out_grad = exchange(back_send.astype(low))
-    inner_grad = nt(out_grad, down_w)
-    gate_pre_grad, up_pre_grad = activation_back(inner_grad)
-    gate_low = gate_pre_grad.astype(low)
-    up_low = up_pre_grad.astype(low)
-    sent_back = exchange((nt(gate_low, gate_w) + nt(up_low, up_w)).astype(low))
-    down_w_grad = tn(inner, out_grad).astype(low)
-    gate_w_grad = tn(expert_rows, gate_low).astype(low)
-    up_w_grad = tn(expert_rows, up_low).astype(low)
-    gate_w_sum, up_w_sum, down_w_sum = (
-        lax.psum_scatter(x[None], "ctx", scatter_dimension=1, tiled=True).astype(f32)
-        for x in (gate_w_grad, up_w_grad, down_w_grad)
-    )
-    ffn_grad = tn(pick_first + pick_second, sent_back)
+    other_gates = gates_all[c ^ jnp.arange(1, nc)].astype(low)
+    other_weighted = (
+        jnp.where(other_first, other_gates[:, 0, None, :], low(0))
+        + jnp.where(other_second, other_gates[:, 1, None, :], low(0))
+    ).reshape(other_picks.shape)
+    out_grad, sent_back, cotangent_all, rows_later = moe_backward(
+        back_send.astype(low).reshape(experts, slots, width), expert_rows, cotangent.astype(low),
+        other_picks[1 : nc // 2], ffn_all[c ^ jnp.arange(2, nc // 2 + 1)], gate_w, up_w, down_w, nc, ns,
+    )
+    ffn_grad = tn(pick_both, sent_back.reshape(experts * slots, width))
     pick_grad = gate_probs * (gate_grad - jnp.sum(gate_probs * gate_grad, axis=-1, keepdims=True))
     logits_grad = jnp.sum(jnp.where(route_hot, pick_grad[:, :, None], 0.0), axis=1)
     router_grad = contract(ffn_in, logits_grad, 0, 0, highest_precision)
@@ -924,9 +1443,18 @@
     residual_from_norm, gain_two_grad = norm_two_back(ffn_grad)
     residual_grad = cotangent + residual_from_norm
     attn_grad_low = residual_grad.astype(low)
-    input_grad, w_grads, gain_one_grad, near_sum, far_sum = attend_backward(
+    input_grad, w_grads, gain_one_grad, near_sum, far_sum, rows_last, other_grads = attend_backward(
         attn_grad_low, residual_grad, mixed, tokens_all, first_all, queries, keys, values, log_total, weights,
-        gain_one[None], query_code, key_code, slopes, nc, ns,
+        gain_one[None], query_code, key_code, slopes,
+        other_picks[nc // 2 :], other_weighted, ffn_all[c ^ jnp.arange(nc // 2 + 1, nc)], cotangent_all, nc, ns,
+    )
+    gate_slice, up_slice, down_slice = slice_grads(
+        [
+            x.reshape(-1, experts * slots, width)
+            for x in (expert_rows, rows_next, rows_later, rows_last)
+        ],
+        [x.reshape(-1, experts * slots, width) for x in (out_grad, other_grads)],
+        gate_w, up_w, down_w, nc,
     )
     own_bias = jnp.einsum("hix,ixb->bh", near_sum, level_hot, precision=highest_precision)
     last_bucket = (jnp.arange(BUCKETS) == BUCKETS - 1).astype(f32)
@@ -942,17 +1470,17 @@
         axis=1,
     )
     small_grads = jnp.pad(small_grads, ((0, 0), (0, EXTRA * part - small_grads.shape[1])))
-    kept_sum, w_sum, small_sum, square_sum = reduce_all(
+    attn_sums, unused, small_sum, square_sum, gate_w_sum, up_w_sum = reduce_all(
         w_grads.reshape(3 + nc, nc, nj, 2, piece, part),
         small_grads.reshape(nc, nj, 2, EXTRA, part),
         jnp.full((8, 128), local_square, f32),
+        [x.reshape(nc, width // nc, -1) for x in (gate_slice, up_slice)],
+        gate_w.shape[1],
         nc,
         ns,
         3,
     )
     loss_value = square_sum[0, 0] / (2.0 * width * valid_count)
-    kept_sum = kept_sum.transpose(0, 2, 1, 3).reshape(3, piece, width)
-    out_sum = w_sum[3:].transpose(1, 0, 2).reshape(piece, width)
     small_sum = small_sum.reshape(-1)
     tails = [small_sum[begin : begin + size] for begin, size in zip(starts[:4], sizes[:4])]
     return (
@@ -960,16 +1488,16 @@
         loss_value,
         input_grad[None],
         tails[0],
-        kept_sum[0],
-        kept_sum[1],
-        kept_sum[2],
-        out_sum,
+        attn_sums[0],
+        attn_sums[1],
+        attn_sums[2],
+        attn_sums[3],
         tails[2],
         tails[1],
         tails[3].reshape(w_router.shape),
-        gate_w_sum,
-        up_w_sum,
-        down_w_sum,
+        gate_w_sum[None],
+        up_w_sum[None],
+        down_slice[None],
     )
 
 

time: 592 us -> 474 us (0.80)
  Pallas kernels: 239 us -> 402 us
  waiting for transfers between devices: 142 us -> 0 us
  matrix products: 81.3 us -> 10.8 us
  blocking collectives: 43.4 us -> 0 us
  between operations: 18 us -> 4.75 us
  starting transfers between devices: 8.61 us -> 0 us
  other arithmetic: 19.2 us -> 13.1 us
    pallas_call x4 -> x7, Pallas kernels: 239 us -> 402 us  [the longest x1 87.1 us: reduce_all(): pl.pallas_call(kernel, name='reduce_all', cost_estimate=pl.CostEstimate(f...]
    reduce_scatter x3 -> x0, waiting for transfers between devices: 112 us -> none  [per_device(): lax.psum_scatter(x[None], 'ctx', scatter_dimension=1, tiled=True)]
    dot_general x11 -> x5, matrix products: 61.3 us -> 5.25 us  [contract(): lax.dot_general(left_side, right_side, (((left_axis,), (right_axis,)), ((...]
    all_to_all x2 -> x0, blocking collectives: 43.4 us -> none  [exchange(): lax.all_to_all(rows.reshape(experts, capacity, width), 'shard', split_axi...]
    all_to_all x2 -> x0, waiting for transfers between devices: 29.4 us -> none  [exchange(): lax.all_to_all(rows.reshape(experts, capacity, width), 'shard', split_axi...]
    dot_general x6 -> x2, matrix products: 17.8 us -> 2.24 us  [dot32(): return jnp.dot(left_side, right_side, preferred_element_type=jnp.float32)]
    all_to_all x2 -> x0, starting transfers between devices: 8.32 us -> none  [exchange(): lax.all_to_all(rows.reshape(experts, capacity, width), 'shard', split_axi...]
    convert_element_type x3 -> x2, other arithmetic: 9.55 us -> 1.8 us  [the longest x1 1.18 us: per_device(): cotangent.astype(low)]
  transfers between devices with their start and end apart: 5 -> 0, of which waited for: 4 -> 0; matrix products, arithmetic and copies ran while one was open for 14% -> 0% of each run, Pallas kernels for 27% -> 0%
where the time goes in v3:
time: 474 us; the launch traced here: 465 us
  Pallas kernels  402 us (85%)
  local copies, waits for them, and re-layouts  34 us (7%)
  other arithmetic  13.1 us (3%)
  matrix products  10.8 us (2%)
  between operations  4.75 us (1%)
    pallas_call x1, Pallas kernels, reduce_all(): pl.pallas_call(kernel, name='reduce_all', cost_estimate=pl.CostEstimate(f...  87.1 us
    pallas_call x1, Pallas kernels, attend_backward(): pl.pallas_call(kernel, name='attend_backward', cost_estimate=pl.CostEstim...  81.6 us
    pallas_call x1, Pallas kernels, moe_forward(): pl.pallas_call(kernel, name='moe_forward', cost_estimate=pl.CostEstimate(...  57.5 us
    pallas_call x1, Pallas kernels, moe_backward(): pl.pallas_call(kernel, name='moe_backward', cost_estimate=pl.CostEstimate...  57.4 us
    pallas_call x1, Pallas kernels, gather_all(): pl.pallas_call(kernel, name='gather_all', cost_estimate=pl.CostEstimate(f...  53.8 us
    pallas_call x1, Pallas kernels, slice_grads(): pl.pallas_call(kernel, name='slice_grads', cost_estimate=pl.CostEstimate(...  36 us
    pallas_call x1, Pallas kernels, attend_forward(): pl.pallas_call(kernel, name='attend_forward', cost_estimate=pl.CostEstima...  28.9 us
    unnamed x50, local copies, waits for them, and re-layouts  13 us

profile of v3, /device:TPU:0, one launch (start us, length us, event | category | flops | bytes accessed | tf_op | source)
XLA Modules:
  0.0 464.9 jit_solution(14032878597300348077)
XLA Ops:
  11.2 53.8 %gather_all.1 = (bf16[7,4,8,32,256]{4,3,2,1,0:T(8,128)(2,1)}, bf16[4,8,16,256]{3,2,1,0:T(8,128)(2,1)}, bf16[4,256,1024]{2,1,0:T(8,128)(2,1)}) custom-call(bf16[4,7,32,256]{3,2,1,0:T(8,128)(2,1)} %pad_maximum_fusion.w_in, bf16[16,256]{1,0:T(8,128)(2,1)} %reshape.501.e_in, bf16[256,1024]{1,0:T(8,128)(2,1)} %bitcast.209), custom_call_target="tpu_custom_call" | custom-call | flops 49999998976 | bytes 10000000 | tf_op jit(solution)/shard_map/gather_all/pallas_call | solution.py:232
  75.8 28.9 %attend_forward.1 = (bf16[1024,1024]{1,0:T(8,128)(2,1)}, bf16[1024,256]{1,0:T(8,128)(2,1)}, bf16[1024,256]{1,0:T(8,128)(2,1)}, bf16[1024,256]{1,0:T(8,128)(2,1)}...) custom-call(bf16[1024,1024]{1,0:T(8,128)(2,1)} %bitcast.215, ...), custom_call_target="tpu_custom_call" | custom-call | flops 24999999488 | bytes 10000000 | tf_op jit(solution)/shard_map/attend_forward/pallas_call | solution.py:604
  104.7 1.3 fusion.56
  106.7 57.5 %moe_forward.1 = (bf16[8,80,1024]{2,1,0:T(8,128)(2,1)}, bf16[8,80,1024]{2,1,0:T(8,128)(2,1)}, bf16[4,256,1024]{2,1,0:T(8,128)(2,1)}, f32[4,8,256]{2,1,0:T(8,128)}, bf16[8,80,1024]{2,1,0:T(8,128)(2,1)}) custom-call(bf16[8,80,256]{2,1,0:T(8,128)(2,1)} %fusion.20.p_in, bf16[8,80,256]{2,1,0:T(8,128)(2,1)} %bitcast.169, ...), custom_call_target="tpu_custom_call" | custom-call | flops 44999999488 | bytes 10000000 | tf_op jit(solution)/shard_map/moe_forward/pallas_call | solution.py:1036
  164.3 1.4 gather_fusion.1
  165.7 1.5 fusion.6.pw_in
  167.2 2.4 constant_dynamic-slice_fusion
  170.3 1.5 fusion.4
  171.8 1.2 broadcast_in_dim.144.q_in
  173.1 1.2 fusion.51
  177.3 1.7 add_convert_fusion
  179.0 57.4 %moe_backward.1 = (bf16[8,80,1024]{2,1,0:T(8,128)(2,1)}, bf16[8,80,1024]{2,1,0:T(8,128)(2,1)}, bf16[4,256,1024]{2,1,0:T(8,128)(2,1)}, bf16[1,8,80,1024]{3,2,1,0:T(8,128)(2,1)}) custom-call(bf16[8,80,1024]{2,1,0:T(8,128)(2,1)} %bitcast.162, bf16[8,80,1024]{2,1,0:T(8,128)(2,1)} %get-tuple-element.55.r_in, bf16[256,1024]{1,0:T(8,128)(2,1)} %get-tuple-element.186.t_in, ...), custom_call_target="tpu_custom_call" | custom-call | flops 44999999488 | bytes 10000000 | tf_op jit(solution)/shard_map/moe_backward/pallas_call | solution.py:1170
  236.4 2.1 multiply_reduce_fusion
  238.5 1.4 fusion.49
  240.0 81.6 %attend_backward.1 = (f32[256,1024]{1,0:T(8,128)}, bf16[7,1024,256]{2,1,0:T(8,128)(2,1)}, f32[1,1024]{1,0:T(1,128)}, f32[4,16,512]{2,1,0:T(8,128)}, f32[4,8,128]...) custom-call(bf16[256,1024]{1,0:T(8,128)(2,1)} %get-tuple-element.184.a_in, ...), custom_call_target="tpu_custom_call" | custom-call | flops 49999998976 | bytes 10000000 | tf_op jit(solution)/shard_map/attend_backward/pallas_call | solution.py:788
  322.5 1.6 fusion.2
  326.2 36.0 %slice_grads.1 = (bf16[1024,768]{1,0:T(8,128)(2,1)}, bf16[1024,768]{1,0:T(8,128)(2,1)}, f32[704,1024]{1,0:T(8,128)}) custom-call(bf16[1,640,1024]{2,1,0:T(8,128)(2,1)} %bitcast.219, bf16[1,640,1024]{2,1,0:T(8,128)(2,1)} %bitcast.220, bf16[1,640,1024]{2,1,0:T(8,128)(2,1)} %bitcast.222, bf16[1,640,1024]{2,1,0:T(8,128)(2,1)} %bitcast.223, ...), custom_call_target="tpu_custom_call" | custom-call | flops 38000001024 | bytes 10000000 | tf_op jit(solution)/shard_map/slice_grads/pallas_call | solution.py:1271
  362.2 87.1 %reduce_all.1 = (f32[4,32,1024]{2,1,0:T(8,128)}, f32[7,32,256]{2,1,0:T(8,128)}, f32[16,256]{1,0:T(8,128)}, f32[8,128]{1,0:T(8,128)}, f32[256,2816]{1,0:T(8,128)}, /*index=5*/f32[256,2816]{1,0:T(8,128)}) custom-call(bf16[7,4,4,2,32,256]{5,4,3,2,1,0:T(8,128)(2,1)} %bitcast.213, bf16[4,4,2,16,256]{4,3,2,1,0:T(8,128)(2,1)} %bitcast.172, ...), custom_call_target="tpu_custom_call" | custom-call | flops 44999999488 | bytes 10000000 | tf_op jit(solution)/shard_map/reduce_all/pallas_call | solution.py:426
  449.3 1.3 slice.133
  454.7 1.9 slice_bitcast_fusion
  456.6 2.3 copy.185
  458.9 1.6 copy.186
  460.5 1.3 copy-done.2
  461.8 1.6 copy.187
  (130 shorter events, 30.6 us)
Async XLA Ops:
  0.6 7.8 %copy-start.13 = (bf16[32]{0:T(256)(128)(2,1)S(1)}, bf16[32]{0:T(256)(128)(2,1)}, u32[]{:S(2)}) copy-start(bf16[32]{0:T(256)(128)(2,1)} %param.27) | copy-start | bytes 196
  0.7 7.8 %copy-start.14 = (bf16[16]{0:T(256)(128)(2,1)S(1)}, bf16[16]{0:T(256)(128)(2,1)}, u32[]{:S(2)}) copy-start(bf16[16]{0:T(256)(128)(2,1)} %param.26) | copy-start | bytes 100
  0.7 8.8 %copy-start.8 = (bf16[32,1024]{1,0:T(8,128)(2,1)S(1)}, bf16[32,1024]{1,0:T(8,128)(2,1)}, u32[]{:S(2)}) copy-start(bf16[32,1024]{1,0:T(8,128)(2,1)} %param.24) | copy-start | bytes 196612
  0.7 8.8 %copy-start.9 = (bf16[32,1024]{1,0:T(8,128)(2,1)S(1)}, bf16[32,1024]{1,0:T(8,128)(2,1)}, u32[]{:S(2)}) copy-start(bf16[32,1024]{1,0:T(8,128)(2,1)} %param.23) | copy-start | bytes 196612
  0.7 7.8 %copy-start.12 = (bf16[32]{0:T(256)(128)(2,1)S(1)}, bf16[32]{0:T(256)(128)(2,1)}, u32[]{:S(2)}) copy-start(bf16[32]{0:T(256)(128)(2,1)} %param.21) | copy-start | bytes 196
  3.6 68.0 %copy-start.10 = (s32[16,512]{1,0:T(8,128)}, s32[16,512]{1,0:T(8,128)S(1)}, u32[]{:S(2)}) copy-start(s32[16,512]{1,0:T(8,128)S(1)} %convert_add_fusion) | copy-start | bytes 98308
  73.2 31.5 %copy-start.4 = (bf16[1024,8]{1,0:T(8,128)(2,1)}, bf16[1024,8]{1,0:T(8,128)(2,1)S(1)}, u32[]{:S(2)}) copy-start(bf16[1024,8]{1,0:T(8,128)(2,1)S(1)} %reshape_reshape.4) | copy-start | bytes 49156
  164.2 5.4 %copy-start.1 = (bf16[8,80,1024]{2,1,0:T(8,128)(2,1)S(1)}, bf16[8,80,1024]{2,1,0:T(8,128)(2,1)}, u32[]{:S(2)}) copy-start(bf16[8,80,1024]{2,1,0:T(8,128)(2,1)} %get-tuple-element.54) | copy-start | bytes 3932164
  167.2 3.1 copy-start
  167.2 3.1 copy-start.6
  174.2 1.0 copy-start.7
  174.2 1.9 copy-start.5
  240.0 82.5 %copy-start.11 = (s32[16,512]{1,0:T(8,128)S(1)}, s32[16,512]{1,0:T(8,128)}, u32[]{:S(2)}) copy-start(s32[16,512]{1,0:T(8,128)} %copy-done.10) | copy-start | bytes 98308
  240.0 82.5 %copy-start.15 = (f32[32]{0:T(128)S(1)}, f32[32]{0:T(128)}, u32[]{:S(2)}) copy-start(f32[32]{0:T(128)} %compare_convert_fusion.2) | copy-start | bytes 388
  449.3 9.7 %copy-start.3 = (f32[256,2816]{1,0:T(8,128)S(1)}, f32[256,2816]{1,0:T(8,128)}, u32[]{:S(2)}) copy-start(f32[256,2816]{1,0:T(8,128)} %get-tuple-element.81) | copy-start | bytes 8650756
  458.9 2.9 copy-start.2
